TPU v7x, 256 devices: a whole 4x4x8 slice. The times are simulated.
256 devices in a mesh: node: 16 (over z, core), local: 16 (over y, x).
Axes of the slice: x: 4, y: 4, z: 8, core: 2. Of those that a mesh axis runs over, the one named last changes fastest.
Arguments:
- tokens: bfloat16 [2048, 7168], P(('node', 'local')), may hold values from -6 to 6
- expert_ids: int32 [2048, 2], P(('node', 'local')), may hold values from 0 to 15, all different within a row; in each aligned block of 8 rows (0 to 7, 8 to 15, ...) at most 2 rows name the same one
- gate_scales: float32 [2048, 2], P(('node', 'local')), may hold values from 0.2 to 1.5
- placement: int32 [16], replicated, may hold values from 0 to 15, each once
- expert_gate: bfloat16 [16, 7168, 2048], P('node', None, 'local'), may hold values from -0.0625 to 0.0625
- expert_up: bfloat16 [16, 7168, 2048], P('node', None, 'local'), may hold values from -0.0625 to 0.0625
- expert_down: bfloat16 [16, 2048, 7168], P('node', 'local'), may hold values from -0.125 to 0.125
- shared_gate: bfloat16 [7168, 2048], P(None, 'local'), may hold values from -0.0625 to 0.0625
- shared_up: bfloat16 [7168, 2048], P(None, 'local'), may hold values from -0.0625 to 0.0625
- shared_down: bfloat16 [2048, 7168], P('local'), may hold values from -0.125 to 0.125
Outputs:
- mixed: bfloat16 [2048, 7168], P(('node', 'local'))
Inputs may be any that keep to these rules, and one draw needn't show every extreme that they name: `expert_ids`: each token names 2 different experts; among the rows of one device no expert is named more than 2 times, and that many is reached. `placement`: every node holds exactly one expert.
All inputs are finite; a program needn't handle non-finite values.
Results may differ from a plain program's by a relative error of at most 0.019.
Values may be sent and summed in bfloat16 or wider, within the bound.
No kernel may reach another device: no remote copies, remote signals or barrier semaphores. Data moves between devices by JAX's collectives and lax.ppermute only.
A program may use at most 128 MiB of HBM per device.

v0:
```python
from functools import partial

import jax
import jax.numpy as jnp
from jax import lax
from jax.sharding import PartitionSpec as P


def destinations(expert_ids, placement):
    labels = jnp.arange(placement.shape[0], dtype=jnp.int32)
    matches = expert_ids[..., None] == labels
    return jnp.sum(jnp.where(matches, placement, 0), axis=-1)


def slot_index(targets, capacity, node_count):
    labels = jnp.arange(node_count, dtype=jnp.int32)
    marks = (targets[:, None] == labels[None, :]).astype(jnp.int32)
    earlier = jnp.cumsum(marks, axis=0) - marks
    position = jnp.sum(earlier * marks, axis=1)
    return targets * capacity + position


def combine(own_slots, gate_scales, outputs, tok_rows, slot_count):
    labels = jnp.arange(outputs.shape[0], dtype=jnp.int32)
    scales = gate_scales.reshape(-1)[:, None]
    weights = jnp.where(own_slots[:, None] == labels[None, :], scales, jnp.float32(0.0))
    weights = jnp.sum(weights.reshape(tok_rows, slot_count, -1), axis=1)
    return jnp.dot(weights, outputs, precision=lax.Precision.HIGHEST)


def expert_part(token_rows, gate_weight, up_weight, down_weight):
    gate = jnp.dot(token_rows, gate_weight, preferred_element_type=jnp.float32)
    lifted = jnp.dot(token_rows, up_weight, preferred_element_type=jnp.float32)
    hidden = (jax.nn.silu(gate) * lifted).astype(jnp.bfloat16)
    return jnp.dot(hidden, down_weight, preferred_element_type=jnp.float32)


def fill_rows(slots, source_rows, row_count):
    labels = jnp.arange(row_count, dtype=jnp.int32)
    table = (labels[:, None] == slots[None, :]).astype(jnp.bfloat16)
    return jnp.dot(table, source_rows, preferred_element_type=jnp.float32).astype(jnp.bfloat16)


def per_device(
    tokens,
    expert_ids,
    gate_scales,
    placement,
    expert_gate,
    expert_up,
    expert_down,
    shared_gate,
    shared_up,
    shared_down,
):
    node_count = lax.axis_size("node")
    local_count = lax.axis_size("local")
    tok_rows, features = tokens.shape
    slot_count = expert_ids.shape[1]
    capacity = max(2, (3 * tok_rows * slot_count + 2 * node_count - 1) // (2 * node_count))
    targets = destinations(expert_ids, placement)
    own_slots = slot_index(targets.reshape(-1), capacity, node_count)
    weights_gate = expert_gate[0]
    weights_up = expert_up[0]
    weights_down = expert_down[0]
    node_tok, node_targets = (
        lax.all_gather(tokens, "local", axis=0, tiled=True),
        lax.all_gather(targets.astype(jnp.bfloat16), "local", axis=0, tiled=True),
    )
    node_targets = node_targets.astype(jnp.int32).reshape(local_count, tok_rows * slot_count)
    block_slots = jax.vmap(partial(slot_index, capacity=capacity, node_count=node_count))(
        node_targets
    )
    position = block_slots - node_targets * capacity
    source = jnp.arange(local_count, dtype=jnp.int32)[:, None]
    node_slots = (node_targets * (local_count * capacity) + source * capacity + position).reshape(
        -1
    )
    repeated = jnp.repeat(node_tok, slot_count, axis=0)
    blocks = fill_rows(node_slots, repeated, node_count * local_count * capacity)
    blocks = blocks.reshape(node_count, local_count * capacity, features)
    arrived = lax.all_to_all(blocks, "node", split_axis=0, concat_axis=0, tiled=True)
    partial_out = expert_part(arrived.reshape(-1, features), weights_gate, weights_up, weights_down)
    partial_out = partial_out.astype(jnp.bfloat16).reshape(
        node_count, local_count * capacity, features
    )
    returned = lax.all_to_all(partial_out, "node", split_axis=0, concat_axis=0, tiled=True)
    returned = returned.reshape(node_count, local_count, capacity, features)
    shared_part = expert_part(node_tok, shared_gate, shared_up, shared_down)
    shared_terms = shared_part.reshape(1, local_count, tok_rows, features)
    routed, shared_out = (
        lax.psum_scatter(
            returned.astype(jnp.float32).astype(jnp.bfloat16),
            "local",
            scatter_dimension=1,
            tiled=True,
        ).astype(jnp.float32),
        lax.psum_scatter(
            shared_terms.astype(jnp.bfloat16), "local", scatter_dimension=1, tiled=True
        ).astype(jnp.float32),
    )
    expert_out = routed.reshape(node_count * capacity, features)
    shared_out = shared_out.reshape(tok_rows, features)
    mixed = shared_out + combine(own_slots, gate_scales, expert_out, tok_rows, slot_count)
    return mixed.astype(jnp.bfloat16)


def solution(mesh):
    placed = (
        P(("node", "local"), None),
        P(("node", "local"), None),
        P(("node", "local"), None),
        P(),
        P("node", None, "local"),
        P("node", None, "local"),
        P("node", "local", None),
        P(None, "local"),
        P(None, "local"),
        P("local", None),
    )
    return jax.shard_map(
        per_device,
        mesh=mesh,
        in_specs=placed,
        out_specs=P(("node", "local"), None),
        check_vma=False,
    )
```

profile of v0, /device:TPU:1, one launch (start us, length us, event | category | flops | bytes accessed | tf_op | source)
XLA Modules:
  0.0 617.2 jit_solution(15838436331493643268)
XLA Ops:
  6.5 0.7 all-gather.3.cloned.1.call-update
  7.3 0.9 select_reduce_fusion.2
  8.7 0.2 select_reduce_fusion.1
  9.0 17.1 %all-gather = bf16[16,8,2]{1,2,0:T(2,128)(2,1)S(1)} all-gather(bf16[1,8,2]{1,2,0:T(2,128)(2,1)S(1)} %get-tuple-element.5), channel_id=1, replica_groups=mesh['node'=16,'local'=16] {'local'}, dimensions={0}, use_global_device_ids=true | all-gather | bytes 544 | tf_op jit(solution)/shard_map/all_gather | solution.py:68
  26.2 0.5 fusion.35
  27.0 0.1 mul.56
  27.2 34.7 %all-gather.3.cloned.1.call-done = bf16[128,7168]{1,0:T(8,128)(2,1)} async-done(((bf16[8,7168]{1,0:T(8,128)(2,1)}), bf16[128,7168]{1,0:T(8,128)(2,1)}) %all-gather.3.cloned.1.call-update) | async-done | bytes 1835024 | tf_op jit(solution)/shard_map/all_gather | solution.py:67
  61.9 5.0 broadcast_in_dim.35
  66.8 8.4 %reshape.92 = bf16[256,7168]{1,0:T(8,128)(2,1)} reshape(bf16[128,2,7168]{2,1,0:T(2,128)(2,1)} %broadcast_in_dim.35) | data formatting | bytes 7340032 | tf_op jit(solution)/shard_map/reshape | solution.py:79
  75.2 4.1 convolution_convert_fusion.1
  79.4 172.1 %all_to_all.10 = bf16[16,32,7168]{2,1,0:T(8,128)(2,1)S(1)} all-to-all(bf16[16,32,7168]{2,1,0:T(8,128)(2,1)S(1)} %bitcast.43), channel_id=1, replica_groups=mesh['node'=16,'local'=16] {'node'}, dimensions={0} | all-to-all | bytes 14680064 | tf_op jit(solution)/shard_map/all_to_all | solution.py:82
  251.5 3.0 copy-done.1
  254.5 2.1 fusion.5
  256.5 15.3 %convolution_convert_fusion = bf16[512,7168]{1,0:T(8,128)(2,1)} fusion(bf16[1,128,7168]{2,1,0:T(8,128)(2,1)S(1)} %copy-done, bf16[512,7168]{1,0:T(8,128)(2,1)} %bitcast.45, bf16[1,7168,128]{2,1,0:T(8,128)(2,1)} %param.15, f32[512,128]{1,0:T(8,128)S(1)} %fusion.5), kind=kOutput, calls=%fused_computation | convolution fusion | flops 1883111424 | bytes 18612224 | tf_op jit(solution)/shard_map/dot_general | solution.py:35
  271.9 166.3 %all_to_all.11 = bf16[16,32,7168]{2,1,0:T(8,128)(2,1)S(1)} all-to-all(bf16[16,32,7168]{2,1,0:T(8,128)(2,1)} %bitcast.46), channel_id=1, replica_groups=mesh['node'=16,'local'=16] {'node'}, dimensions={0} | all-to-all | bytes 14680064 | tf_op jit(solution)/shard_map/all_to_all | solution.py:87
  438.2 7.0 %copy.46 = bf16[16,32,7168]{2,0,1:T(8,128)(2,1)} copy(bf16[16,32,7168]{2,1,0:T(8,128)(2,1)S(1)} %all_to_all.11) | data formatting | bytes 14680064 | tf_op jit(solution)/shard_map/all_to_all | solution.py:87
  445.2 2.7 fusion.36
  447.9 5.1 fusion
  453.1 0.7 copy-done.2
  453.8 73.2 %reduce-scatter.10.cloned.1.call-done = bf16[16,1,2,7168]{3,0,2,1:T(8,128)(2,1)} async-done(((bf16[16,16,2,7168]{3,0,2,1:T(8,128)(2,1)}), bf16[16,1,2,7168]{3,0,2,1:T(8,128)(2,1)}) %reduce-scatter.10.cloned.1.call-update) | async-done | bytes 458768
  527.0 1.5 copy.47
  528.5 0.2 reshape.97
  528.6 80.2 %reduce-scatter.8.cloned.1.call-done = bf16[1,1,8,7168]{3,2,1,0:T(8,128)(2,1)} async-done(((bf16[1,16,8,7168]{3,2,1,0:T(8,128)(2,1)}), bf16[1,1,8,7168]{3,2,1,0:T(8,128)(2,1)}) %reduce-scatter.8.cloned.1.call-update) | async-done | bytes 114704
  608.8 1.8 fusion.1
  (30 shorter events, 1.2 us)
Async XLA Ops:
  6.5 250.0 %copy-start = (bf16[1,128,7168]{2,1,0:T(8,128)(2,1)S(1)}, bf16[1,128,7168]{2,1,0:T(8,128)(2,1)}, u32[]{:S(2)}) copy-start(bf16[1,128,7168]{2,1,0:T(8,128)(2,1)} %param.16) | copy-start | bytes 5505028
  6.5 55.3 %all-gather.3.cloned.1.call-start = ((), (), s32[]{:S(2)}) async-start(), calls=%async_computation.4 | async-start | bytes 1949696 | tf_op jit(solution)/shard_map/all_gather | solution.py:67
  7.3 519.7 %reduce-scatter.10.cloned.1.call-start = ((), (), s32[]{:S(2)}) async-start(), calls=%async_computation.6 | async-start | bytes 7798784
  79.3 175.1 %copy-start.3 = (bf16[1,7168,128]{2,1,0:T(8,128)(2,1)S(1)}, bf16[1,7168,128]{2,1,0:T(8,128)(2,1)}, u32[]{:S(2)}) copy-start(bf16[1,7168,128]{2,1,0:T(8,128)(2,1)} %param.14) | copy-start | bytes 5505028
  251.5 3.0 copy-start.1
  445.2 163.6 %reduce-scatter.8.cloned.1.call-start = ((), (), s32[]{:S(2)}) async-start(), calls=%async_computation.5 | async-start | bytes 1949696
  453.0 0.7 copy-start.2
Sparse Core Ops, SparseCore 0:
  9.8 52.0 all-gather.2
  445.3 81.6 reduce-scatter.9
  530.9 77.8 reduce-scatter.7
where the time goes:
time: 618 us; the launch traced here: 617 us
  blocking collectives  356 us (58%)
  waiting for transfers between devices  189 us (31%)
  matrix products  31.2 us (5%)
  local copies, waits for them, and re-layouts  26.7 us (4%)
  between operations  13.2 us (2%)
    all_to_all x1, blocking collectives, per_device(): lax.all_to_all(blocks, 'node', split_axis=0, concat_axis=0, tiled=True)  172 us
    all_to_all x1, blocking collectives, per_device(): lax.all_to_all(partial_out, 'node', split_axis=0, concat_axis=0, tiled=True)  166 us
    unnamed x5, waiting for transfers between devices  154 us
    all_gather x1, waiting for transfers between devices, per_device(): lax.all_gather(tokens, 'local', axis=0, tiled=True)  34.7 us
    dot_general x2, matrix products, expert_part(): return jnp.dot(hidden, down_weight, preferred_element_type=jnp.float32)  20.5 us
    all_gather x1, blocking collectives, per_device(): lax.all_gather(targets.astype(jnp.bfloat16), 'local', axis=0, tiled=True)  17.1 us
  transfers between devices with their start and end apart: 3, of which 3 were waited for; matrix products, arithmetic and copies ran while one was open for 2% of the time, Pallas kernels for 0%

commit v1 on v0

v1 whole, which is shorter than its diff:
```python
import jax
import jax.numpy as jnp
from jax import lax
from jax.experimental import pallas as pl
from jax.experimental.pallas import tpu as pltpu
from jax.sharding import PartitionSpec as P

SIDE = 4
OFFS = (0, 1, -1, 2)
BF16, F32 = jnp.bfloat16, jnp.float32


def move(value, axis, step):
    pairs = []
    for y in range(SIDE):
        for x in range(SIDE):
            ty, tx = ((y + step) % SIDE, x) if axis == 0 else (y, (x + step) % SIDE)
            pairs.append((y * SIDE + x, ty * SIDE + tx))
    return lax.ppermute(value, "local", pairs)


def gather_ring(block, axis):
    half = block.shape[-1] // 2
    ahead = move(block, axis, -1)
    behind = move(block, axis, 1)
    left = move(ahead[:, :half], axis, -1)
    right = move(behind[:, half:], axis, 1)
    return block, ahead, behind, left, right


def scatter_ring(own, ahead, behind, left, right, axis):
    half = own.shape[-1] // 2
    from_behind = move(left, axis, 1)
    from_ahead = move(right, axis, -1)
    ahead = ahead.astype(F32) + jnp.pad(from_behind.astype(F32), ((0, 0), (0, half)))
    behind = behind.astype(F32) + jnp.pad(from_ahead.astype(F32), ((0, 0), (half, 0)))
    got_one = move(ahead.astype(BF16), axis, 1)
    got_two = move(behind.astype(BF16), axis, -1)
    return own.astype(F32) + got_one.astype(F32) + got_two.astype(F32)


def group(blocks, routed):
    return jnp.concatenate([b[:routed] for b in blocks] + [b[routed:] for b in blocks], axis=0)


def ungroup(stack, index, routed, own):
    base = SIDE * routed
    return jnp.concatenate(
        [stack[index * routed : (index + 1) * routed], stack[base + index * own : base + (index + 1) * own]], axis=0
    )


def mlp_kernel(routed, own, *refs):
    a_in, b_in = refs[0:5], refs[5:10]
    eg, eu, ed, sg, su, sd = refs[10:16]
    a_out, b_out = refs[16:21], refs[21:26]
    acc_e, acc_s, hid_e, hid_s = refs[26:30]
    width = a_in[0].shape[1]
    half = width // 2
    rows_e, rows_s = SIDE * routed, SIDE * own

    def product(parts, rows, weight, base):
        if len(parts) == 1:
            return jnp.dot(parts[0][rows, :], weight[pl.ds(base, width), :], preferred_element_type=F32)
        one = jnp.dot(parts[0][rows, :], weight[pl.ds(base, half), :], preferred_element_type=F32)
        two = jnp.dot(parts[1][rows, :], weight[pl.ds(base + half, half), :], preferred_element_type=F32)
        return one + two

    erows, srows = pl.ds(0, rows_e), pl.ds(rows_e, rows_s)
    for i in range(SIDE):
        parts = a_in[3:5] if i == 3 else a_in[i : i + 1]
        for k, weight in enumerate((eg, eu)):
            acc_e[k, i] = product(parts, erows, weight, 0)
        for k, weight in enumerate((sg, su)):
            acc_s[k, i] = product(parts, srows, weight, 0)
    for j in range(SIDE):
        parts = b_in[3:5] if j == 3 else b_in[j : j + 1]
        for k, weight in enumerate((eg, eu)):
            got = product(parts, erows, weight, width)
            for i in range(SIDE):
                acc_e[k, i, j * routed : (j + 1) * routed] += got[i * routed : (i + 1) * routed]
        for k, weight in enumerate((sg, su)):
            got = product(parts, srows, weight, width)
            for i in range(SIDE):
                acc_s[k, i, j * own : (j + 1) * own] += got[i * own : (i + 1) * own]
    for i in range(SIDE):
        gate = acc_e[0, i]
        acc_e[0, i] = gate / (1.0 + jnp.exp(-gate)) * acc_e[1, i]
        gate = acc_s[0, i]
        acc_s[0, i] = gate / (1.0 + jnp.exp(-gate)) * acc_s[1, i]
    for i in range(SIDE):
        for j in range(SIDE):
            hid_e[j, i * routed : (i + 1) * routed] = acc_e[0, i, j * routed : (j + 1) * routed]
            hid_s[j, i * own : (i + 1) * own] = acc_s[0, i, j * own : (j + 1) * own]

    step = 256
    for outs, base, get_e, get_s in (
        (a_out, 0, lambda i: acc_e[0, i], lambda i: acc_s[0, i]),
        (b_out, width, lambda i: hid_e[i], lambda i: hid_s[i]),
    ):
        for i in range(SIDE):
            he, hs = get_e(i).astype(BF16), get_s(i).astype(BF16)
            targets = ((outs[3], 0), (outs[4], half)) if i == 3 else ((outs[i], 0),)
            for out, start in targets:

                @pl.loop(0, out.shape[1] // step)
                def _(c, out=out, start=start, he=he, hs=hs):
                    at = pl.multiple_of(c * step, step)
                    columns = pl.ds(pl.multiple_of(base + start + at, step), step)
                    out[0:rows_e, pl.ds(at, step)] = jnp.dot(he, ed[:, columns], preferred_element_type=F32).astype(BF16)
                    out[rows_e : rows_e + rows_s, pl.ds(at, step)] = jnp.dot(
                        hs, sd[:, columns], preferred_element_type=F32
                    ).astype(BF16)


def mlp(a_parts, b_parts, weights, routed, own):
    group_width = weights[0].shape[1]
    shapes = [jax.ShapeDtypeStruct(p.shape, BF16) for p in (*a_parts, *b_parts)]
    rows = a_parts[0].shape[0]
    features = weights[0].shape[0]
    return pl.pallas_call(
        lambda *refs: mlp_kernel(routed, own, *refs),
        out_shape=shapes,
        in_specs=[pl.BlockSpec(memory_space=pltpu.VMEM)] * 16,
        out_specs=[pl.BlockSpec(memory_space=pltpu.VMEM)] * 10,
        scratch_shapes=[
            pltpu.VMEM((2, SIDE, SIDE * routed, group_width), F32),
            pltpu.VMEM((2, SIDE, SIDE * own, group_width), F32),
            pltpu.VMEM((SIDE, SIDE * routed, group_width), F32),
            pltpu.VMEM((SIDE, SIDE * own, group_width), F32),
        ],
        compiler_params=pltpu.CompilerParams(vmem_limit_bytes=48 * 1024 * 1024),
        cost_estimate=pl.CostEstimate(
            flops=2 * 3 * SIDE * rows * features * group_width,
            bytes_accessed=2 * (2 * SIDE * rows * features + 6 * features * group_width),
            transcendentals=SIDE * rows * group_width,
        ),
    )(*a_parts, *b_parts, *weights)


def per_device(
    tokens, expert_ids, gate_scales, placement, expert_gate, expert_up, expert_down, shared_gate, shared_up, shared_down
):
    node_count = lax.axis_size("node")
    own, features = tokens.shape
    capacity = 2
    routed = node_count * capacity
    half = features // 2

    ids = expert_ids.reshape(-1)
    labels = jnp.arange(node_count, dtype=jnp.int32)
    targets = jnp.sum(jnp.where(ids[:, None] == labels, placement, 0), axis=-1)
    order = jnp.arange(ids.shape[0], dtype=jnp.int32)
    earlier = (targets[:, None] == targets[None, :]) & (order[None, :] < order[:, None])
    slots = targets * capacity + jnp.sum(earlier.astype(jnp.int32), axis=1)
    slots = slots.reshape(own, -1)
    rows = jnp.arange(routed, dtype=jnp.int32)
    marks = slots[:, :, None] == rows

    table = jnp.sum(marks.astype(F32), axis=1).astype(BF16)
    blocks = lax.dot_general(table, tokens, (((0,), (0,)), ((), ())), preferred_element_type=F32).astype(BF16)
    arrived = lax.all_to_all(
        blocks.reshape(node_count, capacity, features), "node", split_axis=0, concat_axis=0, tiled=True
    ).reshape(routed, features)
    load = jnp.concatenate([arrived, tokens], axis=0)

    def spread(value, first):
        near = gather_ring(value, first)
        four = (*near[:3], jnp.concatenate(near[3:], axis=1))
        return gather_ring(group(four, routed), 1 - first)

    a_parts = spread(load[:, :half], 1)
    b_parts = spread(load[:, half:], 0)
    weights = (expert_gate[0], expert_up[0], expert_down[0], shared_gate, shared_up, shared_down)
    outs = mlp(a_parts, b_parts, weights, routed, own)

    def collect(parts, first):
        four = scatter_ring(*parts, 1 - first).astype(BF16)
        blocks = [ungroup(four, i, routed, own) for i in range(SIDE)]
        quarter = half // 2
        return scatter_ring(*blocks[:3], blocks[3][:, :quarter], blocks[3][:, quarter:], first)

    summed = jnp.concatenate([collect(outs[:5], 1), collect(outs[5:], 0)], axis=1)
    back = lax.all_to_all(
        summed[:routed].astype(BF16).reshape(node_count, capacity, features),
        "node",
        split_axis=0,
        concat_axis=0,
        tiled=True,
    ).reshape(routed, features)
    scales = jnp.sum(jnp.where(marks, gate_scales[:, :, None], jnp.float32(0.0)), axis=1)
    mixed = summed[routed:] + jnp.dot(scales, back.astype(F32), precision=lax.Precision.HIGHEST)
    return mixed.astype(BF16)


def solution(mesh):
    placed = (
        P(("node", "local"), None),
        P(("node", "local"), None),
        P(("node", "local"), None),
        P(),
        P("node", None, "local"),
        P("node", None, "local"),
        P("node", "local", None),
        P(None, "local"),
        P(None, "local"),
        P("local", None),
    )
    return jax.shard_map(
        per_device, mesh=mesh, in_specs=placed, out_specs=P(("node", "local"), None), check_vma=False
    )
```

time: 618 us -> 219 us (0.35)
  blocking collectives: 356 us -> 54.8 us
  waiting for transfers between devices: 189 us -> 72.3 us
  starting transfers between devices: 0.08 us -> 44 us
  Pallas kernels: 0 us -> 33.8 us
  matrix products: 31.2 us -> 2.16 us
  local copies, waits for them, and re-layouts: 26.7 us -> 6.11 us
  between operations: 13.2 us -> 0.48 us
    all_to_all x2, blocking collectives: 338 us -> 54.8 us  [the longest x1 29.1 us: per_device(): lax.all_to_all(summed[:routed].astype(BF16).reshape(node_count, capacity,...]
    unnamed x5 -> x0, waiting for transfers between devices: 154 us -> none
    ppermute x0 -> x32, waiting for transfers between devices: none -> 72.3 us  [move(): return lax.ppermute(value, 'local', pairs)]
    ppermute x0 -> x32, starting transfers between devices: none -> 44 us  [move(): return lax.ppermute(value, 'local', pairs)]
    all_gather x1 -> x0, waiting for transfers between devices: 34.7 us -> none  [per_device(): lax.all_gather(tokens, 'local', axis=0, tiled=True)]
    pallas_call x0 -> x1, Pallas kernels: none -> 33.8 us  [mlp(): pl.pallas_call(lambda *refs: mlp_kernel(routed, own, *refs), out_shape=sh...]
    dot_general x6 -> x2, matrix products: 31.2 us -> 2.16 us  [the longest x1 1.21 us: per_device(): lax.dot_general(table, tokens, (((0,), (0,)), ((), ())), preferred_elemen...]
    all_gather x1 -> x0, blocking collectives: 17.1 us -> none  [per_device(): lax.all_gather(targets.astype(jnp.bfloat16), 'local', axis=0, tiled=True)]
  transfers between devices with their start and end apart: 3 -> 32, of which waited for: 3 -> 16; matrix products, arithmetic and copies ran while one was open for 2% -> 1% of each run, Pallas kernels for 0% -> 0%
where the time goes in v1:
time: 219 us
  waiting for transfers between devices  72.3 us (33%)
  blocking collectives  54.8 us (25%)
  starting transfers between devices  44 us (20%)
  Pallas kernels  33.8 us (15%)
  local copies, waits for them, and re-layouts  6.11 us (3%)
  other arithmetic  5.22 us (2%)
    ppermute x32, waiting for transfers between devices, move(): return lax.ppermute(value, 'local', pairs)  72.3 us
    ppermute x32, starting transfers between devices, move(): return lax.ppermute(value, 'local', pairs)  44 us
    pallas_call x1, Pallas kernels, mlp(): pl.pallas_call(lambda *refs: mlp_kernel(routed, own, *refs), out_shape=sh...  33.8 us
    all_to_all x1, blocking collectives, per_device(): lax.all_to_all(summed[:routed].astype(BF16).reshape(node_count, capacity,...  29.1 us
    all_to_all x1, blocking collectives, per_device(): lax.all_to_all(blocks.reshape(node_count, capacity, features), 'node', sp...  25.8 us
    unnamed x37, local copies, waits for them, and re-layouts  4.74 us
  transfers between devices with their start and end apart: 32, of which 16 were waited for; matrix products, arithmetic and copies ran while one was open for 1% of the time, Pallas kernels for 0%

profile of v1, /device:TPU:1, one launch (start us, length us, event | category | flops | bytes accessed | tf_op | source)
XLA Modules:
  0.0 218.8 jit_solution(11869612858756164501)
XLA Ops:
  4.2 25.8 %all_to_all.10 = bf16[16,2,7168]{2,1,0:T(2,128)(2,1)S(1)} all-to-all(bf16[16,2,7168]{2,1,0:T(2,128)(2,1)S(1)} %reshape.29), channel_id=1, replica_groups=mesh['node'=16,'local'=16] {'node'}, dimensions={0} | all-to-all | bytes 917504 | tf_op jit(solution)/shard_map/all_to_all | solution.py:162
  36.5 3.9 %collective-permute-done.9 = bf16[40,3584]{1,0:T(8,128)(2,1)S(1)} collective-permute-done((bf16[40,3584]{1,0:T(8,128)(2,1)S(1)}, bf16[40,3584]{1,0:T(8,128)(2,1)S(1)}, u32[]{:S(2)}, u32[]{:S(2)}) %collective-permute-start.9) | collective-permute-done | bytes 286752 | tf_op jit(solution)/shard_map/ppermute | solution.py:19
  40.8 2.7 %collective-permute-start.10 = (bf16[40,1792]{1,0:T(8,128)(2,1)S(1)}, bf16[40,1792]{1,0:T(8,128)(2,1)S(1)}, u32[]{:S(2)}, u32[]{:S(2)}) collective-permute-start(bf16[40,1792]{1,0:T(8,128)(2,1)S(1)} %slice.217), channel_id=1, source_target_pairs={{0,12},{1,13},{2,14},{3,15},{4,0},{5,1},{6,2},{7,3},{8,4},{9,5},{1... | collective-permute-start | bytes 430088 | tf_op jit(solution)/shard_map/ppermute | solution.py:19
  50.2 2.5 %collective-permute-start.4 = (bf16[160,3584]{1,0:T(8,128)(2,1)S(1)}, bf16[160,3584]{1,0:T(8,128)(2,1)S(1)}, u32[]{:S(2)}, u32[]{:S(2)}) collective-permute-start(bf16[160,3584]{1,0:T(8,128)(2,1)S(1)} %slice_dynamic-update-slice_fusion.11.refs_0_), channel_id=1, source_target_pairs={{0,12},{1,13},{2,14},{3,15},{4,0},{5,1},{6,2},{7,3},{8,4},{9,5},{1... | collective-permute-start | bytes 3440648 | tf_op jit(solution)/shard_map/ppermute | solution.py:19
  53.2 2.4 %collective-permute-start.12 = (bf16[160,3584]{1,0:T(8,128)(2,1)S(1)}, bf16[160,3584]{1,0:T(8,128)(2,1)S(1)}, u32[]{:S(2)}, u32[]{:S(2)}) collective-permute-start(bf16[160,3584]{1,0:T(8,128)(2,1)S(1)} %slice_dynamic-update-slice_fusion.8.refs_5_), channel_id=1, source_target_pairs={{0,3},{1,0},{2,1},{3,2},{4,7},{5,4},{6,5},{7,6},{8,11},{9,8},{10,9... | collective-permute-start | bytes 3440648 | tf_op jit(solution)/shard_map/ppermute | solution.py:19
  55.7 21.0 %collective-permute-done.5.refs_2_ = bf16[160,3584]{1,0:T(8,128)(2,1)S(1)} collective-permute-done((bf16[160,3584]{1,0:T(8,128)(2,1)S(1)}, bf16[160,3584]{1,0:T(8,128)(2,1)S(1)}, u32[]{:S(2)}, u32[]{:S(2)}) %collective-permute-start.5) | collective-permute-done | bytes 1146912 | tf_op jit(solution)/shard_map/ppermute | solution.py:19
  77.7 2.1 collective-permute-start.6
  80.8 2.7 %collective-permute-start.14 = (bf16[160,1792]{1,0:T(8,128)(2,1)S(1)}, bf16[160,1792]{1,0:T(8,128)(2,1)S(1)}, u32[]{:S(2)}, u32[]{:S(2)}) collective-permute-start(bf16[160,1792]{1,0:T(8,128)(2,1)S(1)} %slice.223), channel_id=1, source_target_pairs={{0,3},{1,0},{2,1},{3,2},{4,7},{5,4},{6,5},{7,6},{8,11},{9,8},{10,9... | collective-permute-start | bytes 1720328 | tf_op jit(solution)/shard_map/ppermute | solution.py:19
  83.6 6.7 %collective-permute-done.7.refs_4_ = bf16[160,1792]{1,0:T(8,128)(2,1)S(1)} collective-permute-done((bf16[160,1792]{1,0:T(8,128)(2,1)S(1)}, bf16[160,1792]{1,0:T(8,128)(2,1)S(1)}, u32[]{:S(2)}, u32[]{:S(2)}) %collective-permute-start.7) | collective-permute-done | bytes 573472 | tf_op jit(solution)/shard_map/ppermute | solution.py:19
  90.3 2.7 %collective-permute-done.15.refs_9_ = bf16[160,1792]{1,0:T(8,128)(2,1)S(1)} collective-permute-done((bf16[160,1792]{1,0:T(8,128)(2,1)S(1)}, bf16[160,1792]{1,0:T(8,128)(2,1)S(1)}, u32[]{:S(2)}, u32[]{:S(2)}) %collective-permute-start.15) | collective-permute-done | bytes 573472 | tf_op jit(solution)/shard_map/ppermute | solution.py:19
  93.1 33.8 %shard_map.100 = (bf16[160,3584]{1,0:T(8,128)(2,1)S(1)}, bf16[160,3584]{1,0:T(8,128)(2,1)}, bf16[160,3584]{1,0:T(8,128)(2,1)}, bf16[160,1792]{1,0:T(8,128)(2,1)S...) custom-call(bf16[160,3584]{1,0:T(8,128)(2,1)} %copy-done.4, ...), custom_call_target="tpu_custom_call" | custom-call | flops 3523215360 | bytes 29360128 | tf_op jit(solution)/shard_map/pallas_call | solution.py:121
  126.9 3.4 %collective-permute-start.26 = (bf16[160,1792]{1,0:T(8,128)(2,1)S(1)}, bf16[160,1792]{1,0:T(8,128)(2,1)S(1)}, u32[]{:S(2)}, u32[]{:S(2)}) collective-permute-start(bf16[160,1792]{1,0:T(8,128)(2,1)S(1)} %get-tuple-element.24), channel_id=1, source_target_pairs={{0,3},{1,0},{2,1},{3,2},{4,7},{5,4},{6,5},{7,6},{8,11},{9,8},{10,9... | collective-permute-start | bytes 1720328 | tf_op jit(solution)/shard_map/ppermute | solution.py:19
  130.3 2.7 %collective-permute-start.18 = (bf16[160,1792]{1,0:T(8,128)(2,1)S(1)}, bf16[160,1792]{1,0:T(8,128)(2,1)S(1)}, u32[]{:S(2)}, u32[]{:S(2)}) collective-permute-start(bf16[160,1792]{1,0:T(8,128)(2,1)S(1)} %get-tuple-element.19), channel_id=1, source_target_pairs={{0,12},{1,13},{2,14},{3,15},{4,0},{5,1},{6,2},{7,3},{8,4},{9,5},{1... | collective-permute-start | bytes 1720328 | tf_op jit(solution)/shard_map/ppermute | solution.py:19
  132.9 5.8 %collective-permute-done.26 = bf16[160,1792]{1,0:T(8,128)(2,1)S(1)} collective-permute-done((bf16[160,1792]{1,0:T(8,128)(2,1)S(1)}, bf16[160,1792]{1,0:T(8,128)(2,1)S(1)}, u32[]{:S(2)}, u32[]{:S(2)}) %collective-permute-start.26) | collective-permute-done | bytes 573472 | tf_op jit(solution)/shard_map/ppermute | solution.py:19
  140.3 3.7 %collective-permute-start.27 = (bf16[160,3584]{1,0:T(8,128)(2,1)S(1)}, bf16[160,3584]{1,0:T(8,128)(2,1)S(1)}, u32[]{:S(2)}, u32[]{:S(2)}) collective-permute-start(bf16[160,3584]{1,0:T(8,128)(2,1)S(1)} %add_convert_fusion.1), channel_id=1, source_target_pairs={{0,3},{1,0},{2,1},{3,2},{4,7},{5,4},{6,5},{7,6},{8,11},{9,8},{10,9... | collective-permute-start | bytes 3440648 | tf_op jit(solution)/shard_map/ppermute | solution.py:19
  147.3 16.6 %collective-permute-done.27 = bf16[160,3584]{1,0:T(8,128)(2,1)S(1)} collective-permute-done((bf16[160,3584]{1,0:T(8,128)(2,1)S(1)}, bf16[160,3584]{1,0:T(8,128)(2,1)S(1)}, u32[]{:S(2)}, u32[]{:S(2)}) %collective-permute-start.27) | collective-permute-done | bytes 1146912 | tf_op jit(solution)/shard_map/ppermute | solution.py:19
  163.9 3.8 %collective-permute-done.25 = bf16[160,3584]{1,0:T(8,128)(2,1)S(1)} collective-permute-done((bf16[160,3584]{1,0:T(8,128)(2,1)S(1)}, bf16[160,3584]{1,0:T(8,128)(2,1)S(1)}, u32[]{:S(2)}, u32[]{:S(2)}) %collective-permute-start.25) | collective-permute-done | bytes 1146912 | tf_op jit(solution)/shard_map/ppermute | solution.py:19
  169.1 2.7 %collective-permute-start.30 = (bf16[40,1792]{1,0:T(8,128)(2,1)S(1)}, bf16[40,1792]{1,0:T(8,128)(2,1)S(1)}, u32[]{:S(2)}, u32[]{:S(2)}) collective-permute-start(bf16[40,1792]{1,0:T(8,128)(2,1)S(1)} %get-tuple-element.50), channel_id=1, source_target_pairs={{0,12},{1,13},{2,14},{3,15},{4,0},{5,1},{6,2},{7,3},{8,4},{9,5},{1... | collective-permute-start | bytes 430088 | tf_op jit(solution)/shard_map/ppermute | solution.py:19
  171.9 2.7 %collective-permute-start.22 = (bf16[40,1792]{1,0:T(8,128)(2,1)S(1)}, bf16[40,1792]{1,0:T(8,128)(2,1)S(1)}, u32[]{:S(2)}, u32[]{:S(2)}) collective-permute-start(bf16[40,1792]{1,0:T(8,128)(2,1)S(1)} %get-tuple-element.48), channel_id=1, source_target_pairs={{0,3},{1,0},{2,1},{3,2},{4,7},{5,4},{6,5},{7,6},{8,11},{9,8},{10,9... | collective-permute-start | bytes 430088 | tf_op jit(solution)/shard_map/ppermute | solution.py:19
  174.6 2.5 %collective-permute-start.31 = (bf16[40,3584]{1,0:T(8,128)(2,1)S(1)}, bf16[40,3584]{1,0:T(8,128)(2,1)S(1)}, u32[]{:S(2)}, u32[]{:S(2)}) collective-permute-start(bf16[40,3584]{1,0:T(8,128)(2,1)S(1)} %add_convert_fusion.6), channel_id=1, source_target_pairs={{0,12},{1,13},{2,14},{3,15},{4,0},{5,1},{6,2},{7,3},{8,4},{9,5},{1... | collective-permute-start | bytes 860168 | tf_op jit(solution)/shard_map/ppermute | solution.py:19
  177.3 2.6 %collective-permute-start.23 = (bf16[40,3584]{1,0:T(8,128)(2,1)S(1)}, bf16[40,3584]{1,0:T(8,128)(2,1)S(1)}, u32[]{:S(2)}, u32[]{:S(2)}) collective-permute-start(bf16[40,3584]{1,0:T(8,128)(2,1)S(1)} %add_convert_fusion.8), channel_id=1, source_target_pairs={{0,3},{1,0},{2,1},{3,2},{4,7},{5,4},{6,5},{7,6},{8,11},{9,8},{10,9... | collective-permute-start | bytes 860168 | tf_op jit(solution)/shard_map/ppermute | solution.py:19
  180.7 5.1 %collective-permute-done.29 = bf16[40,3584]{1,0:T(8,128)(2,1)S(1)} collective-permute-done((bf16[40,3584]{1,0:T(8,128)(2,1)S(1)}, bf16[40,3584]{1,0:T(8,128)(2,1)S(1)}, u32[]{:S(2)}, u32[]{:S(2)}) %collective-permute-start.29) | collective-permute-done | bytes 286752 | tf_op jit(solution)/shard_map/ppermute | solution.py:19
  185.9 2.4 %collective-permute-done.21 = bf16[40,3584]{1,0:T(8,128)(2,1)S(1)} collective-permute-done((bf16[40,3584]{1,0:T(8,128)(2,1)S(1)}, bf16[40,3584]{1,0:T(8,128)(2,1)S(1)}, u32[]{:S(2)}, u32[]{:S(2)}) %collective-permute-start.21) | collective-permute-done | bytes 286752 | tf_op jit(solution)/shard_map/ppermute | solution.py:19
  188.6 29.1 %all_to_all.11 = bf16[16,2,7168]{2,1,0:T(2,128)(2,1)S(1)} all-to-all(bf16[16,2,7168]{2,1,0:T(2,128)(2,1)S(1)} %reshape.31), channel_id=1, replica_groups=mesh['node'=16,'local'=16] {'node'}, dimensions={0} | all-to-all | bytes 917504 | tf_op jit(solution)/shard_map/all_to_all | solution.py:184
  (126 shorter events, 29.0 us)
Async XLA Ops:
  30.9 9.5 %collective-permute-start.9 = (bf16[40,3584]{1,0:T(8,128)(2,1)S(1)}, bf16[40,3584]{1,0:T(8,128)(2,1)S(1)}, u32[]{:S(2)}, u32[]{:S(2)}) collective-permute-start(bf16[40,3584]{1,0:T(8,128)(2,1)S(1)} %get-tuple-element.43), channel_id=1, source_target_pairs={{0,4},{1,5},{2,6},{3,7},{4,8},{5,9},{6,10},{7,11},{8,12},{9,13},{1... | collective-permute-start | bytes 860168 | tf_op jit(solution)/shard_map/ppermute | solution.py:19
  32.3 8.5 %collective-permute-start.8 = (bf16[40,3584]{1,0:T(8,128)(2,1)S(1)}, bf16[40,3584]{1,0:T(8,128)(2,1)S(1)}, u32[]{:S(2)}, u32[]{:S(2)}) collective-permute-start(bf16[40,3584]{1,0:T(8,128)(2,1)S(1)} %get-tuple-element.43), channel_id=1, source_target_pairs={{0,12},{1,13},{2,14},{3,15},{4,0},{5,1},{6,2},{7,3},{8,4},{9,5},{1... | collective-permute-start | bytes 860168 | tf_op jit(solution)/shard_map/ppermute | solution.py:19
  33.8 9.7 %collective-permute-start.1 = (bf16[40,3584]{1,0:T(8,128)(2,1)S(1)}, bf16[40,3584]{1,0:T(8,128)(2,1)S(1)}, u32[]{:S(2)}, u32[]{:S(2)}) collective-permute-start(bf16[40,3584]{1,0:T(8,128)(2,1)S(1)} %get-tuple-element.44), channel_id=1, source_target_pairs={{0,1},{1,2},{2,3},{3,0},{4,5},{5,6},{6,7},{7,4},{8,9},{9,10},{10,1... | collective-permute-start | bytes 860168 | tf_op jit(solution)/shard_map/ppermute | solution.py:19
  35.0 9.5 %collective-permute-start = (bf16[40,3584]{1,0:T(8,128)(2,1)S(1)}, bf16[40,3584]{1,0:T(8,128)(2,1)S(1)}, u32[]{:S(2)}, u32[]{:S(2)}) collective-permute-start(bf16[40,3584]{1,0:T(8,128)(2,1)S(1)} %get-tuple-element.44), channel_id=1, source_target_pairs={{0,3},{1,0},{2,1},{3,2},{4,7},{5,4},{6,5},{7,6},{8,11},{9,8},{10,9... | collective-permute-start | bytes 860168 | tf_op jit(solution)/shard_map/ppermute | solution.py:19
  49.9 26.8 %collective-permute-start.5 = (bf16[160,3584]{1,0:T(8,128)(2,1)S(1)}, bf16[160,3584]{1,0:T(8,128)(2,1)S(1)}, u32[]{:S(2)}, u32[]{:S(2)}) collective-permute-start(bf16[160,3584]{1,0:T(8,128)(2,1)S(1)} %slice_dynamic-update-slice_fusion.11.refs_0_), channel_id=1, source_target_pairs={{0,4},{1,5},{2,6},{3,7},{4,8},{5,9},{6,10},{7,11},{8,12},{9,13},{1... | collective-permute-start | bytes 3440648 | tf_op jit(solution)/shard_map/ppermute | solution.py:19
  50.2 26.7 %collective-permute-start.4 = (bf16[160,3584]{1,0:T(8,128)(2,1)S(1)}, bf16[160,3584]{1,0:T(8,128)(2,1)S(1)}, u32[]{:S(2)}, u32[]{:S(2)}) collective-permute-start(bf16[160,3584]{1,0:T(8,128)(2,1)S(1)} %slice_dynamic-update-slice_fusion.11.refs_0_), channel_id=1, source_target_pairs={{0,12},{1,13},{2,14},{3,15},{4,0},{5,1},{6,2},{7,3},{8,4},{9,5},{1... | collective-permute-start | bytes 3440648 | tf_op jit(solution)/shard_map/ppermute | solution.py:19
  52.6 27.2 %collective-permute-start.13 = (bf16[160,3584]{1,0:T(8,128)(2,1)S(1)}, bf16[160,3584]{1,0:T(8,128)(2,1)S(1)}, u32[]{:S(2)}, u32[]{:S(2)}) collective-permute-start(bf16[160,3584]{1,0:T(8,128)(2,1)S(1)} %slice_dynamic-update-slice_fusion.8.refs_5_), channel_id=1, source_target_pairs={{0,1},{1,2},{2,3},{3,0},{4,5},{5,6},{6,7},{7,4},{8,9},{9,10},{10,1... | collective-permute-start | bytes 3440648 | tf_op jit(solution)/shard_map/ppermute | solution.py:19
  53.2 26.7 %collective-permute-start.12 = (bf16[160,3584]{1,0:T(8,128)(2,1)S(1)}, bf16[160,3584]{1,0:T(8,128)(2,1)S(1)}, u32[]{:S(2)}, u32[]{:S(2)}) collective-permute-start(bf16[160,3584]{1,0:T(8,128)(2,1)S(1)} %slice_dynamic-update-slice_fusion.8.refs_5_), channel_id=1, source_target_pairs={{0,3},{1,0},{2,1},{3,2},{4,7},{5,4},{6,5},{7,6},{8,11},{9,8},{10,9... | collective-permute-start | bytes 3440648 | tf_op jit(solution)/shard_map/ppermute | solution.py:19
  76.7 13.6 %collective-permute-start.7 = (bf16[160,1792]{1,0:T(8,128)(2,1)S(1)}, bf16[160,1792]{1,0:T(8,128)(2,1)S(1)}, u32[]{:S(2)}, u32[]{:S(2)}) collective-permute-start(bf16[160,1792]{1,0:T(8,128)(2,1)S(1)} %slice.212), channel_id=1, source_target_pairs={{0,4},{1,5},{2,6},{3,7},{4,8},{5,9},{6,10},{7,11},{8,12},{9,13},{1... | collective-permute-start | bytes 1720328 | tf_op jit(solution)/shard_map/ppermute | solution.py:19
  77.7 12.6 %collective-permute-start.6 = (bf16[160,1792]{1,0:T(8,128)(2,1)S(1)}, bf16[160,1792]{1,0:T(8,128)(2,1)S(1)}, u32[]{:S(2)}, u32[]{:S(2)}) collective-permute-start(bf16[160,1792]{1,0:T(8,128)(2,1)S(1)} %slice.211), channel_id=1, source_target_pairs={{0,12},{1,13},{2,14},{3,15},{4,0},{5,1},{6,2},{7,3},{8,4},{9,5},{1... | collective-permute-start | bytes 1720328 | tf_op jit(solution)/shard_map/ppermute | solution.py:19
  79.8 13.2 %collective-permute-start.15 = (bf16[160,1792]{1,0:T(8,128)(2,1)S(1)}, bf16[160,1792]{1,0:T(8,128)(2,1)S(1)}, u32[]{:S(2)}, u32[]{:S(2)}) collective-permute-start(bf16[160,1792]{1,0:T(8,128)(2,1)S(1)} %slice.224), channel_id=1, source_target_pairs={{0,1},{1,2},{2,3},{3,0},{4,5},{5,6},{6,7},{7,4},{8,9},{9,10},{10,1... | collective-permute-start | bytes 1720328 | tf_op jit(solution)/shard_map/ppermute | solution.py:19
  80.8 12.2 %collective-permute-start.14 = (bf16[160,1792]{1,0:T(8,128)(2,1)S(1)}, bf16[160,1792]{1,0:T(8,128)(2,1)S(1)}, u32[]{:S(2)}, u32[]{:S(2)}) collective-permute-start(bf16[160,1792]{1,0:T(8,128)(2,1)S(1)} %slice.223), channel_id=1, source_target_pairs={{0,3},{1,0},{2,1},{3,2},{4,7},{5,4},{6,5},{7,6},{8,11},{9,8},{10,9... | collective-permute-start | bytes 1720328 | tf_op jit(solution)/shard_map/ppermute | solution.py:19
  126.9 11.9 %collective-permute-start.26 = (bf16[160,1792]{1,0:T(8,128)(2,1)S(1)}, bf16[160,1792]{1,0:T(8,128)(2,1)S(1)}, u32[]{:S(2)}, u32[]{:S(2)}) collective-permute-start(bf16[160,1792]{1,0:T(8,128)(2,1)S(1)} %get-tuple-element.24), channel_id=1, source_target_pairs={{0,3},{1,0},{2,1},{3,2},{4,7},{5,4},{6,5},{7,6},{8,11},{9,8},{10,9... | collective-permute-start | bytes 1720328 | tf_op jit(solution)/shard_map/ppermute | solution.py:19
  130.3 15.9 %collective-permute-start.16 = (bf16[160,1792]{1,0:T(8,128)(2,1)S(1)}, bf16[160,1792]{1,0:T(8,128)(2,1)S(1)}, u32[]{:S(2)}, u32[]{:S(2)}) collective-permute-start(bf16[160,1792]{1,0:T(8,128)(2,1)S(1)} %get-tuple-element.17), channel_id=1, source_target_pairs={{0,4},{1,5},{2,6},{3,7},{4,8},{5,9},{6,10},{7,11},{8,12},{9,13},{1... | collective-permute-start | bytes 1720328 | tf_op jit(solution)/shard_map/ppermute | solution.py:19
  130.3 14.0 %collective-permute-start.18 = (bf16[160,1792]{1,0:T(8,128)(2,1)S(1)}, bf16[160,1792]{1,0:T(8,128)(2,1)S(1)}, u32[]{:S(2)}, u32[]{:S(2)}) collective-permute-start(bf16[160,1792]{1,0:T(8,128)(2,1)S(1)} %get-tuple-element.19), channel_id=1, source_target_pairs={{0,12},{1,13},{2,14},{3,15},{4,0},{5,1},{6,2},{7,3},{8,4},{9,5},{1... | collective-permute-start | bytes 1720328 | tf_op jit(solution)/shard_map/ppermute | solution.py:19
  132.9 11.1 %collective-permute-start.24 = (bf16[160,1792]{1,0:T(8,128)(2,1)S(1)}, bf16[160,1792]{1,0:T(8,128)(2,1)S(1)}, u32[]{:S(2)}, u32[]{:S(2)}) collective-permute-start(bf16[160,1792]{1,0:T(8,128)(2,1)S(1)} %get-tuple-element.22), channel_id=1, source_target_pairs={{0,1},{1,2},{2,3},{3,0},{4,5},{5,6},{6,7},{7,4},{8,9},{9,10},{10,1... | collective-permute-start | bytes 1720328 | tf_op jit(solution)/shard_map/ppermute | solution.py:19
  140.3 23.6 %collective-permute-start.27 = (bf16[160,3584]{1,0:T(8,128)(2,1)S(1)}, bf16[160,3584]{1,0:T(8,128)(2,1)S(1)}, u32[]{:S(2)}, u32[]{:S(2)}) collective-permute-start(bf16[160,3584]{1,0:T(8,128)(2,1)S(1)} %add_convert_fusion.1), channel_id=1, source_target_pairs={{0,3},{1,0},{2,1},{3,2},{4,7},{5,4},{6,5},{7,6},{8,11},{9,8},{10,9... | collective-permute-start | bytes 3440648 | tf_op jit(solution)/shard_map/ppermute | solution.py:19
  144.2 23.6 %collective-permute-start.25 = (bf16[160,3584]{1,0:T(8,128)(2,1)S(1)}, bf16[160,3584]{1,0:T(8,128)(2,1)S(1)}, u32[]{:S(2)}, u32[]{:S(2)}) collective-permute-start(bf16[160,3584]{1,0:T(8,128)(2,1)S(1)} %add_convert_fusion.2), channel_id=1, source_target_pairs={{0,1},{1,2},{2,3},{3,0},{4,5},{5,6},{6,7},{7,4},{8,9},{9,10},{10,1... | collective-permute-start | bytes 3440648 | tf_op jit(solution)/shard_map/ppermute | solution.py:19
  145.5 22.8 %collective-permute-start.19 = (bf16[160,3584]{1,0:T(8,128)(2,1)S(1)}, bf16[160,3584]{1,0:T(8,128)(2,1)S(1)}, u32[]{:S(2)}, u32[]{:S(2)}) collective-permute-start(bf16[160,3584]{1,0:T(8,128)(2,1)S(1)} %add_convert_fusion.4), channel_id=1, source_target_pairs={{0,12},{1,13},{2,14},{3,15},{4,0},{5,1},{6,2},{7,3},{8,4},{9,5},{1... | collective-permute-start | bytes 3440648 | tf_op jit(solution)/shard_map/ppermute | solution.py:19
  146.7 21.7 %collective-permute-start.17 = (bf16[160,3584]{1,0:T(8,128)(2,1)S(1)}, bf16[160,3584]{1,0:T(8,128)(2,1)S(1)}, u32[]{:S(2)}, u32[]{:S(2)}) collective-permute-start(bf16[160,3584]{1,0:T(8,128)(2,1)S(1)} %add_convert_fusion.5), channel_id=1, source_target_pairs={{0,4},{1,5},{2,6},{3,7},{4,8},{5,9},{6,10},{7,11},{8,12},{9,13},{1... | collective-permute-start | bytes 3440648 | tf_op jit(solution)/shard_map/ppermute | solution.py:19
  169.1 8.1 %collective-permute-start.28 = (bf16[40,1792]{1,0:T(8,128)(2,1)S(1)}, bf16[40,1792]{1,0:T(8,128)(2,1)S(1)}, u32[]{:S(2)}, u32[]{:S(2)}) collective-permute-start(bf16[40,1792]{1,0:T(8,128)(2,1)S(1)} %get-tuple-element.49), channel_id=1, source_target_pairs={{0,4},{1,5},{2,6},{3,7},{4,8},{5,9},{6,10},{7,11},{8,12},{9,13},{1... | collective-permute-start | bytes 430088 | tf_op jit(solution)/shard_map/ppermute | solution.py:19
  177.2 8.6 %collective-permute-start.29 = (bf16[40,3584]{1,0:T(8,128)(2,1)S(1)}, bf16[40,3584]{1,0:T(8,128)(2,1)S(1)}, u32[]{:S(2)}, u32[]{:S(2)}) collective-permute-start(bf16[40,3584]{1,0:T(8,128)(2,1)S(1)} %add_convert_fusion.7), channel_id=1, source_target_pairs={{0,4},{1,5},{2,6},{3,7},{4,8},{5,9},{6,10},{7,11},{8,12},{9,13},{1... | collective-permute-start | bytes 860168 | tf_op jit(solution)/shard_map/ppermute | solution.py:19
  177.3 8.6 %collective-permute-start.23 = (bf16[40,3584]{1,0:T(8,128)(2,1)S(1)}, bf16[40,3584]{1,0:T(8,128)(2,1)S(1)}, u32[]{:S(2)}, u32[]{:S(2)}) collective-permute-start(bf16[40,3584]{1,0:T(8,128)(2,1)S(1)} %add_convert_fusion.8), channel_id=1, source_target_pairs={{0,3},{1,0},{2,1},{3,2},{4,7},{5,4},{6,5},{7,6},{8,11},{9,8},{10,9... | collective-permute-start | bytes 860168 | tf_op jit(solution)/shard_map/ppermute | solution.py:19
  179.9 8.3 %collective-permute-start.21 = (bf16[40,3584]{1,0:T(8,128)(2,1)S(1)}, bf16[40,3584]{1,0:T(8,128)(2,1)S(1)}, u32[]{:S(2)}, u32[]{:S(2)}) collective-permute-start(bf16[40,3584]{1,0:T(8,128)(2,1)S(1)} %add_convert_fusion.9), channel_id=1, source_target_pairs={{0,1},{1,2},{2,3},{3,0},{4,5},{5,6},{6,7},{7,4},{8,9},{9,10},{10,1... | collective-permute-start | bytes 860168 | tf_op jit(solution)/shard_map/ppermute | solution.py:19
  (19 other events, 180.1 us)

commit v2 on v0

v2 whole, which is shorter than its diff:
```python
import jax
import jax.numpy as jnp
from jax import lax
from jax.experimental import pallas as pl
from jax.experimental.pallas import tpu as pltpu
from jax.sharding import PartitionSpec as P

SIDE = 4
CAPACITY = 2
AUX = 128
BF16, F32 = jnp.bfloat16, jnp.float32


def move(value, axis, step):
    pairs = []
    for y in range(SIDE):
        for x in range(SIDE):
            ty, tx = ((y + step) % SIDE, x) if axis == 0 else (y, (x + step) % SIDE)
            pairs.append((y * SIDE + x, ty * SIDE + tx))
    return lax.ppermute(value, "local", pairs)


def gather_direct(block, axis):
    return [block, move(block, axis, -1), move(block, axis, 1), move(block, axis, 2)]


def scatter_direct(terms, axis):
    got = [move(terms[1], axis, 1), move(terms[2], axis, -1), move(terms[3], axis, 2)]
    return sum((g.astype(F32) for g in got), terms[0].astype(F32))


def call(kernel, outs, scratch, cost, *args):
    return pl.pallas_call(
        kernel,
        out_shape=outs,
        in_specs=[pl.BlockSpec(memory_space=pltpu.VMEM)] * len(args),
        out_specs=[pl.BlockSpec(memory_space=pltpu.VMEM)] * len(outs),
        scratch_shapes=scratch,
        compiler_params=pltpu.CompilerParams(vmem_limit_bytes=28 * 1024 * 1024),
        cost_estimate=cost,
    )(*args)


def dispatch_kernel(ids, scales, placement, tokens, blocks, pick):
    own, features = tokens.shape
    nodes, routed = placement.shape[1], blocks.shape[0]
    lanes = AUX
    label = lax.broadcasted_iota(jnp.int32, (own, nodes), 1)
    hits, counts = [], jnp.zeros((own, nodes), F32)
    for k in range(ids.shape[1]):
        target = jnp.sum(jnp.where(ids[:, k : k + 1] == label, placement[...], 0), axis=1, keepdims=True)
        hits.append((target, jnp.where(target == label, 1.0, 0.0)))
        counts += hits[-1][1]
    before = jnp.where(
        lax.broadcasted_iota(jnp.int32, (own, own), 0) > lax.broadcasted_iota(jnp.int32, (own, own), 1), 1.0, 0.0
    )
    earlier = jnp.dot(before, counts, preferred_element_type=F32)
    row = lax.broadcasted_iota(jnp.int32, (own, lanes), 1)
    table, aux = jnp.zeros((own, lanes), F32), jnp.zeros((lanes, lanes), F32)
    for k, (target, hit) in enumerate(hits):
        position = jnp.sum(earlier * hit, axis=1, keepdims=True).astype(jnp.int32)
        mark = jnp.where(target * CAPACITY + position == row, 1.0, 0.0)
        scale = scales[:, k : k + 1]
        high = scale.astype(BF16).astype(F32)
        middle = (scale - high).astype(BF16).astype(F32)
        low = (scale - high - middle).astype(BF16).astype(F32)
        beside = jnp.where(row == 0, high, jnp.where(row == 1, middle, jnp.where(row == 2, low, 0.0)))
        if k == 0:
            beside = jnp.where(row == 3, 1.0, beside)
        table += mark
        aux += jnp.dot(mark.T.astype(BF16), beside.astype(BF16), preferred_element_type=F32)
    pick[...] = table
    spread = table.T[:routed].astype(BF16)
    blocks[:, 0:features] = jnp.dot(spread, tokens[...], preferred_element_type=F32).astype(BF16)
    blocks[:, features : features + AUX] = aux[:routed].astype(BF16)


def dispatch(ids, scales, placement, tokens):
    own, features = tokens.shape
    routed = placement.shape[0] * CAPACITY
    return call(
        dispatch_kernel,
        [jax.ShapeDtypeStruct((routed, features + AUX), BF16), jax.ShapeDtypeStruct((own, AUX), F32)],
        [],
        pl.CostEstimate(flops=2 * own * routed * features, bytes_accessed=4 * routed * features, transcendentals=0),
        ids,
        scales,
        placement.reshape(1, -1),
        tokens,
    )


def mlp_kernel(pieces, *refs):
    count = sum(pieces)
    ins, weights, outs = refs[:count], refs[count : count + 6], refs[count + 6 : 2 * count + 6]
    acc = refs[2 * count + 6]
    gate, up, down, shared_gate, shared_up, shared_down = weights
    features, width = gate.shape
    places, at = [], 0
    for parts in pieces:
        places.append(range(at, at + parts))
        at += parts
    rows = [ins[p[0]].shape[0] for p in places]

    def read(base, size):
        values = []
        for p in places:
            first = outs[p[0]].shape[1]
            which = min(base // first, len(p) - 1)
            values.append(ins[p[which]][:, pl.ds(base - which * first, size)])
        return jnp.concatenate(values, axis=0)

    chunk = 1792
    for base in range(0, features, chunk):
        x = read(base, chunk)
        for k, (one, two) in enumerate(((gate, up), (shared_gate, shared_up))):
            weight = jnp.concatenate([one[pl.ds(base, chunk), :], two[pl.ds(base, chunk), :]], axis=1)
            got = jnp.dot(x, weight, preferred_element_type=F32)
            acc[k] = got if base == 0 else acc[k] + got
    aux = read(features, AUX).astype(F32)
    factors = (aux[:, 0:1] + aux[:, 1:2] + aux[:, 2:3], aux[:, 3:4])
    hidden = []
    for k, factor in enumerate(factors):
        g = acc[k, :, :width]
        hidden.append((g / (1.0 + jnp.exp(-g)) * acc[k, :, width:] * factor).astype(BF16))
    hidden = jnp.concatenate(hidden, axis=1)

    step = 512
    shortest = min(o.shape[1] for o in outs)

    for start in range(0, features, shortest):

        @pl.loop(0, shortest // step)
        def _(c):
            at = pl.multiple_of(c * step, step)
            columns = pl.ds(start + at, step)
            weight = jnp.concatenate([down[:, columns], shared_down[:, columns]], axis=0)
            got = jnp.dot(hidden, weight, preferred_element_type=F32).astype(BF16)
            first = 0
            for p, n in zip(places, rows, strict=True):
                size = outs[p[0]].shape[1]
                outs[p[start // size]][:, pl.ds(start % size + at, step)] = got[first : first + n]
                first += n


def mlp(pieces, weights):
    flat = [a for p in pieces for a in p]
    counts = [len(p) for p in pieces]
    rows = sum(p[0].shape[0] for p in pieces)
    features, width = weights[0].shape
    outs = call(
        lambda *refs: mlp_kernel(counts, *refs),
        [jax.ShapeDtypeStruct((p[0].shape[0], features // len(p)), BF16) for p in pieces for _ in p],
        [pltpu.VMEM((2, rows, 2 * width), F32)],
        pl.CostEstimate(
            flops=2 * 6 * rows * features * width,
            bytes_accessed=2 * (2 * rows * features + 6 * features * width),
            transcendentals=2 * rows * width,
        ),
        *flat,
        *weights,
    )
    split, at = [], 0
    for n in counts:
        split.append(outs[at : at + n])
        at += n
    return split


def per_device(
    tokens, expert_ids, gate_scales, placement, expert_gate, expert_up, expert_down, shared_gate, shared_up, shared_down
):
    nodes = lax.axis_size("node")
    features = tokens.shape[1]
    routed = nodes * CAPACITY
    half = features // 2
    weights = (expert_gate[0], expert_up[0], expert_down[0], shared_gate, shared_up, shared_down)
    hold = lax.optimization_barrier

    blocks, pick = dispatch(expert_ids, gate_scales, placement, tokens)
    arrived = lax.all_to_all(
        blocks.reshape(nodes, CAPACITY, -1), "node", split_axis=0, concat_axis=0, tiled=True
    ).reshape(routed, -1)

    firsts, seconds = (1, 0), (0, 1)
    sets = [
        jnp.concatenate(gather_direct(part, a), axis=0)
        for part, a in zip((arrived[: routed // 2], arrived[routed // 2 :]), firsts, strict=True)
    ]
    sets = hold(sets)
    ahead = [move(s, a, -1) for s, a in zip(sets, seconds, strict=True)]
    behind = [move(s, a, 1) for s, a in zip(sets, seconds, strict=True)]
    out_own = mlp([[s] for s in sets], weights)
    ahead, behind, out_own = hold((ahead, behind, out_own))
    left = [move(s[:, :half], a, -1) for s, a in zip(ahead, seconds, strict=True)]
    right = [move(s[:, half:], a, 1) for s, a in zip(behind, seconds, strict=True)]
    out_near = mlp([[s] for s in (*ahead, *behind)], weights)
    left, right, out_near = hold((left, right, out_near))
    out_far = mlp([[p, q] for p, q in zip(left, right, strict=True)], weights)

    from_behind = [move(o[0], a, 1) for o, a in zip(out_far, seconds, strict=True)]
    from_ahead = [move(o[1], a, -1) for o, a in zip(out_far, seconds, strict=True)]
    from_behind, from_ahead = hold((from_behind, from_ahead))
    one, two = [], []
    for k, a in enumerate(seconds):
        term = out_near[k][0]
        add = (term[:, :half].astype(F32) + from_behind[k].astype(F32)).astype(BF16)
        one.append(move(lax.dynamic_update_slice(term, add, (0, 0)), a, 1))
        term = out_near[2 + k][0]
        add = (term[:, half:].astype(F32) + from_ahead[k].astype(F32)).astype(BF16)
        two.append(move(lax.dynamic_update_slice(term, add, (0, half)), a, -1))
    one, two = hold((one, two))
    summed = []
    for k, a in enumerate(firsts):
        four = (out_own[k][0].astype(F32) + one[k].astype(F32) + two[k].astype(F32)).astype(BF16)
        n = four.shape[0] // SIDE
        summed.append(scatter_direct([four[i * n : (i + 1) * n] for i in range(SIDE)], a).astype(BF16))
    back = lax.all_to_all(
        jnp.concatenate(summed, axis=0).reshape(nodes, CAPACITY, features),
        "node",
        split_axis=0,
        concat_axis=0,
        tiled=True,
    ).reshape(routed, features)
    return jnp.dot(pick[:, :routed].astype(BF16), back, preferred_element_type=F32).astype(BF16)


def solution(mesh):
    placed = (
        P(("node", "local"), None),
        P(("node", "local"), None),
        P(("node", "local"), None),
        P(),
        P("node", None, "local"),
        P("node", None, "local"),
        P("node", "local", None),
        P(None, "local"),
        P(None, "local"),
        P("local", None),
    )
    return jax.shard_map(
        per_device, mesh=mesh, in_specs=placed, out_specs=P(("node", "local"), None), check_vma=False
    )
```

time: 618 us -> 178 us (0.29)
  blocking collectives: 356 us -> 25.9 us
  waiting for transfers between devices: 189 us -> 73.2 us
  starting transfers between devices: 0.08 us -> 52.4 us
  matrix products: 31.2 us -> 0.83 us
  local copies, waits for them, and re-layouts: 26.7 us -> 9.59 us
  Pallas kernels: 0 us -> 13.7 us
  between operations: 13.2 us -> 0.3 us
    all_to_all x2 -> x1, blocking collectives: 338 us -> 25.9 us  [per_device(): lax.all_to_all(blocks.reshape(nodes, CAPACITY, -1), 'node', split_axis=0,...]
    unnamed x5 -> x0, waiting for transfers between devices: 154 us -> none
    ppermute x0 -> x28, waiting for transfers between devices: none -> 57.3 us  [move(): return lax.ppermute(value, 'local', pairs)]
    ppermute x0 -> x28, starting transfers between devices: none -> 39.1 us  [move(): return lax.ppermute(value, 'local', pairs)]
    all_gather x1 -> x0, waiting for transfers between devices: 34.7 us -> none  [per_device(): lax.all_gather(tokens, 'local', axis=0, tiled=True)]
    dot_general x6 -> x1, matrix products: 31.2 us -> 0.83 us  [per_device(): jnp.dot(pick[:, :routed].astype(BF16), back, preferred_element_type=F32)]
    all_gather x1 -> x0, blocking collectives: 17.1 us -> none  [per_device(): lax.all_gather(targets.astype(jnp.bfloat16), 'local', axis=0, tiled=True)]
    all_to_all x0 -> x1, waiting for transfers between devices: none -> 16 us  [per_device(): lax.all_to_all(jnp.concatenate(summed, axis=0).reshape(nodes, CAPACITY, f...]
  transfers between devices with their start and end apart: 3 -> 29, of which waited for: 3 -> 17; matrix products, arithmetic and copies ran while one was open for 2% -> 1% of each run, Pallas kernels for 0% -> 5%
where the time goes in v2:
time: 178 us
  waiting for transfers between devices  73.2 us (41%)
  starting transfers between devices  52.4 us (29%)
  blocking collectives  25.9 us (15%)
  Pallas kernels  13.7 us (8%)
  local copies, waits for them, and re-layouts  9.59 us (5%)
  other arithmetic  2.01 us (1%)
    ppermute x28, waiting for transfers between devices, move(): return lax.ppermute(value, 'local', pairs)  57.3 us
    ppermute x28, starting transfers between devices, move(): return lax.ppermute(value, 'local', pairs)  39.1 us
    all_to_all x1, blocking collectives, per_device(): lax.all_to_all(blocks.reshape(nodes, CAPACITY, -1), 'node', split_axis=0,...  25.9 us
    all_to_all x1, waiting for transfers between devices, per_device(): lax.all_to_all(jnp.concatenate(summed, axis=0).reshape(nodes, CAPACITY, f...  16 us
    pallas_call x4, Pallas kernels, call(): pl.pallas_call(kernel, out_shape=outs, in_specs=[pl.BlockSpec(memory_spac...  13.7 us
    all_to_all x1, starting transfers between devices, per_device(): lax.all_to_all(jnp.concatenate(summed, axis=0).reshape(nodes, CAPACITY, f...  13.3 us
    unnamed x24, local copies, waits for them, and re-layouts  7.58 us
  transfers between devices with their start and end apart: 29, of which 17 were waited for; matrix products, arithmetic and copies ran while one was open for 1% of the time, Pallas kernels for 5%

profile of v2, /device:TPU:1, one launch (start us, length us, event | category | flops | bytes accessed | tf_op | source)
XLA Modules:
  0.0 178.0 jit_solution(11433666818732967144)
XLA Ops:
  4.0 25.9 %all_to_all.10 = bf16[16,2,7296]{2,1,0:T(2,128)(2,1)S(1)} all-to-all(bf16[16,2,7296]{2,1,0:T(2,128)(2,1)S(1)} %reshape.16), channel_id=1, replica_groups=mesh['node'=16,'local'=16] {'node'}, dimensions={0} | all-to-all | bytes 933888 | tf_op jit(solution)/shard_map/all_to_all | solution.py:181
  30.3 2.8 %collective-permute-start.3 = (bf16[16,7296]{1,0:T(8,128)(2,1)S(1)}, bf16[16,7296]{1,0:T(8,128)(2,1)S(1)}, u32[]{:S(2)}, u32[]{:S(2)}) collective-permute-start(bf16[16,7296]{1,0:T(8,128)(2,1)S(1)} %slice.68), channel_id=1, source_target_pairs={{0,12},{1,13},{2,14},{3,15},{4,0},{5,1},{6,2},{7,3},{8,4},{9,5},{1... | collective-permute-start | bytes 700424 | tf_op jit(solution)/shard_map/ppermute | solution.py:20
  34.9 2.6 %collective-permute-start = (bf16[16,7296]{1,0:T(8,128)(2,1)S(1)}, bf16[16,7296]{1,0:T(8,128)(2,1)S(1)}, u32[]{:S(2)}, u32[]{:S(2)}) collective-permute-start(bf16[16,7296]{1,0:T(8,128)(2,1)S(1)} %slice.66), channel_id=1, source_target_pairs={{0,3},{1,0},{2,1},{3,2},{4,7},{5,4},{6,5},{7,6},{8,11},{9,8},{10,9... | collective-permute-start | bytes 700424 | tf_op jit(solution)/shard_map/ppermute | solution.py:20
  37.4 5.6 %collective-permute-done.3 = bf16[16,7296]{1,0:T(8,128)(2,1)S(1)} collective-permute-done((bf16[16,7296]{1,0:T(8,128)(2,1)S(1)}, bf16[16,7296]{1,0:T(8,128)(2,1)S(1)}, u32[]{:S(2)}, u32[]{:S(2)}) %collective-permute-start.3) | collective-permute-done | bytes 233504 | tf_op jit(solution)/shard_map/ppermute | solution.py:20
  43.0 2.7 %collective-permute-start.2 = (bf16[16,7296]{1,0:T(8,128)(2,1)S(1)}, bf16[16,7296]{1,0:T(8,128)(2,1)S(1)}, u32[]{:S(2)}, u32[]{:S(2)}) collective-permute-start(bf16[16,7296]{1,0:T(8,128)(2,1)S(1)} %slice.66), channel_id=1, source_target_pairs={{0,2},{1,3},{2,0},{3,1},{4,6},{5,7},{6,4},{7,5},{8,10},{9,11},{10,... | collective-permute-start | bytes 700424 | tf_op jit(solution)/shard_map/ppermute | solution.py:20
  46.5 5.5 %collective-permute-done.2 = bf16[16,7296]{1,0:T(8,128)(2,1)S(1)} collective-permute-done((bf16[16,7296]{1,0:T(8,128)(2,1)S(1)}, bf16[16,7296]{1,0:T(8,128)(2,1)S(1)}, u32[]{:S(2)}, u32[]{:S(2)}) %collective-permute-start.2) | collective-permute-done | bytes 233504 | tf_op jit(solution)/shard_map/ppermute | solution.py:20
  52.2 3.3 %collective-permute-start.6 = (bf16[64,7296]{1,0:T(8,128)(2,1)S(1)}, bf16[64,7296]{1,0:T(8,128)(2,1)S(1)}, u32[]{:S(2)}, u32[]{:S(2)}) collective-permute-start(bf16[64,7296]{1,0:T(8,128)(2,1)S(1)} %pad_maximum_fusion.refs_0_), channel_id=1, source_target_pairs={{0,12},{1,13},{2,14},{3,15},{4,0},{5,1},{6,2},{7,3},{8,4},{9,5},{1... | collective-permute-start | bytes 2801672 | tf_op jit(solution)/shard_map/ppermute | solution.py:20
  62.1 3.8 %shard_map.101 = (bf16[64,7168]{1,0:T(8,128)(2,1)S(1)}, bf16[64,7168]{1,0:T(8,128)(2,1)S(1)}) custom-call(bf16[64,7296]{1,0:T(8,128)(2,1)S(1)} %pad_maximum_fusion.refs_0_, bf16[64,7296]{1,0:T(8,128)(2,1)S(1)} %pad_maximum_fusion.1.refs_1_, bf16[7168,128]{1,0:T(8,128)(2,1)S(1)} %bitcast.5, bf16[7168,128]{1,0:T(8,128)(2,1)S(1)} %bitcast.8, ...), custom_call_target="tpu_custom_call" | custom-call | flops 1409286144 | bytes 14680064 | tf_op jit(solution)/shard_map/pallas_call | solution.py:33
  65.9 9.0 %collective-permute-done.6.refs_0_ = bf16[64,7296]{1,0:T(8,128)(2,1)S(1)} collective-permute-done((bf16[64,7296]{1,0:T(8,128)(2,1)S(1)}, bf16[64,7296]{1,0:T(8,128)(2,1)S(1)}, u32[]{:S(2)}, u32[]{:S(2)}) %collective-permute-start.6) | collective-permute-done | bytes 933920 | tf_op jit(solution)/shard_map/ppermute | solution.py:20
  76.8 2.7 %collective-permute-done.8.refs_2_ = bf16[64,7296]{1,0:T(8,128)(2,1)S(1)} collective-permute-done((bf16[64,7296]{1,0:T(8,128)(2,1)S(1)}, bf16[64,7296]{1,0:T(8,128)(2,1)S(1)}, u32[]{:S(2)}, u32[]{:S(2)}) %collective-permute-start.8) | collective-permute-done | bytes 933920 | tf_op jit(solution)/shard_map/ppermute | solution.py:20
  79.8 2.9 %collective-permute-start.10 = (bf16[64,3584]{1,0:T(8,128)(2,1)S(1)}, bf16[64,3584]{1,0:T(8,128)(2,1)S(1)}, u32[]{:S(2)}, u32[]{:S(2)}) collective-permute-start(bf16[64,3584]{1,0:T(8,128)(2,1)S(1)} %slice.69), channel_id=1, source_target_pairs={{0,12},{1,13},{2,14},{3,15},{4,0},{5,1},{6,2},{7,3},{8,4},{9,5},{1... | collective-permute-start | bytes 1376264 | tf_op jit(solution)/shard_map/ppermute | solution.py:20
  82.8 2.7 %collective-permute-start.11 = (bf16[64,3584]{1,0:T(8,128)(2,1)S(1)}, bf16[64,3584]{1,0:T(8,128)(2,1)S(1)}, u32[]{:S(2)}, u32[]{:S(2)}) collective-permute-start(bf16[64,3584]{1,0:T(8,128)(2,1)S(1)} %slice.70), channel_id=1, source_target_pairs={{0,3},{1,0},{2,1},{3,2},{4,7},{5,4},{6,5},{7,6},{8,11},{9,8},{10,9... | collective-permute-start | bytes 1376264 | tf_op jit(solution)/shard_map/ppermute | solution.py:20
  85.5 5.4 %shard_map.102 = (bf16[64,7168]{1,0:T(8,128)(2,1)S(1)}, bf16[64,7168]{1,0:T(8,128)(2,1)S(1)}, bf16[64,7168]{1,0:T(8,128)(2,1)S(1)}, bf16[64,7168]{1,0:T(8,128)(2,1)S(1)}) custom-call(bf16[64,7296]{1,0:T(8,128)(2,1)S(1)} %collective-permute-done.6.refs_0_, bf16[64,7296]{1,0:T(8,128)(2,1)S(1)} %collective-permute-done.7.refs_1_, ...), custom_call_target="tpu_custom_call" | custom-call | flops 2818572288 | bytes 18350080 | tf_op jit(solution)/shard_map/pallas_call | solution.py:33
  92.1 3.8 %shard_map.103 = (bf16[64,3584]{1,0:T(8,128)(2,1)S(1)}, bf16[64,3584]{1,0:T(8,128)(2,1)S(1)}, bf16[64,3584]{1,0:T(8,128)(2,1)S(1)}, bf16[64,3584]{1,0:T(8,128)(2,1)S(1)}) custom-call(bf16[64,3584]{1,0:T(8,128)(2,1)S(1)} %collective-permute-done.10.refs_0_, bf16[64,3712]{1,0:T(8,128)(2,1)S(1)} %collective-permute-done.12.refs_1_, ...), custom_call_target="tpu_custom_call" | custom-call | flops 1409286144 | bytes 14680064 | tf_op jit(solution)/shard_map/pallas_call | solution.py:33
  96.1 2.6 %collective-permute-start.16 = (bf16[64,3584]{1,0:T(8,128)(2,1)S(1)}, bf16[64,3584]{1,0:T(8,128)(2,1)S(1)}, u32[]{:S(2)}, u32[]{:S(2)}) collective-permute-start(bf16[64,3584]{1,0:T(8,128)(2,1)S(1)} %get-tuple-element.63), channel_id=1, source_target_pairs={{0,12},{1,13},{2,14},{3,15},{4,0},{5,1},{6,2},{7,3},{8,4},{9,5},{1... | collective-permute-start | bytes 1376264 | tf_op jit(solution)/shard_map/ppermute | solution.py:20
  98.7 3.4 %collective-permute-start.17 = (bf16[64,3584]{1,0:T(8,128)(2,1)S(1)}, bf16[64,3584]{1,0:T(8,128)(2,1)S(1)}, u32[]{:S(2)}, u32[]{:S(2)}) collective-permute-start(bf16[64,3584]{1,0:T(8,128)(2,1)S(1)} %get-tuple-element.64), channel_id=1, source_target_pairs={{0,3},{1,0},{2,1},{3,2},{4,7},{5,4},{6,5},{7,6},{8,11},{9,8},{10,9... | collective-permute-start | bytes 1376264 | tf_op jit(solution)/shard_map/ppermute | solution.py:20
  102.1 3.0 %collective-permute-done.14 = bf16[64,3584]{1,0:T(8,128)(2,1)S(1)} collective-permute-done((bf16[64,3584]{1,0:T(8,128)(2,1)S(1)}, bf16[64,3584]{1,0:T(8,128)(2,1)S(1)}, u32[]{:S(2)}, u32[]{:S(2)}) %collective-permute-start.14) | collective-permute-done | bytes 458784 | tf_op jit(solution)/shard_map/ppermute | solution.py:20
  107.8 3.5 %collective-permute-start.21 = (bf16[64,7168]{1,0:T(8,128)(2,1)S(1)}, bf16[64,7168]{1,0:T(8,128)(2,1)S(1)}, u32[]{:S(2)}, u32[]{:S(2)}) collective-permute-start(bf16[64,7168]{1,0:T(8,128)(2,1)S(1)} %fusion.3), channel_id=1, source_target_pairs={{0,3},{1,0},{2,1},{3,2},{4,7},{5,4},{6,5},{7,6},{8,11},{9,8},{10,9... | collective-permute-start | bytes 2752520 | tf_op jit(solution)/shard_map/ppermute | solution.py:20
  113.7 12.7 %collective-permute-done.21 = bf16[64,7168]{1,0:T(8,128)(2,1)S(1)} collective-permute-done((bf16[64,7168]{1,0:T(8,128)(2,1)S(1)}, bf16[64,7168]{1,0:T(8,128)(2,1)S(1)}, u32[]{:S(2)}, u32[]{:S(2)}) %collective-permute-start.21) | collective-permute-done | bytes 917536 | tf_op jit(solution)/shard_map/ppermute | solution.py:20
  128.9 2.7 %collective-permute-start.23 = (bf16[16,7168]{1,0:T(8,128)(2,1)S(1)}, bf16[16,7168]{1,0:T(8,128)(2,1)S(1)}, u32[]{:S(2)}, u32[]{:S(2)}) collective-permute-start(bf16[16,7168]{1,0:T(8,128)(2,1)S(1)} %get-tuple-element.79), channel_id=1, source_target_pairs={{0,3},{1,0},{2,1},{3,2},{4,7},{5,4},{6,5},{7,6},{8,11},{9,8},{10,9... | collective-permute-start | bytes 688136 | tf_op jit(solution)/shard_map/ppermute | solution.py:20
  135.6 4.6 %collective-permute-done.22 = bf16[16,7168]{1,0:T(8,128)(2,1)S(1)} collective-permute-done((bf16[16,7168]{1,0:T(8,128)(2,1)S(1)}, bf16[16,7168]{1,0:T(8,128)(2,1)S(1)}, u32[]{:S(2)}, u32[]{:S(2)}) %collective-permute-start.22) | collective-permute-done | bytes 229408 | tf_op jit(solution)/shard_map/ppermute | solution.py:20
  140.8 5.8 %collective-permute-done.27 = bf16[16,7168]{1,0:T(8,128)(2,1)S(1)} collective-permute-done((bf16[16,7168]{1,0:T(8,128)(2,1)S(1)}, bf16[16,7168]{1,0:T(8,128)(2,1)S(1)}, u32[]{:S(2)}, u32[]{:S(2)}) %collective-permute-start.27) | collective-permute-done | bytes 229408 | tf_op jit(solution)/shard_map/ppermute | solution.py:20
  147.7 13.3 %all-to-all-start.1 = ((bf16[16,2,7168]{2,1,0:T(2,128)(2,1)}), bf16[16,2,7168]{2,1,0:T(2,128)(2,1)S(1)}, u32[]{:S(2)}, u32[]{:S(2)}) async-start(bf16[16,2,7168]{2,1,0:T(2,128)(2,1)} %reshape.17), calls=%async_computation.1 | async-start | bytes 917504 | tf_op jit(solution)/shard_map/all_to_all | solution.py:218
  161.0 16.0 %all-to-all-done.1 = bf16[16,2,7168]{2,1,0:T(2,128)(2,1)S(1)} async-done(((bf16[16,2,7168]{2,1,0:T(2,128)(2,1)}), bf16[16,2,7168]{2,1,0:T(2,128)(2,1)S(1)}, u32[]{:S(2)}, u32[]{:S(2)}) %all-to-all-start.1) | async-done | bytes 458784 | tf_op jit(solution)/shard_map/all_to_all | solution.py:218
  (88 shorter events, 31.3 us)
Async XLA Ops:
  30.3 12.7 %collective-permute-start.3 = (bf16[16,7296]{1,0:T(8,128)(2,1)S(1)}, bf16[16,7296]{1,0:T(8,128)(2,1)S(1)}, u32[]{:S(2)}, u32[]{:S(2)}) collective-permute-start(bf16[16,7296]{1,0:T(8,128)(2,1)S(1)} %slice.68), channel_id=1, source_target_pairs={{0,12},{1,13},{2,14},{3,15},{4,0},{5,1},{6,2},{7,3},{8,4},{9,5},{1... | collective-permute-start | bytes 700424 | tf_op jit(solution)/shard_map/ppermute | solution.py:20
  33.1 13.3 %collective-permute-start.4 = (bf16[16,7296]{1,0:T(8,128)(2,1)S(1)}, bf16[16,7296]{1,0:T(8,128)(2,1)S(1)}, u32[]{:S(2)}, u32[]{:S(2)}) collective-permute-start(bf16[16,7296]{1,0:T(8,128)(2,1)S(1)} %slice.68), channel_id=1, source_target_pairs={{0,4},{1,5},{2,6},{3,7},{4,8},{5,9},{6,10},{7,11},{8,12},{9,13},{1... | collective-permute-start | bytes 700424 | tf_op jit(solution)/shard_map/ppermute | solution.py:20
  33.1 13.3 %collective-permute-start.5 = (bf16[16,7296]{1,0:T(8,128)(2,1)S(1)}, bf16[16,7296]{1,0:T(8,128)(2,1)S(1)}, u32[]{:S(2)}, u32[]{:S(2)}) collective-permute-start(bf16[16,7296]{1,0:T(8,128)(2,1)S(1)} %slice.68), channel_id=1, source_target_pairs={{0,8},{1,9},{2,10},{3,11},{4,12},{5,13},{6,14},{7,15},{8,0},{9,1},... | collective-permute-start | bytes 700424 | tf_op jit(solution)/shard_map/ppermute | solution.py:20
  34.9 11.6 %collective-permute-start = (bf16[16,7296]{1,0:T(8,128)(2,1)S(1)}, bf16[16,7296]{1,0:T(8,128)(2,1)S(1)}, u32[]{:S(2)}, u32[]{:S(2)}) collective-permute-start(bf16[16,7296]{1,0:T(8,128)(2,1)S(1)} %slice.66), channel_id=1, source_target_pairs={{0,3},{1,0},{2,1},{3,2},{4,7},{5,4},{6,5},{7,6},{8,11},{9,8},{10,9... | collective-permute-start | bytes 700424 | tf_op jit(solution)/shard_map/ppermute | solution.py:20
  37.4 9.1 %collective-permute-start.1 = (bf16[16,7296]{1,0:T(8,128)(2,1)S(1)}, bf16[16,7296]{1,0:T(8,128)(2,1)S(1)}, u32[]{:S(2)}, u32[]{:S(2)}) collective-permute-start(bf16[16,7296]{1,0:T(8,128)(2,1)S(1)} %slice.66), channel_id=1, source_target_pairs={{0,1},{1,2},{2,3},{3,0},{4,5},{5,6},{6,7},{7,4},{8,9},{9,10},{10,1... | collective-permute-start | bytes 700424 | tf_op jit(solution)/shard_map/ppermute | solution.py:20
  52.2 22.7 %collective-permute-start.6 = (bf16[64,7296]{1,0:T(8,128)(2,1)S(1)}, bf16[64,7296]{1,0:T(8,128)(2,1)S(1)}, u32[]{:S(2)}, u32[]{:S(2)}) collective-permute-start(bf16[64,7296]{1,0:T(8,128)(2,1)S(1)} %pad_maximum_fusion.refs_0_), channel_id=1, source_target_pairs={{0,12},{1,13},{2,14},{3,15},{4,0},{5,1},{6,2},{7,3},{8,4},{9,5},{1... | collective-permute-start | bytes 2801672 | tf_op jit(solution)/shard_map/ppermute | solution.py:20
  55.5 21.3 %collective-permute-start.7 = (bf16[64,7296]{1,0:T(8,128)(2,1)S(1)}, bf16[64,7296]{1,0:T(8,128)(2,1)S(1)}, u32[]{:S(2)}, u32[]{:S(2)}) collective-permute-start(bf16[64,7296]{1,0:T(8,128)(2,1)S(1)} %pad_maximum_fusion.1.refs_1_), channel_id=1, source_target_pairs={{0,3},{1,0},{2,1},{3,2},{4,7},{5,4},{6,5},{7,6},{8,11},{9,8},{10,9... | collective-permute-start | bytes 2801672 | tf_op jit(solution)/shard_map/ppermute | solution.py:20
  57.5 22.0 %collective-permute-start.8 = (bf16[64,7296]{1,0:T(8,128)(2,1)S(1)}, bf16[64,7296]{1,0:T(8,128)(2,1)S(1)}, u32[]{:S(2)}, u32[]{:S(2)}) collective-permute-start(bf16[64,7296]{1,0:T(8,128)(2,1)S(1)} %pad_maximum_fusion.refs_0_), channel_id=1, source_target_pairs={{0,4},{1,5},{2,6},{3,7},{4,8},{5,9},{6,10},{7,11},{8,12},{9,13},{1... | collective-permute-start | bytes 2801672 | tf_op jit(solution)/shard_map/ppermute | solution.py:20
  57.5 22.0 %collective-permute-start.9 = (bf16[64,7296]{1,0:T(8,128)(2,1)S(1)}, bf16[64,7296]{1,0:T(8,128)(2,1)S(1)}, u32[]{:S(2)}, u32[]{:S(2)}) collective-permute-start(bf16[64,7296]{1,0:T(8,128)(2,1)S(1)} %pad_maximum_fusion.1.refs_1_), channel_id=1, source_target_pairs={{0,1},{1,2},{2,3},{3,0},{4,5},{5,6},{6,7},{7,4},{8,9},{9,10},{10,1... | collective-permute-start | bytes 2801672 | tf_op jit(solution)/shard_map/ppermute | solution.py:20
  79.5 12.6 %collective-permute-start.12 = (bf16[64,3712]{1,0:T(8,128)(2,1)S(1)}, bf16[64,3712]{1,0:T(8,128)(2,1)S(1)}, u32[]{:S(2)}, u32[]{:S(2)}) collective-permute-start(bf16[64,3712]{1,0:T(8,128)(2,1)S(1)} %slice.71), channel_id=1, source_target_pairs={{0,4},{1,5},{2,6},{3,7},{4,8},{5,9},{6,10},{7,11},{8,12},{9,13},{1... | collective-permute-start | bytes 1425416 | tf_op jit(solution)/shard_map/ppermute | solution.py:20
  79.7 12.4 %collective-permute-start.13 = (bf16[64,3712]{1,0:T(8,128)(2,1)S(1)}, bf16[64,3712]{1,0:T(8,128)(2,1)S(1)}, u32[]{:S(2)}, u32[]{:S(2)}) collective-permute-start(bf16[64,3712]{1,0:T(8,128)(2,1)S(1)} %slice.72), channel_id=1, source_target_pairs={{0,1},{1,2},{2,3},{3,0},{4,5},{5,6},{6,7},{7,4},{8,9},{9,10},{10,1... | collective-permute-start | bytes 1425416 | tf_op jit(solution)/shard_map/ppermute | solution.py:20
  79.8 11.1 %collective-permute-start.10 = (bf16[64,3584]{1,0:T(8,128)(2,1)S(1)}, bf16[64,3584]{1,0:T(8,128)(2,1)S(1)}, u32[]{:S(2)}, u32[]{:S(2)}) collective-permute-start(bf16[64,3584]{1,0:T(8,128)(2,1)S(1)} %slice.69), channel_id=1, source_target_pairs={{0,12},{1,13},{2,14},{3,15},{4,0},{5,1},{6,2},{7,3},{8,4},{9,5},{1... | collective-permute-start | bytes 1376264 | tf_op jit(solution)/shard_map/ppermute | solution.py:20
  82.8 9.4 %collective-permute-start.11 = (bf16[64,3584]{1,0:T(8,128)(2,1)S(1)}, bf16[64,3584]{1,0:T(8,128)(2,1)S(1)}, u32[]{:S(2)}, u32[]{:S(2)}) collective-permute-start(bf16[64,3584]{1,0:T(8,128)(2,1)S(1)} %slice.70), channel_id=1, source_target_pairs={{0,3},{1,0},{2,1},{3,2},{4,7},{5,4},{6,5},{7,6},{8,11},{9,8},{10,9... | collective-permute-start | bytes 1376264 | tf_op jit(solution)/shard_map/ppermute | solution.py:20
  96.0 9.2 %collective-permute-start.14 = (bf16[64,3584]{1,0:T(8,128)(2,1)S(1)}, bf16[64,3584]{1,0:T(8,128)(2,1)S(1)}, u32[]{:S(2)}, u32[]{:S(2)}) collective-permute-start(bf16[64,3584]{1,0:T(8,128)(2,1)S(1)} %get-tuple-element.61), channel_id=1, source_target_pairs={{0,4},{1,5},{2,6},{3,7},{4,8},{5,9},{6,10},{7,11},{8,12},{9,13},{1... | collective-permute-start | bytes 1376264 | tf_op jit(solution)/shard_map/ppermute | solution.py:20
  96.0 10.2 %collective-permute-start.15 = (bf16[64,3584]{1,0:T(8,128)(2,1)S(1)}, bf16[64,3584]{1,0:T(8,128)(2,1)S(1)}, u32[]{:S(2)}, u32[]{:S(2)}) collective-permute-start(bf16[64,3584]{1,0:T(8,128)(2,1)S(1)} %get-tuple-element.62), channel_id=1, source_target_pairs={{0,1},{1,2},{2,3},{3,0},{4,5},{5,6},{6,7},{7,4},{8,9},{9,10},{10,1... | collective-permute-start | bytes 1376264 | tf_op jit(solution)/shard_map/ppermute | solution.py:20
  96.1 10.1 %collective-permute-start.16 = (bf16[64,3584]{1,0:T(8,128)(2,1)S(1)}, bf16[64,3584]{1,0:T(8,128)(2,1)S(1)}, u32[]{:S(2)}, u32[]{:S(2)}) collective-permute-start(bf16[64,3584]{1,0:T(8,128)(2,1)S(1)} %get-tuple-element.63), channel_id=1, source_target_pairs={{0,12},{1,13},{2,14},{3,15},{4,0},{5,1},{6,2},{7,3},{8,4},{9,5},{1... | collective-permute-start | bytes 1376264 | tf_op jit(solution)/shard_map/ppermute | solution.py:20
  107.8 18.6 %collective-permute-start.21 = (bf16[64,7168]{1,0:T(8,128)(2,1)S(1)}, bf16[64,7168]{1,0:T(8,128)(2,1)S(1)}, u32[]{:S(2)}, u32[]{:S(2)}) collective-permute-start(bf16[64,7168]{1,0:T(8,128)(2,1)S(1)} %fusion.3), channel_id=1, source_target_pairs={{0,3},{1,0},{2,1},{3,2},{4,7},{5,4},{6,5},{7,6},{8,11},{9,8},{10,9... | collective-permute-start | bytes 2752520 | tf_op jit(solution)/shard_map/ppermute | solution.py:20
  111.5 15.3 %collective-permute-start.20 = (bf16[64,7168]{1,0:T(8,128)(2,1)S(1)}, bf16[64,7168]{1,0:T(8,128)(2,1)S(1)}, u32[]{:S(2)}, u32[]{:S(2)}) collective-permute-start(bf16[64,7168]{1,0:T(8,128)(2,1)S(1)} %fusion.2), channel_id=1, source_target_pairs={{0,12},{1,13},{2,14},{3,15},{4,0},{5,1},{6,2},{7,3},{8,4},{9,5},{1... | collective-permute-start | bytes 2752520 | tf_op jit(solution)/shard_map/ppermute | solution.py:20
  111.8 16.3 %collective-permute-start.19 = (bf16[64,7168]{1,0:T(8,128)(2,1)S(1)}, bf16[64,7168]{1,0:T(8,128)(2,1)S(1)}, u32[]{:S(2)}, u32[]{:S(2)}) collective-permute-start(bf16[64,7168]{1,0:T(8,128)(2,1)S(1)} %fusion.1), channel_id=1, source_target_pairs={{0,1},{1,2},{2,3},{3,0},{4,5},{5,6},{6,7},{7,4},{8,9},{9,10},{10,1... | collective-permute-start | bytes 2752520 | tf_op jit(solution)/shard_map/ppermute | solution.py:20
  112.1 16.3 %collective-permute-start.18 = (bf16[64,7168]{1,0:T(8,128)(2,1)S(1)}, bf16[64,7168]{1,0:T(8,128)(2,1)S(1)}, u32[]{:S(2)}, u32[]{:S(2)}) collective-permute-start(bf16[64,7168]{1,0:T(8,128)(2,1)S(1)} %fusion), channel_id=1, source_target_pairs={{0,4},{1,5},{2,6},{3,7},{4,8},{5,9},{6,10},{7,11},{8,12},{9,13},{1... | collective-permute-start | bytes 2752520 | tf_op jit(solution)/shard_map/ppermute | solution.py:20
  128.8 11.4 %collective-permute-start.22 = (bf16[16,7168]{1,0:T(8,128)(2,1)S(1)}, bf16[16,7168]{1,0:T(8,128)(2,1)S(1)}, u32[]{:S(2)}, u32[]{:S(2)}) collective-permute-start(bf16[16,7168]{1,0:T(8,128)(2,1)S(1)} %get-tuple-element.77), channel_id=1, source_target_pairs={{0,1},{1,2},{2,3},{3,0},{4,5},{5,6},{6,7},{7,4},{8,9},{9,10},{10,1... | collective-permute-start | bytes 688136 | tf_op jit(solution)/shard_map/ppermute | solution.py:20
  128.9 11.8 %collective-permute-start.23 = (bf16[16,7168]{1,0:T(8,128)(2,1)S(1)}, bf16[16,7168]{1,0:T(8,128)(2,1)S(1)}, u32[]{:S(2)}, u32[]{:S(2)}) collective-permute-start(bf16[16,7168]{1,0:T(8,128)(2,1)S(1)} %get-tuple-element.79), channel_id=1, source_target_pairs={{0,3},{1,0},{2,1},{3,2},{4,7},{5,4},{6,5},{7,6},{8,11},{9,8},{10,9... | collective-permute-start | bytes 688136 | tf_op jit(solution)/shard_map/ppermute | solution.py:20
  131.6 9.1 %collective-permute-start.24 = (bf16[16,7168]{1,0:T(8,128)(2,1)S(1)}, bf16[16,7168]{1,0:T(8,128)(2,1)S(1)}, u32[]{:S(2)}, u32[]{:S(2)}) collective-permute-start(bf16[16,7168]{1,0:T(8,128)(2,1)S(1)} %get-tuple-element.78), channel_id=1, source_target_pairs={{0,2},{1,3},{2,0},{3,1},{4,6},{5,7},{6,4},{7,5},{8,10},{9,11},{10,... | collective-permute-start | bytes 688136 | tf_op jit(solution)/shard_map/ppermute | solution.py:20
  147.7 29.3 %all-to-all-start.1 = ((bf16[16,2,7168]{2,1,0:T(2,128)(2,1)}), bf16[16,2,7168]{2,1,0:T(2,128)(2,1)S(1)}, u32[]{:S(2)}, u32[]{:S(2)}) async-start(bf16[16,2,7168]{2,1,0:T(2,128)(2,1)} %reshape.17), calls=%async_computation.1 | async-start | bytes 917504 | tf_op jit(solution)/shard_map/all_to_all | solution.py:218
  (16 other events, 154.5 us)

commit v3 on v2

--- a/solution.py
+++ b/solution.py
@@ -6,26 +6,32 @@
 from jax.sharding import PartitionSpec as P
 
 SIDE = 4
+NODES, CORES = 16, 2
 CAPACITY = 2
 AUX = 128
 BF16, F32 = jnp.bfloat16, jnp.float32
 
 
-def move(value, axis, step):
+def move(value, phase, step):
     pairs = []
-    for y in range(SIDE):
-        for x in range(SIDE):
-            ty, tx = ((y + step) % SIDE, x) if axis == 0 else (y, (x + step) % SIDE)
-            pairs.append((y * SIDE + x, ty * SIDE + tx))
-    return lax.ppermute(value, "local", pairs)
-
-
-def gather_direct(block, axis):
-    return [block, move(block, axis, -1), move(block, axis, 1), move(block, axis, 2)]
-
-
-def scatter_direct(terms, axis):
-    got = [move(terms[1], axis, 1), move(terms[2], axis, -1), move(terms[3], axis, 2)]
+    for node in range(NODES):
+        for y in range(SIDE):
+            for x in range(SIDE):
+                if node % CORES == phase:
+                    ty, tx = y, (x + step) % SIDE
+                else:
+                    ty, tx = (y + step) % SIDE, x
+                base = node * SIDE * SIDE
+                pairs.append((base + y * SIDE + x, base + ty * SIDE + tx))
+    return lax.ppermute(value, ("node", "local"), pairs)
+
+
+def gather_direct(block, phase):
+    return [block, move(block, phase, -1), move(block, phase, 1), move(block, phase, 2)]
+
+
+def scatter_direct(terms, phase):
+    got = [move(terms[1], phase, 1), move(terms[2], phase, -1), move(terms[3], phase, 2)]
     return sum((g.astype(F32) for g in got), terms[0].astype(F32))
 
 
@@ -44,35 +50,38 @@
 def dispatch_kernel(ids, scales, placement, tokens, blocks, pick):
     own, features = tokens.shape
     nodes, routed = placement.shape[1], blocks.shape[0]
-    lanes = AUX
-    label = lax.broadcasted_iota(jnp.int32, (own, nodes), 1)
-    hits, counts = [], jnp.zeros((own, nodes), F32)
-    for k in range(ids.shape[1]):
-        target = jnp.sum(jnp.where(ids[:, k : k + 1] == label, placement[...], 0), axis=1, keepdims=True)
+
+    def iota(shape, axis):
+        return lax.broadcasted_iota(jnp.int32, shape, axis)
+
+    square = (nodes, nodes)
+    place = jnp.sum(jnp.where(iota(square, 0) == iota(square, 1), placement[...], 0), axis=1, keepdims=True)
+    label = iota((nodes, own), 0)
+    hits, counts = [], jnp.zeros((nodes, own), F32)
+    for k in range(ids.shape[0]):
+        target = jnp.sum(jnp.where(ids[k : k + 1, :] == label, place, 0), axis=0, keepdims=True)
         hits.append((target, jnp.where(target == label, 1.0, 0.0)))
         counts += hits[-1][1]
-    before = jnp.where(
-        lax.broadcasted_iota(jnp.int32, (own, own), 0) > lax.broadcasted_iota(jnp.int32, (own, own), 1), 1.0, 0.0
-    )
-    earlier = jnp.dot(before, counts, preferred_element_type=F32)
-    row = lax.broadcasted_iota(jnp.int32, (own, lanes), 1)
-    table, aux = jnp.zeros((own, lanes), F32), jnp.zeros((lanes, lanes), F32)
+    before = jnp.where(iota((own, own), 0) < iota((own, own), 1), 1.0, 0.0)
+    earlier = jnp.dot(counts, before, preferred_element_type=F32)
+    row = iota((routed, own), 0)
+    table, scale = jnp.zeros((routed, own), F32), jnp.zeros((routed, 1), F32)
     for k, (target, hit) in enumerate(hits):
-        position = jnp.sum(earlier * hit, axis=1, keepdims=True).astype(jnp.int32)
+        position = jnp.sum(earlier * hit, axis=0, keepdims=True).astype(jnp.int32)
         mark = jnp.where(target * CAPACITY + position == row, 1.0, 0.0)
-        scale = scales[:, k : k + 1]
-        high = scale.astype(BF16).astype(F32)
-        middle = (scale - high).astype(BF16).astype(F32)
-        low = (scale - high - middle).astype(BF16).astype(F32)
-        beside = jnp.where(row == 0, high, jnp.where(row == 1, middle, jnp.where(row == 2, low, 0.0)))
+        table += mark
+        scale += jnp.sum(mark * scales[k : k + 1, :], axis=1, keepdims=True)
         if k == 0:
-            beside = jnp.where(row == 3, 1.0, beside)
-        table += mark
-        aux += jnp.dot(mark.T.astype(BF16), beside.astype(BF16), preferred_element_type=F32)
+            flag = jnp.sum(mark, axis=1, keepdims=True)
+    high = scale.astype(BF16).astype(F32)
+    middle = (scale - high).astype(BF16).astype(F32)
+    low = scale - high - middle
+    column = iota((routed, AUX), 1)
+    aux = jnp.where(column == 0, high, jnp.where(column == 1, middle, jnp.where(column == 2, low, 0.0)))
+    aux = jnp.where(column == 3, flag, aux)
     pick[...] = table
-    spread = table.T[:routed].astype(BF16)
-    blocks[:, 0:features] = jnp.dot(spread, tokens[...], preferred_element_type=F32).astype(BF16)
-    blocks[:, features : features + AUX] = aux[:routed].astype(BF16)
+    blocks[:, 0:features] = jnp.dot(table.astype(BF16), tokens[...], preferred_element_type=F32).astype(BF16)
+    blocks[:, features : features + AUX] = aux.astype(BF16)
 
 
 def dispatch(ids, scales, placement, tokens):
@@ -80,11 +89,11 @@
     routed = placement.shape[0] * CAPACITY
     return call(
         dispatch_kernel,
-        [jax.ShapeDtypeStruct((routed, features + AUX), BF16), jax.ShapeDtypeStruct((own, AUX), F32)],
+        [jax.ShapeDtypeStruct((routed, features + AUX), BF16), jax.ShapeDtypeStruct((routed, own), F32)],
         [],
         pl.CostEstimate(flops=2 * own * routed * features, bytes_accessed=4 * routed * features, transcendentals=0),
-        ids,
-        scales,
+        ids.T,
+        scales.T,
         placement.reshape(1, -1),
         tokens,
     )
@@ -182,47 +191,36 @@
         blocks.reshape(nodes, CAPACITY, -1), "node", split_axis=0, concat_axis=0, tiled=True
     ).reshape(routed, -1)
 
-    firsts, seconds = (1, 0), (0, 1)
-    sets = [
-        jnp.concatenate(gather_direct(part, a), axis=0)
-        for part, a in zip((arrived[: routed // 2], arrived[routed // 2 :]), firsts, strict=True)
-    ]
-    sets = hold(sets)
-    ahead = [move(s, a, -1) for s, a in zip(sets, seconds, strict=True)]
-    behind = [move(s, a, 1) for s, a in zip(sets, seconds, strict=True)]
-    out_own = mlp([[s] for s in sets], weights)
-    ahead, behind, out_own = hold((ahead, behind, out_own))
-    left = [move(s[:, :half], a, -1) for s, a in zip(ahead, seconds, strict=True)]
-    right = [move(s[:, half:], a, 1) for s, a in zip(behind, seconds, strict=True)]
-    out_near = mlp([[s] for s in (*ahead, *behind)], weights)
-    left, right, out_near = hold((left, right, out_near))
-    out_far = mlp([[p, q] for p, q in zip(left, right, strict=True)], weights)
-
-    from_behind = [move(o[0], a, 1) for o, a in zip(out_far, seconds, strict=True)]
-    from_ahead = [move(o[1], a, -1) for o, a in zip(out_far, seconds, strict=True)]
-    from_behind, from_ahead = hold((from_behind, from_ahead))
-    one, two = [], []
-    for k, a in enumerate(seconds):
-        term = out_near[k][0]
-        add = (term[:, :half].astype(F32) + from_behind[k].astype(F32)).astype(BF16)
-        one.append(move(lax.dynamic_update_slice(term, add, (0, 0)), a, 1))
-        term = out_near[2 + k][0]
-        add = (term[:, half:].astype(F32) + from_ahead[k].astype(F32)).astype(BF16)
-        two.append(move(lax.dynamic_update_slice(term, add, (0, half)), a, -1))
-    one, two = hold((one, two))
+    size = routed // 2
+    near = [jnp.concatenate(gather_direct(arrived[h * size : (h + 1) * size], 0), axis=0) for h in range(2)]
+    ahead, behind = [move(n, 1, -1) for n in near], [move(n, 1, 1) for n in near]
+    out_own = mlp([[n] for n in near], weights)
+    ahead[0], behind[0], out_own = hold((ahead[0], behind[0], out_own))
+    left = [move(v[:, :half], 1, -1) for v in ahead]
+    right = [move(v[:, half:], 1, 1) for v in behind]
+    out_near = [mlp([[ahead[0]], [behind[0]]], weights)]
+    left[0], right[0], out_near = hold((left[0], right[0], out_near))
+    out_far = [mlp([[p, q]], weights)[0] for p, q in zip(left, right, strict=True)]
+    ahead[1], behind[1], out_far[1] = hold((ahead[1], behind[1], out_far[1]))
+    out_near.append(mlp([[ahead[1]], [behind[1]]], weights))
+
     summed = []
-    for k, a in enumerate(firsts):
-        four = (out_own[k][0].astype(F32) + one[k].astype(F32) + two[k].astype(F32)).astype(BF16)
-        n = four.shape[0] // SIDE
-        summed.append(scatter_direct([four[i * n : (i + 1) * n] for i in range(SIDE)], a).astype(BF16))
+    for h in range(2):
+        from_behind, from_ahead = move(out_far[h][0], 1, 1), move(out_far[h][1], 1, -1)
+        (out_ahead,), (out_behind,) = out_near[h]
+        add = (out_ahead[:, :half].astype(F32) + from_behind.astype(F32)).astype(BF16)
+        one = move(lax.dynamic_update_slice(out_ahead, add, (0, 0)), 1, 1)
+        add = (out_behind[:, half:].astype(F32) + from_ahead.astype(F32)).astype(BF16)
+        two = move(lax.dynamic_update_slice(out_behind, add, (0, half)), 1, -1)
+        four = (out_own[h][0].astype(F32) + one.astype(F32) + two.astype(F32)).astype(BF16)
+        summed.append(scatter_direct([four[i * size : (i + 1) * size] for i in range(SIDE)], 0).astype(BF16))
+    summed = jnp.concatenate(summed, axis=0)
     back = lax.all_to_all(
-        jnp.concatenate(summed, axis=0).reshape(nodes, CAPACITY, features),
-        "node",
-        split_axis=0,
-        concat_axis=0,
-        tiled=True,
+        summed.reshape(nodes, CAPACITY, features), "node", split_axis=0, concat_axis=0, tiled=True
     ).reshape(routed, features)
-    return jnp.dot(pick[:, :routed].astype(BF16), back, preferred_element_type=F32).astype(BF16)
+    return lax.dot_general(
+        pick.astype(BF16), back, (((0,), (0,)), ((), ())), preferred_element_type=F32
+    ).astype(BF16)
 
 
 def solution(mesh):

time: 178 us -> 164 us (0.921)
  waiting for transfers between devices: 73.2 us -> 34.6 us
  blocking collectives: 25.9 us -> 57.6 us
  starting transfers between devices: 52.4 us -> 35.9 us
  Pallas kernels: 13.7 us -> 19.4 us
  local copies, waits for them, and re-layouts: 9.59 us -> 13.2 us
    all_to_all x0 -> x1, blocking collectives: none -> 31.7 us  [per_device(): lax.all_to_all(summed.reshape(nodes, CAPACITY, features), 'node', split_a...]
    ppermute x28, waiting for transfers between devices: 57.3 us -> 34.6 us  [move(): return lax.ppermute(value, ('node', 'local'), pairs)]
    all_to_all x1 -> x0, waiting for transfers between devices: 16 us -> none  [per_device(): lax.all_to_all(jnp.concatenate(summed, axis=0).reshape(nodes, CAPACITY, f...]
    all_to_all x1 -> x0, starting transfers between devices: 13.3 us -> none  [per_device(): lax.all_to_all(jnp.concatenate(summed, axis=0).reshape(nodes, CAPACITY, f...]
    pallas_call x4 -> x6, Pallas kernels: 13.7 us -> 19.4 us  [call(): pl.pallas_call(kernel, out_shape=outs, in_specs=[pl.BlockSpec(memory_spac...]
    unnamed x24 -> x34, local copies, waits for them, and re-layouts: 7.58 us -> 10.9 us
    ppermute x28, starting transfers between devices: 39.1 us -> 35.9 us  [move(): return lax.ppermute(value, ('node', 'local'), pairs)]
  transfers between devices with their start and end apart: 29 -> 28, of which waited for: 17 -> 7; matrix products, arithmetic and copies ran while one was open for 1% -> 3% of each run, Pallas kernels for 5% -> 12%
where the time goes in v3:
time: 164 us
  blocking collectives  57.6 us (35%)
  starting transfers between devices  35.9 us (22%)
  waiting for transfers between devices  34.6 us (21%)
  Pallas kernels  19.4 us (12%)
  local copies, waits for them, and re-layouts  13.2 us (8%)
  other arithmetic  1.84 us (1%)
    ppermute x28, starting transfers between devices, move(): return lax.ppermute(value, ('node', 'local'), pairs)  35.9 us
    ppermute x28, waiting for transfers between devices, move(): return lax.ppermute(value, ('node', 'local'), pairs)  34.6 us
    all_to_all x1, blocking collectives, per_device(): lax.all_to_all(summed.reshape(nodes, CAPACITY, features), 'node', split_a...  31.7 us
    all_to_all x1, blocking collectives, per_device(): lax.all_to_all(blocks.reshape(nodes, CAPACITY, -1), 'node', split_axis=0,...  25.9 us
    pallas_call x6, Pallas kernels, call(): pl.pallas_call(kernel, out_shape=outs, in_specs=[pl.BlockSpec(memory_spac...  19.4 us
    unnamed x34, local copies, waits for them, and re-layouts  10.9 us
  transfers between devices with their start and end apart: 28, of which 7 were waited for; matrix products, arithmetic and copies ran while one was open for 3% of the time, Pallas kernels for 12%

profile of v3, /device:TPU:1, one launch (start us, length us, event | category | flops | bytes accessed | tf_op | source)
XLA Modules:
  0.0 163.9 jit_solution(9100439372015987221)
XLA Ops:
  3.6 25.9 %all_to_all.10 = bf16[16,2,7296]{2,1,0:T(2,128)(2,1)S(1)} all-to-all(bf16[16,2,7296]{2,1,0:T(2,128)(2,1)S(1)} %reshape.16), channel_id=1, replica_groups=mesh['node'=16,'local'=16] {'node'}, dimensions={0} | all-to-all | bytes 933888 | tf_op jit(solution)/shard_map/all_to_all | solution.py:190
  29.9 2.8 %collective-permute-start = (bf16[16,7296]{1,0:T(8,128)(2,1)S(1)}, bf16[16,7296]{1,0:T(8,128)(2,1)}, u32[]{:S(2)}, u32[]{:S(2)}) collective-permute-start(bf16[16,7296]{1,0:T(8,128)(2,1)S(1)} %slice.61), channel_id=1, source_target_pairs={{0,3},{1,0},{2,1},{3,2},{4,7},{5,4},{6,5},{7,6},{8,11},{9,8},{10,9... | collective-permute-start | bytes 700424 | tf_op jit(solution)/shard_map/ppermute | solution.py:26
  32.8 1.6 %collective-permute-start.2 = (bf16[16,7296]{1,0:T(8,128)(2,1)S(1)}, bf16[16,7296]{1,0:T(8,128)(2,1)}, u32[]{:S(2)}, u32[]{:S(2)}) collective-permute-start(bf16[16,7296]{1,0:T(8,128)(2,1)S(1)} %slice.61), channel_id=1, source_target_pairs={{0,2},{1,3},{2,0},{3,1},{4,6},{5,7},{6,4},{7,5},{8,10},{9,11},{10,... | collective-permute-start | bytes 700424 | tf_op jit(solution)/shard_map/ppermute | solution.py:26
  36.3 1.7 %collective-permute-start.7 = (bf16[16,7296]{1,0:T(8,128)(2,1)S(1)}, bf16[16,7296]{1,0:T(8,128)(2,1)S(1)}, u32[]{:S(2)}, u32[]{:S(2)}) collective-permute-start(bf16[16,7296]{1,0:T(8,128)(2,1)S(1)} %slice.63), channel_id=1, source_target_pairs={{0,2},{1,3},{2,0},{3,1},{4,6},{5,7},{6,4},{7,5},{8,10},{9,11},{10,... | collective-permute-start | bytes 700424 | tf_op jit(solution)/shard_map/ppermute | solution.py:26
  39.0 2.7 %collective-permute-done.1 = bf16[16,7296]{1,0:T(8,128)(2,1)} collective-permute-done((bf16[16,7296]{1,0:T(8,128)(2,1)S(1)}, bf16[16,7296]{1,0:T(8,128)(2,1)}, u32[]{:S(2)}, u32[]{:S(2)}) %collective-permute-start.1) | collective-permute-done | bytes 233504 | tf_op jit(solution)/shard_map/ppermute | solution.py:26
  43.6 2.6 %collective-permute-start.3 = (bf16[64,7296]{1,0:T(8,128)(2,1)S(1)}, bf16[64,7296]{1,0:T(8,128)(2,1)S(1)}, u32[]{:S(2)}, u32[]{:S(2)}) collective-permute-start(bf16[64,7296]{1,0:T(8,128)(2,1)S(1)} %constant_dynamic-update-slice_fusion.refs_0_), channel_id=1, source_target_pairs={{0,12},{1,13},{2,14},{3,15},{4,0},{5,1},{6,2},{7,3},{8,4},{9,5},{1... | collective-permute-start | bytes 2801672 | tf_op jit(solution)/shard_map/ppermute | solution.py:26
  55.2 3.8 %shard_map.101 = (bf16[64,7168]{1,0:T(8,128)(2,1)S(1)}, bf16[64,7168]{1,0:T(8,128)(2,1)S(1)}) custom-call(bf16[64,7296]{1,0:T(8,128)(2,1)S(1)} %constant_dynamic-update-slice_fusion.refs_0_, bf16[64,7296]{1,0:T(8,128)(2,1)S(1)} %constant_dynamic-update-slice_fusion.4.refs_1_, bf16[7168,128]{1,0:T(8,128)(2,1)S(1)} %bitcast.7, bf16[7168,128]{1,0:T(8,128)(2,1)S(1)} %bitcast.12, ...), custom_call_target="tpu_custom_call" | custom-call | flops 1409286144 | bytes 14680064 | tf_op jit(solution)/shard_map/pallas_call | solution.py:39
  60.3 2.7 %collective-permute-start.8 = (bf16[64,3584]{1,0:T(8,128)(2,1)S(1)}, bf16[64,3584]{1,0:T(8,128)(2,1)S(1)}, u32[]{:S(2)}, u32[]{:S(2)}) collective-permute-start(bf16[64,3584]{1,0:T(8,128)(2,1)S(1)} %slice.64), channel_id=1, source_target_pairs={{0,12},{1,13},{2,14},{3,15},{4,0},{5,1},{6,2},{7,3},{8,4},{9,5},{1... | collective-permute-start | bytes 1376264 | tf_op jit(solution)/shard_map/ppermute | solution.py:26
  63.0 7.1 %collective-permute-done.18.refs_1_ = bf16[64,7296]{1,0:T(8,128)(2,1)S(1)} collective-permute-done((bf16[64,7296]{1,0:T(8,128)(2,1)S(1)}, bf16[64,7296]{1,0:T(8,128)(2,1)S(1)}, u32[]{:S(2)}, u32[]{:S(2)}) %collective-permute-start.18) | collective-permute-done | bytes 933920 | tf_op jit(solution)/shard_map/ppermute | solution.py:26
  70.5 2.7 %collective-permute-start.19 = (bf16[64,3584]{1,0:T(8,128)(2,1)S(1)}, bf16[64,3584]{1,0:T(8,128)(2,1)S(1)}, u32[]{:S(2)}, u32[]{:S(2)}) collective-permute-start(bf16[64,3584]{1,0:T(8,128)(2,1)S(1)} %slice.86), channel_id=1, source_target_pairs={{0,12},{1,13},{2,14},{3,15},{4,0},{5,1},{6,2},{7,3},{8,4},{9,5},{1... | collective-permute-start | bytes 1376264 | tf_op jit(solution)/shard_map/ppermute | solution.py:26
  73.2 3.8 %shard_map.102 = (bf16[64,7168]{1,0:T(8,128)(2,1)S(1)}, bf16[64,7168]{1,0:T(8,128)(2,1)S(1)}) custom-call(bf16[64,7296]{1,0:T(8,128)(2,1)S(1)} %collective-permute-done.3.refs_0_, bf16[64,7296]{1,0:T(8,128)(2,1)S(1)} %collective-permute-done.4.refs_1_, bf16[7168,128]{1,0:T(8,128)(2,1)S(1)} %bitcast.8, bf16[7168,128]{1,0:T(8,128)(2,1)S(1)} %bitcast.13, ...), custom_call_target="tpu_custom_call" | custom-call | flops 1409286144 | bytes 14680064 | tf_op jit(solution)/shard_map/pallas_call | solution.py:39
  77.1 3.8 %shard_map.103 = (bf16[64,3584]{1,0:T(8,128)(2,1)S(1)}, bf16[64,3584]{1,0:T(8,128)(2,1)S(1)}) custom-call(bf16[64,3584]{1,0:T(8,128)(2,1)S(1)} %collective-permute-done.8.refs_0_, bf16[64,3712]{1,0:T(8,128)(2,1)S(1)} %collective-permute-done.9.refs_1_, bf16[7168,128]{1,0:T(8,128)(2,1)S(1)} %bitcast.9, bf16[7168,128]{1,0:T(8,128)(2,1)S(1)} %bitcast.14, ...), custom_call_target="tpu_custom_call" | custom-call | flops 704643072 | bytes 12845056 | tf_op jit(solution)/shard_map/pallas_call | solution.py:39
  81.0 2.7 %collective-permute-start.12 = (bf16[64,3584]{1,0:T(8,128)(2,1)S(1)}, bf16[64,3584]{1,0:T(8,128)(2,1)S(1)}, u32[]{:S(2)}, u32[]{:S(2)}) collective-permute-start(bf16[64,3584]{1,0:T(8,128)(2,1)S(1)} %get-tuple-element.43), channel_id=1, source_target_pairs={{0,12},{1,13},{2,14},{3,15},{4,0},{5,1},{6,2},{7,3},{8,4},{9,5},{1... | collective-permute-start | bytes 1376264 | tf_op jit(solution)/shard_map/ppermute | solution.py:26
  83.6 3.8 %shard_map.104 = (bf16[64,3584]{1,0:T(8,128)(2,1)S(1)}, bf16[64,3584]{1,0:T(8,128)(2,1)S(1)}) custom-call(bf16[64,3584]{1,0:T(8,128)(2,1)S(1)} %collective-permute-done.19.refs_0_, bf16[64,3712]{1,0:T(8,128)(2,1)S(1)} %collective-permute-done.20.refs_1_, bf16[7168,128]{1,0:T(8,128)(2,1)S(1)} %bitcast.10, bf16[7168,128]{1,0:T(8,128)(2,1)S(1)} %bitcast.15, ...), custom_call_target="tpu_custom_call" | custom-call | flops 704643072 | bytes 12845056 | tf_op jit(solution)/shard_map/pallas_call | solution.py:39
  87.5 2.7 %collective-permute-start.23 = (bf16[64,3584]{1,0:T(8,128)(2,1)S(1)}, bf16[64,3584]{1,0:T(8,128)(2,1)S(1)}, u32[]{:S(2)}, u32[]{:S(2)}) collective-permute-start(bf16[64,3584]{1,0:T(8,128)(2,1)S(1)} %get-tuple-element.52), channel_id=1, source_target_pairs={{0,12},{1,13},{2,14},{3,15},{4,0},{5,1},{6,2},{7,3},{8,4},{9,5},{1... | collective-permute-start | bytes 1376264 | tf_op jit(solution)/shard_map/ppermute | solution.py:26
  90.1 3.8 %shard_map.105 = (bf16[64,7168]{1,0:T(8,128)(2,1)S(1)}, bf16[64,7168]{1,0:T(8,128)(2,1)S(1)}) custom-call(bf16[64,7296]{1,0:T(8,128)(2,1)S(1)} %collective-permute-done.17.refs_0_, bf16[64,7296]{1,0:T(8,128)(2,1)S(1)} %collective-permute-done.18.refs_1_, bf16[7168,128]{1,0:T(8,128)(2,1)S(1)} %bitcast.11, bf16[7168,128]{1,0:T(8,128)(2,1)S(1)} %bitcast.16, ...), custom_call_target="tpu_custom_call" | custom-call | flops 1409286144 | bytes 14680064 | tf_op jit(solution)/shard_map/pallas_call | solution.py:39
  94.5 2.7 %collective-permute-start.13 = (bf16[64,7168]{1,0:T(8,128)(2,1)S(1)}, bf16[64,7168]{1,0:T(8,128)(2,1)S(1)}, u32[]{:S(2)}, u32[]{:S(2)}) collective-permute-start(bf16[64,7168]{1,0:T(8,128)(2,1)S(1)} %fusion.1), channel_id=1, source_target_pairs={{0,12},{1,13},{2,14},{3,15},{4,0},{5,1},{6,2},{7,3},{8,4},{9,5},{1... | collective-permute-start | bytes 2752520 | tf_op jit(solution)/shard_map/ppermute | solution.py:26
  97.8 3.0 %collective-permute-start.24 = (bf16[64,7168]{1,0:T(8,128)(2,1)S(1)}, bf16[64,7168]{1,0:T(8,128)(2,1)S(1)}, u32[]{:S(2)}, u32[]{:S(2)}) collective-permute-start(bf16[64,7168]{1,0:T(8,128)(2,1)S(1)} %fusion.3), channel_id=1, source_target_pairs={{0,12},{1,13},{2,14},{3,15},{4,0},{5,1},{6,2},{7,3},{8,4},{9,5},{1... | collective-permute-start | bytes 2752520 | tf_op jit(solution)/shard_map/ppermute | solution.py:26
  100.8 7.2 %collective-permute-done.11 = bf16[64,7168]{1,0:T(8,128)(2,1)S(1)} collective-permute-done((bf16[64,7168]{1,0:T(8,128)(2,1)S(1)}, bf16[64,7168]{1,0:T(8,128)(2,1)S(1)}, u32[]{:S(2)}, u32[]{:S(2)}) %collective-permute-start.11) | collective-permute-done | bytes 917536 | tf_op jit(solution)/shard_map/ppermute | solution.py:26
  108.5 2.7 %collective-permute-start.15 = (bf16[16,7168]{1,0:T(8,128)(2,1)S(1)}, bf16[16,7168]{1,0:T(8,128)(2,1)S(1)}, u32[]{:S(2)}, u32[]{:S(2)}) collective-permute-start(bf16[16,7168]{1,0:T(8,128)(2,1)S(1)} %get-tuple-element.55), channel_id=1, source_target_pairs={{0,3},{1,0},{2,1},{3,2},{4,7},{5,4},{6,5},{7,6},{8,11},{9,8},{10,9... | collective-permute-start | bytes 688136 | tf_op jit(solution)/shard_map/ppermute | solution.py:26
  111.2 7.8 %collective-permute-done.22 = bf16[64,7168]{1,0:T(8,128)(2,1)S(1)} collective-permute-done((bf16[64,7168]{1,0:T(8,128)(2,1)S(1)}, bf16[64,7168]{1,0:T(8,128)(2,1)S(1)}, u32[]{:S(2)}, u32[]{:S(2)}) %collective-permute-start.22) | collective-permute-done | bytes 917536 | tf_op jit(solution)/shard_map/ppermute | solution.py:26
  119.4 2.7 %collective-permute-start.26 = (bf16[16,7168]{1,0:T(8,128)(2,1)S(1)}, bf16[16,7168]{1,0:T(8,128)(2,1)S(1)}, u32[]{:S(2)}, u32[]{:S(2)}) collective-permute-start(bf16[16,7168]{1,0:T(8,128)(2,1)S(1)} %get-tuple-element.58), channel_id=1, source_target_pairs={{0,3},{1,0},{2,1},{3,2},{4,7},{5,4},{6,5},{7,6},{8,11},{9,8},{10,9... | collective-permute-start | bytes 688136 | tf_op jit(solution)/shard_map/ppermute | solution.py:26
  122.3 8.5 %collective-permute-done.25 = bf16[16,7168]{1,0:T(8,128)(2,1)S(1)} collective-permute-done((bf16[16,7168]{1,0:T(8,128)(2,1)S(1)}, bf16[16,7168]{1,0:T(8,128)(2,1)S(1)}, u32[]{:S(2)}, u32[]{:S(2)}) %collective-permute-start.25) | collective-permute-done | bytes 229408 | tf_op jit(solution)/shard_map/ppermute | solution.py:26
  131.1 31.7 %all_to_all.11 = bf16[16,2,7168]{2,1,0:T(2,128)(2,1)S(1)} all-to-all(bf16[16,2,7168]{2,1,0:T(2,128)(2,1)S(1)} %reshape.17), channel_id=1, replica_groups=mesh['node'=16,'local'=16] {'node'}, dimensions={0} | all-to-all | bytes 917504 | tf_op jit(solution)/shard_map/all_to_all | solution.py:218
  (98 shorter events, 23.1 us)
Async XLA Ops:
  34.5 11.6 %collective-permute-start.5 = (bf16[16,7296]{1,0:T(8,128)(2,1)S(1)}, bf16[16,7296]{1,0:T(8,128)(2,1)S(1)}, u32[]{:S(2)}, u32[]{:S(2)}) collective-permute-start(bf16[16,7296]{1,0:T(8,128)(2,1)S(1)} %slice.63), channel_id=1, source_target_pairs={{0,3},{1,0},{2,1},{3,2},{4,7},{5,4},{6,5},{7,6},{8,11},{9,8},{10,9... | collective-permute-start | bytes 700424 | tf_op jit(solution)/shard_map/ppermute | solution.py:26
  35.6 10.7 %collective-permute-start.6 = (bf16[16,7296]{1,0:T(8,128)(2,1)S(1)}, bf16[16,7296]{1,0:T(8,128)(2,1)S(1)}, u32[]{:S(2)}, u32[]{:S(2)}) collective-permute-start(bf16[16,7296]{1,0:T(8,128)(2,1)S(1)} %slice.63), channel_id=1, source_target_pairs={{0,1},{1,2},{2,3},{3,0},{4,5},{5,6},{6,7},{7,4},{8,9},{9,10},{10,1... | collective-permute-start | bytes 700424 | tf_op jit(solution)/shard_map/ppermute | solution.py:26
  36.3 10.1 %collective-permute-start.7 = (bf16[16,7296]{1,0:T(8,128)(2,1)S(1)}, bf16[16,7296]{1,0:T(8,128)(2,1)S(1)}, u32[]{:S(2)}, u32[]{:S(2)}) collective-permute-start(bf16[16,7296]{1,0:T(8,128)(2,1)S(1)} %slice.63), channel_id=1, source_target_pairs={{0,2},{1,3},{2,0},{3,1},{4,6},{5,7},{6,4},{7,5},{8,10},{9,11},{10,... | collective-permute-start | bytes 700424 | tf_op jit(solution)/shard_map/ppermute | solution.py:26
  43.6 15.4 %collective-permute-start.3 = (bf16[64,7296]{1,0:T(8,128)(2,1)S(1)}, bf16[64,7296]{1,0:T(8,128)(2,1)S(1)}, u32[]{:S(2)}, u32[]{:S(2)}) collective-permute-start(bf16[64,7296]{1,0:T(8,128)(2,1)S(1)} %constant_dynamic-update-slice_fusion.refs_0_), channel_id=1, source_target_pairs={{0,12},{1,13},{2,14},{3,15},{4,0},{5,1},{6,2},{7,3},{8,4},{9,5},{1... | collective-permute-start | bytes 2801672 | tf_op jit(solution)/shard_map/ppermute | solution.py:26
  46.2 13.9 %collective-permute-start.4 = (bf16[64,7296]{1,0:T(8,128)(2,1)S(1)}, bf16[64,7296]{1,0:T(8,128)(2,1)S(1)}, u32[]{:S(2)}, u32[]{:S(2)}) collective-permute-start(bf16[64,7296]{1,0:T(8,128)(2,1)S(1)} %constant_dynamic-update-slice_fusion.refs_0_), channel_id=1, source_target_pairs={{0,4},{1,5},{2,6},{3,7},{4,8},{5,9},{6,10},{7,11},{8,12},{9,13},{1... | collective-permute-start | bytes 2801672 | tf_op jit(solution)/shard_map/ppermute | solution.py:26
  46.4 23.7 %collective-permute-start.18 = (bf16[64,7296]{1,0:T(8,128)(2,1)S(1)}, bf16[64,7296]{1,0:T(8,128)(2,1)S(1)}, u32[]{:S(2)}, u32[]{:S(2)}) collective-permute-start(bf16[64,7296]{1,0:T(8,128)(2,1)S(1)} %constant_dynamic-update-slice_fusion.4.refs_1_), channel_id=1, source_target_pairs={{0,4},{1,5},{2,6},{3,7},{4,8},{5,9},{6,10},{7,11},{8,12},{9,13},{1... | collective-permute-start | bytes 2801672 | tf_op jit(solution)/shard_map/ppermute | solution.py:26
  47.7 22.7 %collective-permute-start.17 = (bf16[64,7296]{1,0:T(8,128)(2,1)S(1)}, bf16[64,7296]{1,0:T(8,128)(2,1)S(1)}, u32[]{:S(2)}, u32[]{:S(2)}) collective-permute-start(bf16[64,7296]{1,0:T(8,128)(2,1)S(1)} %constant_dynamic-update-slice_fusion.4.refs_1_), channel_id=1, source_target_pairs={{0,12},{1,13},{2,14},{3,15},{4,0},{5,1},{6,2},{7,3},{8,4},{9,5},{1... | collective-permute-start | bytes 2801672 | tf_op jit(solution)/shard_map/ppermute | solution.py:26
  60.1 16.9 %collective-permute-start.9 = (bf16[64,3712]{1,0:T(8,128)(2,1)S(1)}, bf16[64,3712]{1,0:T(8,128)(2,1)S(1)}, u32[]{:S(2)}, u32[]{:S(2)}) collective-permute-start(bf16[64,3712]{1,0:T(8,128)(2,1)S(1)} %slice.65), channel_id=1, source_target_pairs={{0,4},{1,5},{2,6},{3,7},{4,8},{5,9},{6,10},{7,11},{8,12},{9,13},{1... | collective-permute-start | bytes 1425416 | tf_op jit(solution)/shard_map/ppermute | solution.py:26
  60.3 16.8 %collective-permute-start.8 = (bf16[64,3584]{1,0:T(8,128)(2,1)S(1)}, bf16[64,3584]{1,0:T(8,128)(2,1)S(1)}, u32[]{:S(2)}, u32[]{:S(2)}) collective-permute-start(bf16[64,3584]{1,0:T(8,128)(2,1)S(1)} %slice.64), channel_id=1, source_target_pairs={{0,12},{1,13},{2,14},{3,15},{4,0},{5,1},{6,2},{7,3},{8,4},{9,5},{1... | collective-permute-start | bytes 1376264 | tf_op jit(solution)/shard_map/ppermute | solution.py:26
  70.1 13.5 %collective-permute-start.20 = (bf16[64,3712]{1,0:T(8,128)(2,1)S(1)}, bf16[64,3712]{1,0:T(8,128)(2,1)S(1)}, u32[]{:S(2)}, u32[]{:S(2)}) collective-permute-start(bf16[64,3712]{1,0:T(8,128)(2,1)S(1)} %slice.87), channel_id=1, source_target_pairs={{0,4},{1,5},{2,6},{3,7},{4,8},{5,9},{6,10},{7,11},{8,12},{9,13},{1... | collective-permute-start | bytes 1425416 | tf_op jit(solution)/shard_map/ppermute | solution.py:26
  70.5 13.1 %collective-permute-start.19 = (bf16[64,3584]{1,0:T(8,128)(2,1)S(1)}, bf16[64,3584]{1,0:T(8,128)(2,1)S(1)}, u32[]{:S(2)}, u32[]{:S(2)}) collective-permute-start(bf16[64,3584]{1,0:T(8,128)(2,1)S(1)} %slice.86), channel_id=1, source_target_pairs={{0,12},{1,13},{2,14},{3,15},{4,0},{5,1},{6,2},{7,3},{8,4},{9,5},{1... | collective-permute-start | bytes 1376264 | tf_op jit(solution)/shard_map/ppermute | solution.py:26
  80.9 13.1 %collective-permute-start.10 = (bf16[64,3584]{1,0:T(8,128)(2,1)S(1)}, bf16[64,3584]{1,0:T(8,128)(2,1)S(1)}, u32[]{:S(2)}, u32[]{:S(2)}) collective-permute-start(bf16[64,3584]{1,0:T(8,128)(2,1)S(1)} %get-tuple-element.41), channel_id=1, source_target_pairs={{0,4},{1,5},{2,6},{3,7},{4,8},{5,9},{6,10},{7,11},{8,12},{9,13},{1... | collective-permute-start | bytes 1376264 | tf_op jit(solution)/shard_map/ppermute | solution.py:26
  81.0 13.4 %collective-permute-start.12 = (bf16[64,3584]{1,0:T(8,128)(2,1)S(1)}, bf16[64,3584]{1,0:T(8,128)(2,1)S(1)}, u32[]{:S(2)}, u32[]{:S(2)}) collective-permute-start(bf16[64,3584]{1,0:T(8,128)(2,1)S(1)} %get-tuple-element.43), channel_id=1, source_target_pairs={{0,12},{1,13},{2,14},{3,15},{4,0},{5,1},{6,2},{7,3},{8,4},{9,5},{1... | collective-permute-start | bytes 1376264 | tf_op jit(solution)/shard_map/ppermute | solution.py:26
  87.4 9.9 %collective-permute-start.21 = (bf16[64,3584]{1,0:T(8,128)(2,1)S(1)}, bf16[64,3584]{1,0:T(8,128)(2,1)S(1)}, u32[]{:S(2)}, u32[]{:S(2)}) collective-permute-start(bf16[64,3584]{1,0:T(8,128)(2,1)S(1)} %get-tuple-element.50), channel_id=1, source_target_pairs={{0,4},{1,5},{2,6},{3,7},{4,8},{5,9},{6,10},{7,11},{8,12},{9,13},{1... | collective-permute-start | bytes 1376264 | tf_op jit(solution)/shard_map/ppermute | solution.py:26
  87.5 10.1 %collective-permute-start.23 = (bf16[64,3584]{1,0:T(8,128)(2,1)S(1)}, bf16[64,3584]{1,0:T(8,128)(2,1)S(1)}, u32[]{:S(2)}, u32[]{:S(2)}) collective-permute-start(bf16[64,3584]{1,0:T(8,128)(2,1)S(1)} %get-tuple-element.52), channel_id=1, source_target_pairs={{0,12},{1,13},{2,14},{3,15},{4,0},{5,1},{6,2},{7,3},{8,4},{9,5},{1... | collective-permute-start | bytes 1376264 | tf_op jit(solution)/shard_map/ppermute | solution.py:26
  94.2 13.8 %collective-permute-start.11 = (bf16[64,7168]{1,0:T(8,128)(2,1)S(1)}, bf16[64,7168]{1,0:T(8,128)(2,1)S(1)}, u32[]{:S(2)}, u32[]{:S(2)}) collective-permute-start(bf16[64,7168]{1,0:T(8,128)(2,1)S(1)} %fusion), channel_id=1, source_target_pairs={{0,4},{1,5},{2,6},{3,7},{4,8},{5,9},{6,10},{7,11},{8,12},{9,13},{1... | collective-permute-start | bytes 2752520 | tf_op jit(solution)/shard_map/ppermute | solution.py:26
  94.5 13.5 %collective-permute-start.13 = (bf16[64,7168]{1,0:T(8,128)(2,1)S(1)}, bf16[64,7168]{1,0:T(8,128)(2,1)S(1)}, u32[]{:S(2)}, u32[]{:S(2)}) collective-permute-start(bf16[64,7168]{1,0:T(8,128)(2,1)S(1)} %fusion.1), channel_id=1, source_target_pairs={{0,12},{1,13},{2,14},{3,15},{4,0},{5,1},{6,2},{7,3},{8,4},{9,5},{1... | collective-permute-start | bytes 2752520 | tf_op jit(solution)/shard_map/ppermute | solution.py:26
  97.5 21.4 %collective-permute-start.22 = (bf16[64,7168]{1,0:T(8,128)(2,1)S(1)}, bf16[64,7168]{1,0:T(8,128)(2,1)S(1)}, u32[]{:S(2)}, u32[]{:S(2)}) collective-permute-start(bf16[64,7168]{1,0:T(8,128)(2,1)S(1)} %fusion.2), channel_id=1, source_target_pairs={{0,4},{1,5},{2,6},{3,7},{4,8},{5,9},{6,10},{7,11},{8,12},{9,13},{1... | collective-permute-start | bytes 2752520 | tf_op jit(solution)/shard_map/ppermute | solution.py:26
  97.8 21.1 %collective-permute-start.24 = (bf16[64,7168]{1,0:T(8,128)(2,1)S(1)}, bf16[64,7168]{1,0:T(8,128)(2,1)S(1)}, u32[]{:S(2)}, u32[]{:S(2)}) collective-permute-start(bf16[64,7168]{1,0:T(8,128)(2,1)S(1)} %fusion.3), channel_id=1, source_target_pairs={{0,12},{1,13},{2,14},{3,15},{4,0},{5,1},{6,2},{7,3},{8,4},{9,5},{1... | collective-permute-start | bytes 2752520 | tf_op jit(solution)/shard_map/ppermute | solution.py:26
  108.4 13.7 %collective-permute-start.14 = (bf16[16,7168]{1,0:T(8,128)(2,1)S(1)}, bf16[16,7168]{1,0:T(8,128)(2,1)S(1)}, u32[]{:S(2)}, u32[]{:S(2)}) collective-permute-start(bf16[16,7168]{1,0:T(8,128)(2,1)S(1)} %get-tuple-element.53), channel_id=1, source_target_pairs={{0,1},{1,2},{2,3},{3,0},{4,5},{5,6},{6,7},{7,4},{8,9},{9,10},{10,1... | collective-permute-start | bytes 688136 | tf_op jit(solution)/shard_map/ppermute | solution.py:26
  108.5 13.6 %collective-permute-start.15 = (bf16[16,7168]{1,0:T(8,128)(2,1)S(1)}, bf16[16,7168]{1,0:T(8,128)(2,1)S(1)}, u32[]{:S(2)}, u32[]{:S(2)}) collective-permute-start(bf16[16,7168]{1,0:T(8,128)(2,1)S(1)} %get-tuple-element.55), channel_id=1, source_target_pairs={{0,3},{1,0},{2,1},{3,2},{4,7},{5,4},{6,5},{7,6},{8,11},{9,8},{10,9... | collective-permute-start | bytes 688136 | tf_op jit(solution)/shard_map/ppermute | solution.py:26
  111.2 10.9 %collective-permute-start.16 = (bf16[16,7168]{1,0:T(8,128)(2,1)S(1)}, bf16[16,7168]{1,0:T(8,128)(2,1)S(1)}, u32[]{:S(2)}, u32[]{:S(2)}) collective-permute-start(bf16[16,7168]{1,0:T(8,128)(2,1)S(1)} %get-tuple-element.54), channel_id=1, source_target_pairs={{0,2},{1,3},{2,0},{3,1},{4,6},{5,7},{6,4},{7,5},{8,10},{9,11},{10,... | collective-permute-start | bytes 688136 | tf_op jit(solution)/shard_map/ppermute | solution.py:26
  119.4 11.4 %collective-permute-start.25 = (bf16[16,7168]{1,0:T(8,128)(2,1)S(1)}, bf16[16,7168]{1,0:T(8,128)(2,1)S(1)}, u32[]{:S(2)}, u32[]{:S(2)}) collective-permute-start(bf16[16,7168]{1,0:T(8,128)(2,1)S(1)} %get-tuple-element.56), channel_id=1, source_target_pairs={{0,1},{1,2},{2,3},{3,0},{4,5},{5,6},{6,7},{7,4},{8,9},{9,10},{10,1... | collective-permute-start | bytes 688136 | tf_op jit(solution)/shard_map/ppermute | solution.py:26
  119.4 11.3 %collective-permute-start.26 = (bf16[16,7168]{1,0:T(8,128)(2,1)S(1)}, bf16[16,7168]{1,0:T(8,128)(2,1)S(1)}, u32[]{:S(2)}, u32[]{:S(2)}) collective-permute-start(bf16[16,7168]{1,0:T(8,128)(2,1)S(1)} %get-tuple-element.58), channel_id=1, source_target_pairs={{0,3},{1,0},{2,1},{3,2},{4,7},{5,4},{6,5},{7,6},{8,11},{9,8},{10,9... | collective-permute-start | bytes 688136 | tf_op jit(solution)/shard_map/ppermute | solution.py:26
  (18 other events, 101.2 us)

commit v4 on v3

--- a/solution.py
+++ b/solution.py
@@ -196,10 +196,10 @@
     ahead, behind = [move(n, 1, -1) for n in near], [move(n, 1, 1) for n in near]
     out_own = mlp([[n] for n in near], weights)
     ahead[0], behind[0], out_own = hold((ahead[0], behind[0], out_own))
+    out_near = [mlp([[ahead[0]], [behind[0]]], weights)]
+    ahead[1], behind[1], out_near = hold((ahead[1], behind[1], out_near))
     left = [move(v[:, :half], 1, -1) for v in ahead]
     right = [move(v[:, half:], 1, 1) for v in behind]
-    out_near = [mlp([[ahead[0]], [behind[0]]], weights)]
-    left[0], right[0], out_near = hold((left[0], right[0], out_near))
     out_far = [mlp([[p, q]], weights)[0] for p, q in zip(left, right, strict=True)]
     ahead[1], behind[1], out_far[1] = hold((ahead[1], behind[1], out_far[1]))
     out_near.append(mlp([[ahead[1]], [behind[1]]], weights))

time: 164 us -> 162 us (0.988)
  transfers between devices with their start and end apart: 28 -> 28, of which waited for: 7 -> 11; matrix products, arithmetic and copies ran while one was open for 3% -> 3% of each run, Pallas kernels for 12% -> 12%
where the time goes in v4:
time: 162 us; the launch traced here: 161 us
  blocking collectives  56.9 us (35%)
  starting transfers between devices  35.7 us (22%)
  waiting for transfers between devices  33.1 us (20%)
  Pallas kernels  19.4 us (12%)
  local copies, waits for them, and re-layouts  13.2 us (8%)
  other arithmetic  1.84 us (1%)
    ppermute x28, starting transfers between devices, move(): return lax.ppermute(value, ('node', 'local'), pairs)  35.7 us
    ppermute x28, waiting for transfers between devices, move(): return lax.ppermute(value, ('node', 'local'), pairs)  33.1 us
    all_to_all x1, blocking collectives, per_device(): lax.all_to_all(summed.reshape(nodes, CAPACITY, features), 'node', split_a...  30.9 us
    all_to_all x1, blocking collectives, per_device(): lax.all_to_all(blocks.reshape(nodes, CAPACITY, -1), 'node', split_axis=0,...  25.9 us
    pallas_call x6, Pallas kernels, call(): pl.pallas_call(kernel, out_shape=outs, in_specs=[pl.BlockSpec(memory_spac...  19.4 us
    unnamed x34, local copies, waits for them, and re-layouts  10.9 us
  transfers between devices with their start and end apart: 28, of which 11 were waited for; matrix products, arithmetic and copies ran while one was open for 3% of the time, Pallas kernels for 12%

profile of v4, /device:TPU:1, one launch (start us, length us, event | category | flops | bytes accessed | tf_op | source)
XLA Modules:
  0.0 161.4 jit_solution(3406039965162124061)
XLA Ops:
  3.6 25.9 %all_to_all.10 = bf16[16,2,7296]{2,1,0:T(2,128)(2,1)S(1)} all-to-all(bf16[16,2,7296]{2,1,0:T(2,128)(2,1)S(1)} %reshape.16), channel_id=1, replica_groups=mesh['node'=16,'local'=16] {'node'}, dimensions={0} | all-to-all | bytes 933888 | tf_op jit(solution)/shard_map/all_to_all | solution.py:190
  29.9 2.8 %collective-permute-start = (bf16[16,7296]{1,0:T(8,128)(2,1)S(1)}, bf16[16,7296]{1,0:T(8,128)(2,1)}, u32[]{:S(2)}, u32[]{:S(2)}) collective-permute-start(bf16[16,7296]{1,0:T(8,128)(2,1)S(1)} %slice.61), channel_id=1, source_target_pairs={{0,3},{1,0},{2,1},{3,2},{4,7},{5,4},{6,5},{7,6},{8,11},{9,8},{10,9... | collective-permute-start | bytes 700424 | tf_op jit(solution)/shard_map/ppermute | solution.py:26
  39.0 2.7 %collective-permute-done.1 = bf16[16,7296]{1,0:T(8,128)(2,1)} collective-permute-done((bf16[16,7296]{1,0:T(8,128)(2,1)S(1)}, bf16[16,7296]{1,0:T(8,128)(2,1)}, u32[]{:S(2)}, u32[]{:S(2)}) %collective-permute-start.1) | collective-permute-done | bytes 233504 | tf_op jit(solution)/shard_map/ppermute | solution.py:26
  43.6 2.6 %collective-permute-start.3 = (bf16[64,7296]{1,0:T(8,128)(2,1)S(1)}, bf16[64,7296]{1,0:T(8,128)(2,1)S(1)}, u32[]{:S(2)}, u32[]{:S(2)}) collective-permute-start(bf16[64,7296]{1,0:T(8,128)(2,1)S(1)} %constant_dynamic-update-slice_fusion.refs_0_), channel_id=1, source_target_pairs={{0,12},{1,13},{2,14},{3,15},{4,0},{5,1},{6,2},{7,3},{8,4},{9,5},{1... | collective-permute-start | bytes 2801672 | tf_op jit(solution)/shard_map/ppermute | solution.py:26
  46.4 2.6 %collective-permute-start.8 = (bf16[64,7296]{1,0:T(8,128)(2,1)S(1)}, bf16[64,7296]{1,0:T(8,128)(2,1)S(1)}, u32[]{:S(2)}, u32[]{:S(2)}) collective-permute-start(bf16[64,7296]{1,0:T(8,128)(2,1)S(1)} %constant_dynamic-update-slice_fusion.4.refs_1_), channel_id=1, source_target_pairs={{0,12},{1,13},{2,14},{3,15},{4,0},{5,1},{6,2},{7,3},{8,4},{9,5},{1... | collective-permute-start | bytes 2801672 | tf_op jit(solution)/shard_map/ppermute | solution.py:26
  55.0 3.8 %shard_map.101 = (bf16[64,7168]{1,0:T(8,128)(2,1)S(1)}, bf16[64,7168]{1,0:T(8,128)(2,1)S(1)}) custom-call(bf16[64,7296]{1,0:T(8,128)(2,1)S(1)} %constant_dynamic-update-slice_fusion.refs_0_, bf16[64,7296]{1,0:T(8,128)(2,1)S(1)} %constant_dynamic-update-slice_fusion.4.refs_1_, bf16[7168,128]{1,0:T(8,128)(2,1)S(1)} %bitcast.7, bf16[7168,128]{1,0:T(8,128)(2,1)S(1)} %bitcast.12, ...), custom_call_target="tpu_custom_call" | custom-call | flops 1409286144 | bytes 14680064 | tf_op jit(solution)/shard_map/pallas_call | solution.py:39
  60.3 2.9 %collective-permute-start.10 = (bf16[64,3584]{1,0:T(8,128)(2,1)S(1)}, bf16[64,3584]{1,0:T(8,128)(2,1)S(1)}, u32[]{:S(2)}, u32[]{:S(2)}) collective-permute-start(bf16[64,3584]{1,0:T(8,128)(2,1)S(1)} %slice.65), channel_id=1, source_target_pairs={{0,12},{1,13},{2,14},{3,15},{4,0},{5,1},{6,2},{7,3},{8,4},{9,5},{1... | collective-permute-start | bytes 1376264 | tf_op jit(solution)/shard_map/ppermute | solution.py:26
  63.2 3.8 %shard_map.102 = (bf16[64,7168]{1,0:T(8,128)(2,1)S(1)}, bf16[64,7168]{1,0:T(8,128)(2,1)S(1)}) custom-call(bf16[64,7296]{1,0:T(8,128)(2,1)S(1)} %collective-permute-done.3.refs_0_, bf16[64,7296]{1,0:T(8,128)(2,1)S(1)} %collective-permute-done.4.refs_1_, bf16[7168,128]{1,0:T(8,128)(2,1)S(1)} %bitcast.8, bf16[7168,128]{1,0:T(8,128)(2,1)S(1)} %bitcast.13, ...), custom_call_target="tpu_custom_call" | custom-call | flops 1409286144 | bytes 14680064 | tf_op jit(solution)/shard_map/pallas_call | solution.py:39
  67.0 3.1 %collective-permute-done.9.refs_1_ = bf16[64,7296]{1,0:T(8,128)(2,1)S(1)} collective-permute-done((bf16[64,7296]{1,0:T(8,128)(2,1)S(1)}, bf16[64,7296]{1,0:T(8,128)(2,1)S(1)}, u32[]{:S(2)}, u32[]{:S(2)}) %collective-permute-start.9) | collective-permute-done | bytes 933920 | tf_op jit(solution)/shard_map/ppermute | solution.py:26
  70.3 2.7 %collective-permute-start.19 = (bf16[64,3584]{1,0:T(8,128)(2,1)S(1)}, bf16[64,3584]{1,0:T(8,128)(2,1)S(1)}, u32[]{:S(2)}, u32[]{:S(2)}) collective-permute-start(bf16[64,3584]{1,0:T(8,128)(2,1)S(1)} %slice.72), channel_id=1, source_target_pairs={{0,12},{1,13},{2,14},{3,15},{4,0},{5,1},{6,2},{7,3},{8,4},{9,5},{1... | collective-permute-start | bytes 1376264 | tf_op jit(solution)/shard_map/ppermute | solution.py:26
  75.2 3.7 %shard_map.103 = (bf16[64,3584]{1,0:T(8,128)(2,1)S(1)}, bf16[64,3584]{1,0:T(8,128)(2,1)S(1)}) custom-call(bf16[64,3584]{1,0:T(8,128)(2,1)S(1)} %collective-permute-done.10.refs_0_, bf16[64,3712]{1,0:T(8,128)(2,1)S(1)} %collective-permute-done.11.refs_1_, bf16[7168,128]{1,0:T(8,128)(2,1)S(1)} %bitcast.9, bf16[7168,128]{1,0:T(8,128)(2,1)S(1)} %bitcast.14, ...), custom_call_target="tpu_custom_call" | custom-call | flops 704643072 | bytes 12845056 | tf_op jit(solution)/shard_map/pallas_call | solution.py:39
  79.1 2.7 %collective-permute-start.14 = (bf16[64,3584]{1,0:T(8,128)(2,1)S(1)}, bf16[64,3584]{1,0:T(8,128)(2,1)S(1)}, u32[]{:S(2)}, u32[]{:S(2)}) collective-permute-start(bf16[64,3584]{1,0:T(8,128)(2,1)S(1)} %get-tuple-element.41), channel_id=1, source_target_pairs={{0,12},{1,13},{2,14},{3,15},{4,0},{5,1},{6,2},{7,3},{8,4},{9,5},{1... | collective-permute-start | bytes 1376264 | tf_op jit(solution)/shard_map/ppermute | solution.py:26
  81.7 3.8 %shard_map.104 = (bf16[64,3584]{1,0:T(8,128)(2,1)S(1)}, bf16[64,3584]{1,0:T(8,128)(2,1)S(1)}) custom-call(bf16[64,3584]{1,0:T(8,128)(2,1)S(1)} %collective-permute-done.19.refs_0_, bf16[64,3712]{1,0:T(8,128)(2,1)S(1)} %collective-permute-done.20.refs_1_, bf16[7168,128]{1,0:T(8,128)(2,1)S(1)} %bitcast.10, bf16[7168,128]{1,0:T(8,128)(2,1)S(1)} %bitcast.15, ...), custom_call_target="tpu_custom_call" | custom-call | flops 704643072 | bytes 12845056 | tf_op jit(solution)/shard_map/pallas_call | solution.py:39
  85.6 2.7 %collective-permute-start.23 = (bf16[64,3584]{1,0:T(8,128)(2,1)S(1)}, bf16[64,3584]{1,0:T(8,128)(2,1)S(1)}, u32[]{:S(2)}, u32[]{:S(2)}) collective-permute-start(bf16[64,3584]{1,0:T(8,128)(2,1)S(1)} %get-tuple-element.52), channel_id=1, source_target_pairs={{0,12},{1,13},{2,14},{3,15},{4,0},{5,1},{6,2},{7,3},{8,4},{9,5},{1... | collective-permute-start | bytes 1376264 | tf_op jit(solution)/shard_map/ppermute | solution.py:26
  88.2 3.8 %shard_map.105 = (bf16[64,7168]{1,0:T(8,128)(2,1)S(1)}, bf16[64,7168]{1,0:T(8,128)(2,1)S(1)}) custom-call(bf16[64,7296]{1,0:T(8,128)(2,1)S(1)} %collective-permute-done.8.refs_0_, bf16[64,7296]{1,0:T(8,128)(2,1)S(1)} %collective-permute-done.9.refs_1_, bf16[7168,128]{1,0:T(8,128)(2,1)S(1)} %bitcast.11, bf16[7168,128]{1,0:T(8,128)(2,1)S(1)} %bitcast.16, ...), custom_call_target="tpu_custom_call" | custom-call | flops 1409286144 | bytes 14680064 | tf_op jit(solution)/shard_map/pallas_call | solution.py:39
  92.6 2.7 %collective-permute-start.15 = (bf16[64,7168]{1,0:T(8,128)(2,1)S(1)}, bf16[64,7168]{1,0:T(8,128)(2,1)S(1)}, u32[]{:S(2)}, u32[]{:S(2)}) collective-permute-start(bf16[64,7168]{1,0:T(8,128)(2,1)S(1)} %fusion.1), channel_id=1, source_target_pairs={{0,12},{1,13},{2,14},{3,15},{4,0},{5,1},{6,2},{7,3},{8,4},{9,5},{1... | collective-permute-start | bytes 2752520 | tf_op jit(solution)/shard_map/ppermute | solution.py:26
  96.2 2.7 %collective-permute-start.24 = (bf16[64,7168]{1,0:T(8,128)(2,1)S(1)}, bf16[64,7168]{1,0:T(8,128)(2,1)S(1)}, u32[]{:S(2)}, u32[]{:S(2)}) collective-permute-start(bf16[64,7168]{1,0:T(8,128)(2,1)S(1)} %fusion.3), channel_id=1, source_target_pairs={{0,12},{1,13},{2,14},{3,15},{4,0},{5,1},{6,2},{7,3},{8,4},{9,5},{1... | collective-permute-start | bytes 2752520 | tf_op jit(solution)/shard_map/ppermute | solution.py:26
  98.9 7.2 %collective-permute-done.13 = bf16[64,7168]{1,0:T(8,128)(2,1)S(1)} collective-permute-done((bf16[64,7168]{1,0:T(8,128)(2,1)S(1)}, bf16[64,7168]{1,0:T(8,128)(2,1)S(1)}, u32[]{:S(2)}, u32[]{:S(2)}) %collective-permute-start.13) | collective-permute-done | bytes 917536 | tf_op jit(solution)/shard_map/ppermute | solution.py:26
  106.6 2.7 %collective-permute-start.17 = (bf16[16,7168]{1,0:T(8,128)(2,1)S(1)}, bf16[16,7168]{1,0:T(8,128)(2,1)S(1)}, u32[]{:S(2)}, u32[]{:S(2)}) collective-permute-start(bf16[16,7168]{1,0:T(8,128)(2,1)S(1)} %get-tuple-element.55), channel_id=1, source_target_pairs={{0,3},{1,0},{2,1},{3,2},{4,7},{5,4},{6,5},{7,6},{8,11},{9,8},{10,9... | collective-permute-start | bytes 688136 | tf_op jit(solution)/shard_map/ppermute | solution.py:26
  109.3 8.3 %collective-permute-done.22 = bf16[64,7168]{1,0:T(8,128)(2,1)S(1)} collective-permute-done((bf16[64,7168]{1,0:T(8,128)(2,1)S(1)}, bf16[64,7168]{1,0:T(8,128)(2,1)S(1)}, u32[]{:S(2)}, u32[]{:S(2)}) %collective-permute-start.22) | collective-permute-done | bytes 917536 | tf_op jit(solution)/shard_map/ppermute | solution.py:26
  120.0 2.7 %collective-permute-start.26 = (bf16[16,7168]{1,0:T(8,128)(2,1)S(1)}, bf16[16,7168]{1,0:T(8,128)(2,1)S(1)}, u32[]{:S(2)}, u32[]{:S(2)}) collective-permute-start(bf16[16,7168]{1,0:T(8,128)(2,1)S(1)} %get-tuple-element.58), channel_id=1, source_target_pairs={{0,3},{1,0},{2,1},{3,2},{4,7},{5,4},{6,5},{7,6},{8,11},{9,8},{10,9... | collective-permute-start | bytes 688136 | tf_op jit(solution)/shard_map/ppermute | solution.py:26
  122.8 3.3 %collective-permute-done.25 = bf16[16,7168]{1,0:T(8,128)(2,1)S(1)} collective-permute-done((bf16[16,7168]{1,0:T(8,128)(2,1)S(1)}, bf16[16,7168]{1,0:T(8,128)(2,1)S(1)}, u32[]{:S(2)}, u32[]{:S(2)}) %collective-permute-start.25) | collective-permute-done | bytes 229408 | tf_op jit(solution)/shard_map/ppermute | solution.py:26
  126.1 2.4 %collective-permute-done.26 = bf16[16,7168]{1,0:T(8,128)(2,1)S(1)} collective-permute-done((bf16[16,7168]{1,0:T(8,128)(2,1)S(1)}, bf16[16,7168]{1,0:T(8,128)(2,1)S(1)}, u32[]{:S(2)}, u32[]{:S(2)}) %collective-permute-start.26) | collective-permute-done | bytes 229408 | tf_op jit(solution)/shard_map/ppermute | solution.py:26
  129.4 30.9 %all_to_all.11 = bf16[16,2,7168]{2,1,0:T(2,128)(2,1)S(1)} all-to-all(bf16[16,2,7168]{2,1,0:T(2,128)(2,1)S(1)} %reshape.17), channel_id=1, replica_groups=mesh['node'=16,'local'=16] {'node'}, dimensions={0} | all-to-all | bytes 917504 | tf_op jit(solution)/shard_map/all_to_all | solution.py:218
  (98 shorter events, 28.5 us)
Async XLA Ops:
  32.7 8.9 %collective-permute-start.1 = (bf16[16,7296]{1,0:T(8,128)(2,1)S(1)}, bf16[16,7296]{1,0:T(8,128)(2,1)}, u32[]{:S(2)}, u32[]{:S(2)}) collective-permute-start(bf16[16,7296]{1,0:T(8,128)(2,1)S(1)} %slice.61), channel_id=1, source_target_pairs={{0,1},{1,2},{2,3},{3,0},{4,5},{5,6},{6,7},{7,4},{8,9},{9,10},{10,1... | collective-permute-start | bytes 700424 | tf_op jit(solution)/shard_map/ppermute | solution.py:26
  32.8 9.9 %collective-permute-start.2 = (bf16[16,7296]{1,0:T(8,128)(2,1)S(1)}, bf16[16,7296]{1,0:T(8,128)(2,1)}, u32[]{:S(2)}, u32[]{:S(2)}) collective-permute-start(bf16[16,7296]{1,0:T(8,128)(2,1)S(1)} %slice.61), channel_id=1, source_target_pairs={{0,2},{1,3},{2,0},{3,1},{4,6},{5,7},{6,4},{7,5},{8,10},{9,11},{10,... | collective-permute-start | bytes 700424 | tf_op jit(solution)/shard_map/ppermute | solution.py:26
  34.5 11.6 %collective-permute-start.5 = (bf16[16,7296]{1,0:T(8,128)(2,1)S(1)}, bf16[16,7296]{1,0:T(8,128)(2,1)S(1)}, u32[]{:S(2)}, u32[]{:S(2)}) collective-permute-start(bf16[16,7296]{1,0:T(8,128)(2,1)S(1)} %slice.63), channel_id=1, source_target_pairs={{0,3},{1,0},{2,1},{3,2},{4,7},{5,4},{6,5},{7,6},{8,11},{9,8},{10,9... | collective-permute-start | bytes 700424 | tf_op jit(solution)/shard_map/ppermute | solution.py:26
  35.6 10.7 %collective-permute-start.6 = (bf16[16,7296]{1,0:T(8,128)(2,1)S(1)}, bf16[16,7296]{1,0:T(8,128)(2,1)S(1)}, u32[]{:S(2)}, u32[]{:S(2)}) collective-permute-start(bf16[16,7296]{1,0:T(8,128)(2,1)S(1)} %slice.63), channel_id=1, source_target_pairs={{0,1},{1,2},{2,3},{3,0},{4,5},{5,6},{6,7},{7,4},{8,9},{9,10},{10,1... | collective-permute-start | bytes 700424 | tf_op jit(solution)/shard_map/ppermute | solution.py:26
  36.3 10.1 %collective-permute-start.7 = (bf16[16,7296]{1,0:T(8,128)(2,1)S(1)}, bf16[16,7296]{1,0:T(8,128)(2,1)S(1)}, u32[]{:S(2)}, u32[]{:S(2)}) collective-permute-start(bf16[16,7296]{1,0:T(8,128)(2,1)S(1)} %slice.63), channel_id=1, source_target_pairs={{0,2},{1,3},{2,0},{3,1},{4,6},{5,7},{6,4},{7,5},{8,10},{9,11},{10,... | collective-permute-start | bytes 700424 | tf_op jit(solution)/shard_map/ppermute | solution.py:26
  43.6 15.3 %collective-permute-start.3 = (bf16[64,7296]{1,0:T(8,128)(2,1)S(1)}, bf16[64,7296]{1,0:T(8,128)(2,1)S(1)}, u32[]{:S(2)}, u32[]{:S(2)}) collective-permute-start(bf16[64,7296]{1,0:T(8,128)(2,1)S(1)} %constant_dynamic-update-slice_fusion.refs_0_), channel_id=1, source_target_pairs={{0,12},{1,13},{2,14},{3,15},{4,0},{5,1},{6,2},{7,3},{8,4},{9,5},{1... | collective-permute-start | bytes 2801672 | tf_op jit(solution)/shard_map/ppermute | solution.py:26
  46.2 13.9 %collective-permute-start.4 = (bf16[64,7296]{1,0:T(8,128)(2,1)S(1)}, bf16[64,7296]{1,0:T(8,128)(2,1)S(1)}, u32[]{:S(2)}, u32[]{:S(2)}) collective-permute-start(bf16[64,7296]{1,0:T(8,128)(2,1)S(1)} %constant_dynamic-update-slice_fusion.refs_0_), channel_id=1, source_target_pairs={{0,4},{1,5},{2,6},{3,7},{4,8},{5,9},{6,10},{7,11},{8,12},{9,13},{1... | collective-permute-start | bytes 2801672 | tf_op jit(solution)/shard_map/ppermute | solution.py:26
  46.4 20.6 %collective-permute-start.8 = (bf16[64,7296]{1,0:T(8,128)(2,1)S(1)}, bf16[64,7296]{1,0:T(8,128)(2,1)S(1)}, u32[]{:S(2)}, u32[]{:S(2)}) collective-permute-start(bf16[64,7296]{1,0:T(8,128)(2,1)S(1)} %constant_dynamic-update-slice_fusion.4.refs_1_), channel_id=1, source_target_pairs={{0,12},{1,13},{2,14},{3,15},{4,0},{5,1},{6,2},{7,3},{8,4},{9,5},{1... | collective-permute-start | bytes 2801672 | tf_op jit(solution)/shard_map/ppermute | solution.py:26
  49.0 21.1 %collective-permute-start.9 = (bf16[64,7296]{1,0:T(8,128)(2,1)S(1)}, bf16[64,7296]{1,0:T(8,128)(2,1)S(1)}, u32[]{:S(2)}, u32[]{:S(2)}) collective-permute-start(bf16[64,7296]{1,0:T(8,128)(2,1)S(1)} %constant_dynamic-update-slice_fusion.4.refs_1_), channel_id=1, source_target_pairs={{0,4},{1,5},{2,6},{3,7},{4,8},{5,9},{6,10},{7,11},{8,12},{9,13},{1... | collective-permute-start | bytes 2801672 | tf_op jit(solution)/shard_map/ppermute | solution.py:26
  60.1 15.1 %collective-permute-start.11 = (bf16[64,3712]{1,0:T(8,128)(2,1)S(1)}, bf16[64,3712]{1,0:T(8,128)(2,1)S(1)}, u32[]{:S(2)}, u32[]{:S(2)}) collective-permute-start(bf16[64,3712]{1,0:T(8,128)(2,1)S(1)} %slice.66), channel_id=1, source_target_pairs={{0,4},{1,5},{2,6},{3,7},{4,8},{5,9},{6,10},{7,11},{8,12},{9,13},{1... | collective-permute-start | bytes 1425416 | tf_op jit(solution)/shard_map/ppermute | solution.py:26
  60.3 12.8 %collective-permute-start.10 = (bf16[64,3584]{1,0:T(8,128)(2,1)S(1)}, bf16[64,3584]{1,0:T(8,128)(2,1)S(1)}, u32[]{:S(2)}, u32[]{:S(2)}) collective-permute-start(bf16[64,3584]{1,0:T(8,128)(2,1)S(1)} %slice.65), channel_id=1, source_target_pairs={{0,12},{1,13},{2,14},{3,15},{4,0},{5,1},{6,2},{7,3},{8,4},{9,5},{1... | collective-permute-start | bytes 1376264 | tf_op jit(solution)/shard_map/ppermute | solution.py:26
  70.1 11.6 %collective-permute-start.20 = (bf16[64,3712]{1,0:T(8,128)(2,1)S(1)}, bf16[64,3712]{1,0:T(8,128)(2,1)S(1)}, u32[]{:S(2)}, u32[]{:S(2)}) collective-permute-start(bf16[64,3712]{1,0:T(8,128)(2,1)S(1)} %slice.73), channel_id=1, source_target_pairs={{0,4},{1,5},{2,6},{3,7},{4,8},{5,9},{6,10},{7,11},{8,12},{9,13},{1... | collective-permute-start | bytes 1425416 | tf_op jit(solution)/shard_map/ppermute | solution.py:26
  70.3 11.4 %collective-permute-start.19 = (bf16[64,3584]{1,0:T(8,128)(2,1)S(1)}, bf16[64,3584]{1,0:T(8,128)(2,1)S(1)}, u32[]{:S(2)}, u32[]{:S(2)}) collective-permute-start(bf16[64,3584]{1,0:T(8,128)(2,1)S(1)} %slice.72), channel_id=1, source_target_pairs={{0,12},{1,13},{2,14},{3,15},{4,0},{5,1},{6,2},{7,3},{8,4},{9,5},{1... | collective-permute-start | bytes 1376264 | tf_op jit(solution)/shard_map/ppermute | solution.py:26
  78.9 13.1 %collective-permute-start.12 = (bf16[64,3584]{1,0:T(8,128)(2,1)S(1)}, bf16[64,3584]{1,0:T(8,128)(2,1)S(1)}, u32[]{:S(2)}, u32[]{:S(2)}) collective-permute-start(bf16[64,3584]{1,0:T(8,128)(2,1)S(1)} %get-tuple-element.39), channel_id=1, source_target_pairs={{0,4},{1,5},{2,6},{3,7},{4,8},{5,9},{6,10},{7,11},{8,12},{9,13},{1... | collective-permute-start | bytes 1376264 | tf_op jit(solution)/shard_map/ppermute | solution.py:26
  79.1 13.4 %collective-permute-start.14 = (bf16[64,3584]{1,0:T(8,128)(2,1)S(1)}, bf16[64,3584]{1,0:T(8,128)(2,1)S(1)}, u32[]{:S(2)}, u32[]{:S(2)}) collective-permute-start(bf16[64,3584]{1,0:T(8,128)(2,1)S(1)} %get-tuple-element.41), channel_id=1, source_target_pairs={{0,12},{1,13},{2,14},{3,15},{4,0},{5,1},{6,2},{7,3},{8,4},{9,5},{1... | collective-permute-start | bytes 1376264 | tf_op jit(solution)/shard_map/ppermute | solution.py:26
  85.5 9.9 %collective-permute-start.21 = (bf16[64,3584]{1,0:T(8,128)(2,1)S(1)}, bf16[64,3584]{1,0:T(8,128)(2,1)S(1)}, u32[]{:S(2)}, u32[]{:S(2)}) collective-permute-start(bf16[64,3584]{1,0:T(8,128)(2,1)S(1)} %get-tuple-element.50), channel_id=1, source_target_pairs={{0,4},{1,5},{2,6},{3,7},{4,8},{5,9},{6,10},{7,11},{8,12},{9,13},{1... | collective-permute-start | bytes 1376264 | tf_op jit(solution)/shard_map/ppermute | solution.py:26
  85.6 10.4 %collective-permute-start.23 = (bf16[64,3584]{1,0:T(8,128)(2,1)S(1)}, bf16[64,3584]{1,0:T(8,128)(2,1)S(1)}, u32[]{:S(2)}, u32[]{:S(2)}) collective-permute-start(bf16[64,3584]{1,0:T(8,128)(2,1)S(1)} %get-tuple-element.52), channel_id=1, source_target_pairs={{0,12},{1,13},{2,14},{3,15},{4,0},{5,1},{6,2},{7,3},{8,4},{9,5},{1... | collective-permute-start | bytes 1376264 | tf_op jit(solution)/shard_map/ppermute | solution.py:26
  92.3 13.8 %collective-permute-start.13 = (bf16[64,7168]{1,0:T(8,128)(2,1)S(1)}, bf16[64,7168]{1,0:T(8,128)(2,1)S(1)}, u32[]{:S(2)}, u32[]{:S(2)}) collective-permute-start(bf16[64,7168]{1,0:T(8,128)(2,1)S(1)} %fusion), channel_id=1, source_target_pairs={{0,4},{1,5},{2,6},{3,7},{4,8},{5,9},{6,10},{7,11},{8,12},{9,13},{1... | collective-permute-start | bytes 2752520 | tf_op jit(solution)/shard_map/ppermute | solution.py:26
  92.6 13.5 %collective-permute-start.15 = (bf16[64,7168]{1,0:T(8,128)(2,1)S(1)}, bf16[64,7168]{1,0:T(8,128)(2,1)S(1)}, u32[]{:S(2)}, u32[]{:S(2)}) collective-permute-start(bf16[64,7168]{1,0:T(8,128)(2,1)S(1)} %fusion.1), channel_id=1, source_target_pairs={{0,12},{1,13},{2,14},{3,15},{4,0},{5,1},{6,2},{7,3},{8,4},{9,5},{1... | collective-permute-start | bytes 2752520 | tf_op jit(solution)/shard_map/ppermute | solution.py:26
  95.6 22.0 %collective-permute-start.22 = (bf16[64,7168]{1,0:T(8,128)(2,1)S(1)}, bf16[64,7168]{1,0:T(8,128)(2,1)S(1)}, u32[]{:S(2)}, u32[]{:S(2)}) collective-permute-start(bf16[64,7168]{1,0:T(8,128)(2,1)S(1)} %fusion.2), channel_id=1, source_target_pairs={{0,4},{1,5},{2,6},{3,7},{4,8},{5,9},{6,10},{7,11},{8,12},{9,13},{1... | collective-permute-start | bytes 2752520 | tf_op jit(solution)/shard_map/ppermute | solution.py:26
  96.2 23.4 %collective-permute-start.24 = (bf16[64,7168]{1,0:T(8,128)(2,1)S(1)}, bf16[64,7168]{1,0:T(8,128)(2,1)S(1)}, u32[]{:S(2)}, u32[]{:S(2)}) collective-permute-start(bf16[64,7168]{1,0:T(8,128)(2,1)S(1)} %fusion.3), channel_id=1, source_target_pairs={{0,12},{1,13},{2,14},{3,15},{4,0},{5,1},{6,2},{7,3},{8,4},{9,5},{1... | collective-permute-start | bytes 2752520 | tf_op jit(solution)/shard_map/ppermute | solution.py:26
  106.5 16.2 %collective-permute-start.16 = (bf16[16,7168]{1,0:T(8,128)(2,1)S(1)}, bf16[16,7168]{1,0:T(8,128)(2,1)S(1)}, u32[]{:S(2)}, u32[]{:S(2)}) collective-permute-start(bf16[16,7168]{1,0:T(8,128)(2,1)S(1)} %get-tuple-element.53), channel_id=1, source_target_pairs={{0,1},{1,2},{2,3},{3,0},{4,5},{5,6},{6,7},{7,4},{8,9},{9,10},{10,1... | collective-permute-start | bytes 688136 | tf_op jit(solution)/shard_map/ppermute | solution.py:26
  106.6 16.1 %collective-permute-start.17 = (bf16[16,7168]{1,0:T(8,128)(2,1)S(1)}, bf16[16,7168]{1,0:T(8,128)(2,1)S(1)}, u32[]{:S(2)}, u32[]{:S(2)}) collective-permute-start(bf16[16,7168]{1,0:T(8,128)(2,1)S(1)} %get-tuple-element.55), channel_id=1, source_target_pairs={{0,3},{1,0},{2,1},{3,2},{4,7},{5,4},{6,5},{7,6},{8,11},{9,8},{10,9... | collective-permute-start | bytes 688136 | tf_op jit(solution)/shard_map/ppermute | solution.py:26
  109.3 13.4 %collective-permute-start.18 = (bf16[16,7168]{1,0:T(8,128)(2,1)S(1)}, bf16[16,7168]{1,0:T(8,128)(2,1)S(1)}, u32[]{:S(2)}, u32[]{:S(2)}) collective-permute-start(bf16[16,7168]{1,0:T(8,128)(2,1)S(1)} %get-tuple-element.54), channel_id=1, source_target_pairs={{0,2},{1,3},{2,0},{3,1},{4,6},{5,7},{6,4},{7,5},{8,10},{9,11},{10,... | collective-permute-start | bytes 688136 | tf_op jit(solution)/shard_map/ppermute | solution.py:26
  (18 other events, 106.3 us)

commit v5 on v4

--- a/solution.py
+++ b/solution.py
@@ -139,7 +139,7 @@
 
     for start in range(0, features, shortest):
 
-        @pl.loop(0, shortest // step)
+        @pl.loop(0, shortest // step, unroll=True)
         def _(c):
             at = pl.multiple_of(c * step, step)
             columns = pl.ds(start + at, step)

time: 162 us -> 157 us (0.969)
  Pallas kernels: 19.4 us -> 9.9 us
  waiting for transfers between devices: 33.1 us -> 38.1 us
    pallas_call x6, Pallas kernels: 19.4 us -> 9.9 us  [call(): pl.pallas_call(kernel, out_shape=outs, in_specs=[pl.BlockSpec(memory_spac...]
    ppermute x28, waiting for transfers between devices: 33.1 us -> 38.1 us  [move(): return lax.ppermute(value, ('node', 'local'), pairs)]
  transfers between devices with their start and end apart: 28 -> 28, of which waited for: 11 -> 14; matrix products, arithmetic and copies ran while one was open for 3% -> 3% of each run, Pallas kernels for 12% -> 6%
where the time goes in v5:
time: 157 us; the launch traced here: 156 us
  blocking collectives  56.2 us (36%)
  waiting for transfers between devices  38.1 us (24%)
  starting transfers between devices  35.7 us (23%)
  local copies, waits for them, and re-layouts  13.2 us (8%)
  Pallas kernels  9.9 us (6%)
  other arithmetic  1.84 us (1%)
    ppermute x28, waiting for transfers between devices, move(): return lax.ppermute(value, ('node', 'local'), pairs)  38.1 us
    ppermute x28, starting transfers between devices, move(): return lax.ppermute(value, ('node', 'local'), pairs)  35.7 us
    all_to_all x1, blocking collectives, per_device(): lax.all_to_all(summed.reshape(nodes, CAPACITY, features), 'node', split_a...  30.2 us
    all_to_all x1, blocking collectives, per_device(): lax.all_to_all(blocks.reshape(nodes, CAPACITY, -1), 'node', split_axis=0,...  25.9 us
    unnamed x34, local copies, waits for them, and re-layouts  10.9 us
    pallas_call x6, Pallas kernels, call(): pl.pallas_call(kernel, out_shape=outs, in_specs=[pl.BlockSpec(memory_spac...  9.9 us
  transfers between devices with their start and end apart: 28, of which 14 were waited for; matrix products, arithmetic and copies ran while one was open for 3% of the time, Pallas kernels for 6%

profile of v5, /device:TPU:1, one launch (start us, length us, event | category | flops | bytes accessed | tf_op | source)
XLA Modules:
  0.0 156.1 jit_solution(1512591987554598267)
XLA Ops:
  3.6 25.9 %all_to_all.10 = bf16[16,2,7296]{2,1,0:T(2,128)(2,1)S(1)} all-to-all(bf16[16,2,7296]{2,1,0:T(2,128)(2,1)S(1)} %reshape.16), channel_id=1, replica_groups=mesh['node'=16,'local'=16] {'node'}, dimensions={0} | all-to-all | bytes 933888 | tf_op jit(solution)/shard_map/all_to_all | solution.py:190
  29.9 2.8 %collective-permute-start = (bf16[16,7296]{1,0:T(8,128)(2,1)S(1)}, bf16[16,7296]{1,0:T(8,128)(2,1)}, u32[]{:S(2)}, u32[]{:S(2)}) collective-permute-start(bf16[16,7296]{1,0:T(8,128)(2,1)S(1)} %slice.61), channel_id=1, source_target_pairs={{0,3},{1,0},{2,1},{3,2},{4,7},{5,4},{6,5},{7,6},{8,11},{9,8},{10,9... | collective-permute-start | bytes 700424 | tf_op jit(solution)/shard_map/ppermute | solution.py:26
  39.0 2.7 %collective-permute-done.1 = bf16[16,7296]{1,0:T(8,128)(2,1)} collective-permute-done((bf16[16,7296]{1,0:T(8,128)(2,1)S(1)}, bf16[16,7296]{1,0:T(8,128)(2,1)}, u32[]{:S(2)}, u32[]{:S(2)}) %collective-permute-start.1) | collective-permute-done | bytes 233504 | tf_op jit(solution)/shard_map/ppermute | solution.py:26
  43.6 2.6 %collective-permute-start.3 = (bf16[64,7296]{1,0:T(8,128)(2,1)S(1)}, bf16[64,7296]{1,0:T(8,128)(2,1)S(1)}, u32[]{:S(2)}, u32[]{:S(2)}) collective-permute-start(bf16[64,7296]{1,0:T(8,128)(2,1)S(1)} %constant_dynamic-update-slice_fusion.refs_0_), channel_id=1, source_target_pairs={{0,12},{1,13},{2,14},{3,15},{4,0},{5,1},{6,2},{7,3},{8,4},{9,5},{1... | collective-permute-start | bytes 2801672 | tf_op jit(solution)/shard_map/ppermute | solution.py:26
  46.4 2.6 %collective-permute-start.8 = (bf16[64,7296]{1,0:T(8,128)(2,1)S(1)}, bf16[64,7296]{1,0:T(8,128)(2,1)S(1)}, u32[]{:S(2)}, u32[]{:S(2)}) collective-permute-start(bf16[64,7296]{1,0:T(8,128)(2,1)S(1)} %constant_dynamic-update-slice_fusion.4.refs_1_), channel_id=1, source_target_pairs={{0,12},{1,13},{2,14},{3,15},{4,0},{5,1},{6,2},{7,3},{8,4},{9,5},{1... | collective-permute-start | bytes 2801672 | tf_op jit(solution)/shard_map/ppermute | solution.py:26
  56.8 3.3 %collective-permute-done.4.refs_1_ = bf16[64,7296]{1,0:T(8,128)(2,1)S(1)} collective-permute-done((bf16[64,7296]{1,0:T(8,128)(2,1)S(1)}, bf16[64,7296]{1,0:T(8,128)(2,1)S(1)}, u32[]{:S(2)}, u32[]{:S(2)}) %collective-permute-start.4) | collective-permute-done | bytes 933920 | tf_op jit(solution)/shard_map/ppermute | solution.py:26
  60.3 2.9 %collective-permute-start.10 = (bf16[64,3584]{1,0:T(8,128)(2,1)S(1)}, bf16[64,3584]{1,0:T(8,128)(2,1)S(1)}, u32[]{:S(2)}, u32[]{:S(2)}) collective-permute-start(bf16[64,3584]{1,0:T(8,128)(2,1)S(1)} %slice.65), channel_id=1, source_target_pairs={{0,12},{1,13},{2,14},{3,15},{4,0},{5,1},{6,2},{7,3},{8,4},{9,5},{1... | collective-permute-start | bytes 1376264 | tf_op jit(solution)/shard_map/ppermute | solution.py:26
  64.9 1.7 %collective-permute-done.8.refs_0_ = bf16[64,7296]{1,0:T(8,128)(2,1)S(1)} collective-permute-done((bf16[64,7296]{1,0:T(8,128)(2,1)S(1)}, bf16[64,7296]{1,0:T(8,128)(2,1)S(1)}, u32[]{:S(2)}, u32[]{:S(2)}) %collective-permute-start.8) | collective-permute-done | bytes 933920 | tf_op jit(solution)/shard_map/ppermute | solution.py:26
  66.7 3.4 %collective-permute-done.9.refs_1_ = bf16[64,7296]{1,0:T(8,128)(2,1)S(1)} collective-permute-done((bf16[64,7296]{1,0:T(8,128)(2,1)S(1)}, bf16[64,7296]{1,0:T(8,128)(2,1)S(1)}, u32[]{:S(2)}, u32[]{:S(2)}) %collective-permute-start.9) | collective-permute-done | bytes 933920 | tf_op jit(solution)/shard_map/ppermute | solution.py:26
  70.3 2.7 %collective-permute-start.19 = (bf16[64,3584]{1,0:T(8,128)(2,1)S(1)}, bf16[64,3584]{1,0:T(8,128)(2,1)S(1)}, u32[]{:S(2)}, u32[]{:S(2)}) collective-permute-start(bf16[64,3584]{1,0:T(8,128)(2,1)S(1)} %slice.72), channel_id=1, source_target_pairs={{0,12},{1,13},{2,14},{3,15},{4,0},{5,1},{6,2},{7,3},{8,4},{9,5},{1... | collective-permute-start | bytes 1376264 | tf_op jit(solution)/shard_map/ppermute | solution.py:26
  73.0 2.2 %collective-permute-done.11.refs_1_ = bf16[64,3712]{1,0:T(8,128)(2,1)S(1)} collective-permute-done((bf16[64,3712]{1,0:T(8,128)(2,1)S(1)}, bf16[64,3712]{1,0:T(8,128)(2,1)S(1)}, u32[]{:S(2)}, u32[]{:S(2)}) %collective-permute-start.11) | collective-permute-done | bytes 475168 | tf_op jit(solution)/shard_map/ppermute | solution.py:26
  75.2 2.1 %shard_map.103 = (bf16[64,3584]{1,0:T(8,128)(2,1)S(1)}, bf16[64,3584]{1,0:T(8,128)(2,1)S(1)}) custom-call(bf16[64,3584]{1,0:T(8,128)(2,1)S(1)} %collective-permute-done.10.refs_0_, bf16[64,3712]{1,0:T(8,128)(2,1)S(1)} %collective-permute-done.11.refs_1_, bf16[7168,128]{1,0:T(8,128)(2,1)S(1)} %bitcast.9, bf16[7168,128]{1,0:T(8,128)(2,1)S(1)} %bitcast.14, ...), custom_call_target="tpu_custom_call" | custom-call | flops 704643072 | bytes 12845056 | tf_op jit(solution)/shard_map/pallas_call | solution.py:39
  77.4 2.7 %collective-permute-start.14 = (bf16[64,3584]{1,0:T(8,128)(2,1)S(1)}, bf16[64,3584]{1,0:T(8,128)(2,1)S(1)}, u32[]{:S(2)}, u32[]{:S(2)}) collective-permute-start(bf16[64,3584]{1,0:T(8,128)(2,1)S(1)} %get-tuple-element.41), channel_id=1, source_target_pairs={{0,12},{1,13},{2,14},{3,15},{4,0},{5,1},{6,2},{7,3},{8,4},{9,5},{1... | collective-permute-start | bytes 1376264 | tf_op jit(solution)/shard_map/ppermute | solution.py:26
  80.3 2.1 %shard_map.104 = (bf16[64,3584]{1,0:T(8,128)(2,1)S(1)}, bf16[64,3584]{1,0:T(8,128)(2,1)S(1)}) custom-call(bf16[64,3584]{1,0:T(8,128)(2,1)S(1)} %collective-permute-done.19.refs_0_, bf16[64,3712]{1,0:T(8,128)(2,1)S(1)} %collective-permute-done.20.refs_1_, bf16[7168,128]{1,0:T(8,128)(2,1)S(1)} %bitcast.10, bf16[7168,128]{1,0:T(8,128)(2,1)S(1)} %bitcast.15, ...), custom_call_target="tpu_custom_call" | custom-call | flops 704643072 | bytes 12845056 | tf_op jit(solution)/shard_map/pallas_call | solution.py:39
  82.5 2.7 %collective-permute-start.23 = (bf16[64,3584]{1,0:T(8,128)(2,1)S(1)}, bf16[64,3584]{1,0:T(8,128)(2,1)S(1)}, u32[]{:S(2)}, u32[]{:S(2)}) collective-permute-start(bf16[64,3584]{1,0:T(8,128)(2,1)S(1)} %get-tuple-element.52), channel_id=1, source_target_pairs={{0,12},{1,13},{2,14},{3,15},{4,0},{5,1},{6,2},{7,3},{8,4},{9,5},{1... | collective-permute-start | bytes 1376264 | tf_op jit(solution)/shard_map/ppermute | solution.py:26
  87.5 3.0 %collective-permute-start.15 = (bf16[64,7168]{1,0:T(8,128)(2,1)S(1)}, bf16[64,7168]{1,0:T(8,128)(2,1)S(1)}, u32[]{:S(2)}, u32[]{:S(2)}) collective-permute-start(bf16[64,7168]{1,0:T(8,128)(2,1)S(1)} %fusion.1), channel_id=1, source_target_pairs={{0,12},{1,13},{2,14},{3,15},{4,0},{5,1},{6,2},{7,3},{8,4},{9,5},{1... | collective-permute-start | bytes 2752520 | tf_op jit(solution)/shard_map/ppermute | solution.py:26
  91.9 2.7 %collective-permute-start.24 = (bf16[64,7168]{1,0:T(8,128)(2,1)S(1)}, bf16[64,7168]{1,0:T(8,128)(2,1)S(1)}, u32[]{:S(2)}, u32[]{:S(2)}) collective-permute-start(bf16[64,7168]{1,0:T(8,128)(2,1)S(1)} %fusion.3), channel_id=1, source_target_pairs={{0,12},{1,13},{2,14},{3,15},{4,0},{5,1},{6,2},{7,3},{8,4},{9,5},{1... | collective-permute-start | bytes 2752520 | tf_op jit(solution)/shard_map/ppermute | solution.py:26
  94.6 6.5 %collective-permute-done.13 = bf16[64,7168]{1,0:T(8,128)(2,1)S(1)} collective-permute-done((bf16[64,7168]{1,0:T(8,128)(2,1)S(1)}, bf16[64,7168]{1,0:T(8,128)(2,1)S(1)}, u32[]{:S(2)}, u32[]{:S(2)}) %collective-permute-start.13) | collective-permute-done | bytes 917536 | tf_op jit(solution)/shard_map/ppermute | solution.py:26
  101.6 2.7 %collective-permute-start.17 = (bf16[16,7168]{1,0:T(8,128)(2,1)S(1)}, bf16[16,7168]{1,0:T(8,128)(2,1)S(1)}, u32[]{:S(2)}, u32[]{:S(2)}) collective-permute-start(bf16[16,7168]{1,0:T(8,128)(2,1)S(1)} %get-tuple-element.55), channel_id=1, source_target_pairs={{0,3},{1,0},{2,1},{3,2},{4,7},{5,4},{6,5},{7,6},{8,11},{9,8},{10,9... | collective-permute-start | bytes 688136 | tf_op jit(solution)/shard_map/ppermute | solution.py:26
  104.3 9.0 %collective-permute-done.22 = bf16[64,7168]{1,0:T(8,128)(2,1)S(1)} collective-permute-done((bf16[64,7168]{1,0:T(8,128)(2,1)S(1)}, bf16[64,7168]{1,0:T(8,128)(2,1)S(1)}, u32[]{:S(2)}, u32[]{:S(2)}) %collective-permute-start.22) | collective-permute-done | bytes 917536 | tf_op jit(solution)/shard_map/ppermute | solution.py:26
  115.4 2.7 %collective-permute-start.26 = (bf16[16,7168]{1,0:T(8,128)(2,1)S(1)}, bf16[16,7168]{1,0:T(8,128)(2,1)S(1)}, u32[]{:S(2)}, u32[]{:S(2)}) collective-permute-start(bf16[16,7168]{1,0:T(8,128)(2,1)S(1)} %get-tuple-element.58), channel_id=1, source_target_pairs={{0,3},{1,0},{2,1},{3,2},{4,7},{5,4},{6,5},{7,6},{8,11},{9,8},{10,9... | collective-permute-start | bytes 688136 | tf_op jit(solution)/shard_map/ppermute | solution.py:26
  118.2 3.3 %collective-permute-done.25 = bf16[16,7168]{1,0:T(8,128)(2,1)S(1)} collective-permute-done((bf16[16,7168]{1,0:T(8,128)(2,1)S(1)}, bf16[16,7168]{1,0:T(8,128)(2,1)S(1)}, u32[]{:S(2)}, u32[]{:S(2)}) %collective-permute-start.25) | collective-permute-done | bytes 229408 | tf_op jit(solution)/shard_map/ppermute | solution.py:26
  121.5 2.0 %collective-permute-done.26 = bf16[16,7168]{1,0:T(8,128)(2,1)S(1)} collective-permute-done((bf16[16,7168]{1,0:T(8,128)(2,1)S(1)}, bf16[16,7168]{1,0:T(8,128)(2,1)S(1)}, u32[]{:S(2)}, u32[]{:S(2)}) %collective-permute-start.26) | collective-permute-done | bytes 229408 | tf_op jit(solution)/shard_map/ppermute | solution.py:26
  124.8 30.2 %all_to_all.11 = bf16[16,2,7168]{2,1,0:T(2,128)(2,1)S(1)} all-to-all(bf16[16,2,7168]{2,1,0:T(2,128)(2,1)S(1)} %reshape.17), channel_id=1, replica_groups=mesh['node'=16,'local'=16] {'node'}, dimensions={0} | all-to-all | bytes 917504 | tf_op jit(solution)/shard_map/all_to_all | solution.py:218
  (98 shorter events, 31.3 us)
Async XLA Ops:
  32.7 8.9 %collective-permute-start.1 = (bf16[16,7296]{1,0:T(8,128)(2,1)S(1)}, bf16[16,7296]{1,0:T(8,128)(2,1)}, u32[]{:S(2)}, u32[]{:S(2)}) collective-permute-start(bf16[16,7296]{1,0:T(8,128)(2,1)S(1)} %slice.61), channel_id=1, source_target_pairs={{0,1},{1,2},{2,3},{3,0},{4,5},{5,6},{6,7},{7,4},{8,9},{9,10},{10,1... | collective-permute-start | bytes 700424 | tf_op jit(solution)/shard_map/ppermute | solution.py:26
  32.8 9.9 %collective-permute-start.2 = (bf16[16,7296]{1,0:T(8,128)(2,1)S(1)}, bf16[16,7296]{1,0:T(8,128)(2,1)}, u32[]{:S(2)}, u32[]{:S(2)}) collective-permute-start(bf16[16,7296]{1,0:T(8,128)(2,1)S(1)} %slice.61), channel_id=1, source_target_pairs={{0,2},{1,3},{2,0},{3,1},{4,6},{5,7},{6,4},{7,5},{8,10},{9,11},{10,... | collective-permute-start | bytes 700424 | tf_op jit(solution)/shard_map/ppermute | solution.py:26
  34.5 11.6 %collective-permute-start.5 = (bf16[16,7296]{1,0:T(8,128)(2,1)S(1)}, bf16[16,7296]{1,0:T(8,128)(2,1)S(1)}, u32[]{:S(2)}, u32[]{:S(2)}) collective-permute-start(bf16[16,7296]{1,0:T(8,128)(2,1)S(1)} %slice.63), channel_id=1, source_target_pairs={{0,3},{1,0},{2,1},{3,2},{4,7},{5,4},{6,5},{7,6},{8,11},{9,8},{10,9... | collective-permute-start | bytes 700424 | tf_op jit(solution)/shard_map/ppermute | solution.py:26
  35.6 10.7 %collective-permute-start.6 = (bf16[16,7296]{1,0:T(8,128)(2,1)S(1)}, bf16[16,7296]{1,0:T(8,128)(2,1)S(1)}, u32[]{:S(2)}, u32[]{:S(2)}) collective-permute-start(bf16[16,7296]{1,0:T(8,128)(2,1)S(1)} %slice.63), channel_id=1, source_target_pairs={{0,1},{1,2},{2,3},{3,0},{4,5},{5,6},{6,7},{7,4},{8,9},{9,10},{10,1... | collective-permute-start | bytes 700424 | tf_op jit(solution)/shard_map/ppermute | solution.py:26
  36.3 10.1 %collective-permute-start.7 = (bf16[16,7296]{1,0:T(8,128)(2,1)S(1)}, bf16[16,7296]{1,0:T(8,128)(2,1)S(1)}, u32[]{:S(2)}, u32[]{:S(2)}) collective-permute-start(bf16[16,7296]{1,0:T(8,128)(2,1)S(1)} %slice.63), channel_id=1, source_target_pairs={{0,2},{1,3},{2,0},{3,1},{4,6},{5,7},{6,4},{7,5},{8,10},{9,11},{10,... | collective-permute-start | bytes 700424 | tf_op jit(solution)/shard_map/ppermute | solution.py:26
  43.6 13.2 %collective-permute-start.3 = (bf16[64,7296]{1,0:T(8,128)(2,1)S(1)}, bf16[64,7296]{1,0:T(8,128)(2,1)S(1)}, u32[]{:S(2)}, u32[]{:S(2)}) collective-permute-start(bf16[64,7296]{1,0:T(8,128)(2,1)S(1)} %constant_dynamic-update-slice_fusion.refs_0_), channel_id=1, source_target_pairs={{0,12},{1,13},{2,14},{3,15},{4,0},{5,1},{6,2},{7,3},{8,4},{9,5},{1... | collective-permute-start | bytes 2801672 | tf_op jit(solution)/shard_map/ppermute | solution.py:26
  46.2 13.9 %collective-permute-start.4 = (bf16[64,7296]{1,0:T(8,128)(2,1)S(1)}, bf16[64,7296]{1,0:T(8,128)(2,1)S(1)}, u32[]{:S(2)}, u32[]{:S(2)}) collective-permute-start(bf16[64,7296]{1,0:T(8,128)(2,1)S(1)} %constant_dynamic-update-slice_fusion.refs_0_), channel_id=1, source_target_pairs={{0,4},{1,5},{2,6},{3,7},{4,8},{5,9},{6,10},{7,11},{8,12},{9,13},{1... | collective-permute-start | bytes 2801672 | tf_op jit(solution)/shard_map/ppermute | solution.py:26
  46.4 20.2 %collective-permute-start.8 = (bf16[64,7296]{1,0:T(8,128)(2,1)S(1)}, bf16[64,7296]{1,0:T(8,128)(2,1)S(1)}, u32[]{:S(2)}, u32[]{:S(2)}) collective-permute-start(bf16[64,7296]{1,0:T(8,128)(2,1)S(1)} %constant_dynamic-update-slice_fusion.4.refs_1_), channel_id=1, source_target_pairs={{0,12},{1,13},{2,14},{3,15},{4,0},{5,1},{6,2},{7,3},{8,4},{9,5},{1... | collective-permute-start | bytes 2801672 | tf_op jit(solution)/shard_map/ppermute | solution.py:26
  49.0 21.1 %collective-permute-start.9 = (bf16[64,7296]{1,0:T(8,128)(2,1)S(1)}, bf16[64,7296]{1,0:T(8,128)(2,1)S(1)}, u32[]{:S(2)}, u32[]{:S(2)}) collective-permute-start(bf16[64,7296]{1,0:T(8,128)(2,1)S(1)} %constant_dynamic-update-slice_fusion.4.refs_1_), channel_id=1, source_target_pairs={{0,4},{1,5},{2,6},{3,7},{4,8},{5,9},{6,10},{7,11},{8,12},{9,13},{1... | collective-permute-start | bytes 2801672 | tf_op jit(solution)/shard_map/ppermute | solution.py:26
  60.1 15.1 %collective-permute-start.11 = (bf16[64,3712]{1,0:T(8,128)(2,1)S(1)}, bf16[64,3712]{1,0:T(8,128)(2,1)S(1)}, u32[]{:S(2)}, u32[]{:S(2)}) collective-permute-start(bf16[64,3712]{1,0:T(8,128)(2,1)S(1)} %slice.66), channel_id=1, source_target_pairs={{0,4},{1,5},{2,6},{3,7},{4,8},{5,9},{6,10},{7,11},{8,12},{9,13},{1... | collective-permute-start | bytes 1425416 | tf_op jit(solution)/shard_map/ppermute | solution.py:26
  60.3 12.8 %collective-permute-start.10 = (bf16[64,3584]{1,0:T(8,128)(2,1)S(1)}, bf16[64,3584]{1,0:T(8,128)(2,1)S(1)}, u32[]{:S(2)}, u32[]{:S(2)}) collective-permute-start(bf16[64,3584]{1,0:T(8,128)(2,1)S(1)} %slice.65), channel_id=1, source_target_pairs={{0,12},{1,13},{2,14},{3,15},{4,0},{5,1},{6,2},{7,3},{8,4},{9,5},{1... | collective-permute-start | bytes 1376264 | tf_op jit(solution)/shard_map/ppermute | solution.py:26
  70.1 10.1 %collective-permute-start.20 = (bf16[64,3712]{1,0:T(8,128)(2,1)S(1)}, bf16[64,3712]{1,0:T(8,128)(2,1)S(1)}, u32[]{:S(2)}, u32[]{:S(2)}) collective-permute-start(bf16[64,3712]{1,0:T(8,128)(2,1)S(1)} %slice.73), channel_id=1, source_target_pairs={{0,4},{1,5},{2,6},{3,7},{4,8},{5,9},{6,10},{7,11},{8,12},{9,13},{1... | collective-permute-start | bytes 1425416 | tf_op jit(solution)/shard_map/ppermute | solution.py:26
  70.3 9.8 %collective-permute-start.19 = (bf16[64,3584]{1,0:T(8,128)(2,1)S(1)}, bf16[64,3584]{1,0:T(8,128)(2,1)S(1)}, u32[]{:S(2)}, u32[]{:S(2)}) collective-permute-start(bf16[64,3584]{1,0:T(8,128)(2,1)S(1)} %slice.72), channel_id=1, source_target_pairs={{0,12},{1,13},{2,14},{3,15},{4,0},{5,1},{6,2},{7,3},{8,4},{9,5},{1... | collective-permute-start | bytes 1376264 | tf_op jit(solution)/shard_map/ppermute | solution.py:26
  77.3 9.6 %collective-permute-start.12 = (bf16[64,3584]{1,0:T(8,128)(2,1)S(1)}, bf16[64,3584]{1,0:T(8,128)(2,1)S(1)}, u32[]{:S(2)}, u32[]{:S(2)}) collective-permute-start(bf16[64,3584]{1,0:T(8,128)(2,1)S(1)} %get-tuple-element.39), channel_id=1, source_target_pairs={{0,4},{1,5},{2,6},{3,7},{4,8},{5,9},{6,10},{7,11},{8,12},{9,13},{1... | collective-permute-start | bytes 1376264 | tf_op jit(solution)/shard_map/ppermute | solution.py:26
  77.4 9.8 %collective-permute-start.14 = (bf16[64,3584]{1,0:T(8,128)(2,1)S(1)}, bf16[64,3584]{1,0:T(8,128)(2,1)S(1)}, u32[]{:S(2)}, u32[]{:S(2)}) collective-permute-start(bf16[64,3584]{1,0:T(8,128)(2,1)S(1)} %get-tuple-element.41), channel_id=1, source_target_pairs={{0,12},{1,13},{2,14},{3,15},{4,0},{5,1},{6,2},{7,3},{8,4},{9,5},{1... | collective-permute-start | bytes 1376264 | tf_op jit(solution)/shard_map/ppermute | solution.py:26
  82.4 8.9 %collective-permute-start.21 = (bf16[64,3584]{1,0:T(8,128)(2,1)S(1)}, bf16[64,3584]{1,0:T(8,128)(2,1)S(1)}, u32[]{:S(2)}, u32[]{:S(2)}) collective-permute-start(bf16[64,3584]{1,0:T(8,128)(2,1)S(1)} %get-tuple-element.50), channel_id=1, source_target_pairs={{0,4},{1,5},{2,6},{3,7},{4,8},{5,9},{6,10},{7,11},{8,12},{9,13},{1... | collective-permute-start | bytes 1376264 | tf_op jit(solution)/shard_map/ppermute | solution.py:26
  82.5 9.1 %collective-permute-start.23 = (bf16[64,3584]{1,0:T(8,128)(2,1)S(1)}, bf16[64,3584]{1,0:T(8,128)(2,1)S(1)}, u32[]{:S(2)}, u32[]{:S(2)}) collective-permute-start(bf16[64,3584]{1,0:T(8,128)(2,1)S(1)} %get-tuple-element.52), channel_id=1, source_target_pairs={{0,12},{1,13},{2,14},{3,15},{4,0},{5,1},{6,2},{7,3},{8,4},{9,5},{1... | collective-permute-start | bytes 1376264 | tf_op jit(solution)/shard_map/ppermute | solution.py:26
  87.1 14.0 %collective-permute-start.13 = (bf16[64,7168]{1,0:T(8,128)(2,1)S(1)}, bf16[64,7168]{1,0:T(8,128)(2,1)S(1)}, u32[]{:S(2)}, u32[]{:S(2)}) collective-permute-start(bf16[64,7168]{1,0:T(8,128)(2,1)S(1)} %fusion), channel_id=1, source_target_pairs={{0,4},{1,5},{2,6},{3,7},{4,8},{5,9},{6,10},{7,11},{8,12},{9,13},{1... | collective-permute-start | bytes 2752520 | tf_op jit(solution)/shard_map/ppermute | solution.py:26
  87.5 13.7 %collective-permute-start.15 = (bf16[64,7168]{1,0:T(8,128)(2,1)S(1)}, bf16[64,7168]{1,0:T(8,128)(2,1)S(1)}, u32[]{:S(2)}, u32[]{:S(2)}) collective-permute-start(bf16[64,7168]{1,0:T(8,128)(2,1)S(1)} %fusion.1), channel_id=1, source_target_pairs={{0,12},{1,13},{2,14},{3,15},{4,0},{5,1},{6,2},{7,3},{8,4},{9,5},{1... | collective-permute-start | bytes 2752520 | tf_op jit(solution)/shard_map/ppermute | solution.py:26
  91.5 21.7 %collective-permute-start.22 = (bf16[64,7168]{1,0:T(8,128)(2,1)S(1)}, bf16[64,7168]{1,0:T(8,128)(2,1)S(1)}, u32[]{:S(2)}, u32[]{:S(2)}) collective-permute-start(bf16[64,7168]{1,0:T(8,128)(2,1)S(1)} %fusion.2), channel_id=1, source_target_pairs={{0,4},{1,5},{2,6},{3,7},{4,8},{5,9},{6,10},{7,11},{8,12},{9,13},{1... | collective-permute-start | bytes 2752520 | tf_op jit(solution)/shard_map/ppermute | solution.py:26
  91.9 23.1 %collective-permute-start.24 = (bf16[64,7168]{1,0:T(8,128)(2,1)S(1)}, bf16[64,7168]{1,0:T(8,128)(2,1)S(1)}, u32[]{:S(2)}, u32[]{:S(2)}) collective-permute-start(bf16[64,7168]{1,0:T(8,128)(2,1)S(1)} %fusion.3), channel_id=1, source_target_pairs={{0,12},{1,13},{2,14},{3,15},{4,0},{5,1},{6,2},{7,3},{8,4},{9,5},{1... | collective-permute-start | bytes 2752520 | tf_op jit(solution)/shard_map/ppermute | solution.py:26
  101.5 16.6 %collective-permute-start.16 = (bf16[16,7168]{1,0:T(8,128)(2,1)S(1)}, bf16[16,7168]{1,0:T(8,128)(2,1)S(1)}, u32[]{:S(2)}, u32[]{:S(2)}) collective-permute-start(bf16[16,7168]{1,0:T(8,128)(2,1)S(1)} %get-tuple-element.53), channel_id=1, source_target_pairs={{0,1},{1,2},{2,3},{3,0},{4,5},{5,6},{6,7},{7,4},{8,9},{9,10},{10,1... | collective-permute-start | bytes 688136 | tf_op jit(solution)/shard_map/ppermute | solution.py:26
  101.6 16.5 %collective-permute-start.17 = (bf16[16,7168]{1,0:T(8,128)(2,1)S(1)}, bf16[16,7168]{1,0:T(8,128)(2,1)S(1)}, u32[]{:S(2)}, u32[]{:S(2)}) collective-permute-start(bf16[16,7168]{1,0:T(8,128)(2,1)S(1)} %get-tuple-element.55), channel_id=1, source_target_pairs={{0,3},{1,0},{2,1},{3,2},{4,7},{5,4},{6,5},{7,6},{8,11},{9,8},{10,9... | collective-permute-start | bytes 688136 | tf_op jit(solution)/shard_map/ppermute | solution.py:26
  104.3 13.8 %collective-permute-start.18 = (bf16[16,7168]{1,0:T(8,128)(2,1)S(1)}, bf16[16,7168]{1,0:T(8,128)(2,1)S(1)}, u32[]{:S(2)}, u32[]{:S(2)}) collective-permute-start(bf16[16,7168]{1,0:T(8,128)(2,1)S(1)} %get-tuple-element.54), channel_id=1, source_target_pairs={{0,2},{1,3},{2,0},{3,1},{4,6},{5,7},{6,4},{7,5},{8,10},{9,11},{10,... | collective-permute-start | bytes 688136 | tf_op jit(solution)/shard_map/ppermute | solution.py:26
  (18 other events, 105.1 us)
